TPU v7x, 32 devices: a whole 2x2x4 slice. The times are simulated.
32 devices in a mesh: grp: 8 (over z, core), head: 4 (over y, x).
Axes of the slice: x: 2, y: 2, z: 4, core: 2. Of those that a mesh axis runs over, the one named last changes fastest.
Arguments:
- query_rows: bfloat16 [32, 128, 2048], P(('grp', 'head')), may hold values from -6 to 6
- key_rows: bfloat16 [32, 128, 2048], P(('grp', 'head')), may hold values from -6 to 6
- value_rows: bfloat16 [32, 128, 2048], P(('grp', 'head')), may hold values from -6 to 6
- log_decay: bfloat16 [32, 128, 2048], P(('grp', 'head')), may hold values from -1.5 to 0, as said below
- beta_logit: bfloat16 [32, 128, 16], P(('grp', 'head')), may hold values from -6 to 6
- out_grad: bfloat16 [32, 128, 2048], P(('grp', 'head')), may hold values from -6 to 6
- fork_state: float32 [8, 16, 128, 128], P(None, 'head'), may hold values from -6 to 6
- branch_prompt: int32 [32], replicated, may hold values from 0 to 7, as said below
- valid_len: int32 [32], replicated, may hold values from 32 to 128, as said below
Outputs:
- grad_query: bfloat16 [32, 128, 2048], P(('grp', 'head'))
- grad_key: bfloat16 [32, 128, 2048], P(('grp', 'head'))
- grad_value: bfloat16 [32, 128, 2048], P(('grp', 'head'))
- grad_decay: bfloat16 [32, 128, 2048], P(('grp', 'head'))
- grad_beta: bfloat16 [32, 128, 16], P(('grp', 'head'))
- grad_fork: float32 [8, 16, 128, 128], P(None, 'head')
Inputs may be any that keep to these rules, and one draw needn't show every extreme that they name: `log_decay`: never positive; a few tokens of each branch lose a large share of every channel at once. `branch_prompt`: every prompt has at least one branch. A branch counts its first valid_len tokens; some branch uses all 128.
All inputs are finite; a program needn't handle non-finite values.
Results may differ from a plain program's by a relative error of at most 0.0015.
Values may be sent and summed in bfloat16 or wider, within the bound.
No kernel may reach another device: no remote copies, remote signals or barrier semaphores. Data moves between devices by JAX's collectives and lax.ppermute only.
A program may use at most 64 MiB of HBM per device.

v0:
```python
from functools import partial

import jax
import jax.numpy as jnp
from jax import lax
from jax.sharding import PartitionSpec as P


def decay_forward(query_in, key_in, value_in, decay_in, beta_in, state_in, keep_mask, block_len):
    head_dim = query_in.shape[-1]
    upper_limit = lax.Precision.HIGHEST
    unit_query = (
        query_in
        * lax.rsqrt(jnp.sum(query_in * query_in, axis=-1, keepdims=True) + 1e-06)
        * head_dim ** (-0.5)
    )
    unit_key = key_in * lax.rsqrt(jnp.sum(key_in * key_in, axis=-1, keepdims=True) + 1e-06)
    beta_value = jax.nn.sigmoid(beta_in) * keep_mask[None, :]
    decay_value = decay_in * keep_mask[None, :, None]
    token_positions = jnp.arange(block_len, dtype=jnp.int32)
    lower_strict = (token_positions[:, None] > token_positions[None, :]).astype(jnp.float32)
    lower_closed = (token_positions[:, None] >= token_positions[None, :]).astype(jnp.float32)
    identity_block = jnp.eye(block_len, dtype=jnp.float32)
    cum_decay = jnp.cumsum(decay_value, axis=1)
    growth = jnp.exp(cum_decay)
    shrink = jnp.exp(-cum_decay)
    key_forward_rows = unit_key * growth
    key_earlier_rows = unit_key * shrink
    query_forward_rows = unit_query * growth
    coupling = (
        jnp.einsum("htk,hsk->hts", key_forward_rows, key_earlier_rows, precision=upper_limit)
        * beta_value[:, :, None]
        * lower_strict
    )
    attend_scores = (
        jnp.einsum("htk,hsk->hts", query_forward_rows, key_earlier_rows, precision=upper_limit)
        * lower_closed
    )
    target_output = beta_value[:, :, None] * (
        value_in - jnp.einsum("led,ldf->lef", key_forward_rows, state_in, precision=upper_limit)
    )
    state_update = jax.scipy.linalg.solve_triangular(
        identity_block + coupling, target_output, lower=True, unit_diagonal=True
    )
    output_block_rows = jnp.einsum(
        "led,ldf->lef", query_forward_rows, state_in, precision=upper_limit
    ) + jnp.einsum("ifj,ijo->ifo", attend_scores, state_update, precision=upper_limit)
    outputs = [output_block_rows]
    return jnp.concatenate(outputs, axis=1)


def branch_backward(
    query_rows, key_rows, value_rows, log_decay, out_grad, beta_logit, states, valid_rows, block_len
):
    count, window_len, row_width = query_rows.shape
    heads_here = states.shape[1]
    head_dim = states.shape[-1]

    def split_heads(array_in):
        return (
            array_in.astype(jnp.float32)
            .reshape(count, window_len, heads_here, head_dim)
            .transpose(0, 2, 1, 3)
        )

    def join_heads(array_in):
        return (
            array_in.transpose(0, 2, 1, 3)
            .reshape(count, window_len, row_width)
            .astype(jnp.bfloat16)
        )

    keep_mask = (jnp.arange(window_len, dtype=jnp.int32)[None, :] < valid_rows[:, None]).astype(
        jnp.float32
    )
    beta_in = beta_logit.astype(jnp.float32).transpose(0, 2, 1)
    mapped = jax.vmap(partial(decay_forward, block_len=block_len))

    def forward_all(query_in, key_in, value_in, decay_in, beta_all, state_all):
        return mapped(query_in, key_in, value_in, decay_in, beta_all, state_all, keep_mask)

    outputs, pullback = jax.vjp(
        forward_all,
        split_heads(query_rows),
        split_heads(key_rows),
        split_heads(value_rows),
        split_heads(log_decay),
        beta_in,
        states,
    )
    cotangent = split_heads(out_grad) * keep_mask[:, None, :, None]
    grad_q, grad_k, grad_v, grad_g, grad_b, grad_s = pullback(cotangent)
    gradients = (
        join_heads(grad_q),
        join_heads(grad_k),
        join_heads(grad_v),
        join_heads(grad_g),
        grad_b.transpose(0, 2, 1).astype(jnp.bfloat16),
    )
    return (gradients, grad_s)


def per_device(
    query_rows,
    key_rows,
    value_rows,
    log_decay,
    beta_logit,
    out_grad,
    fork_state,
    branch_prompt,
    valid_len,
):
    upper_limit = lax.Precision.HIGHEST
    local_count = query_rows.shape[0]
    head_count = lax.axis_size("head")
    group_size = local_count * head_count
    group_first = lax.axis_index("grp") * group_size
    prompt_count = fork_state.shape[0]
    prompt_ids = jnp.arange(prompt_count, dtype=jnp.int32)
    window_len = query_rows.shape[1]
    group_prompt = lax.dynamic_slice_in_dim(branch_prompt, group_first, group_size)
    group_onehot = (group_prompt[:, None] == prompt_ids[None, :]).astype(jnp.float32)
    group_states = jnp.einsum("bp,phij->bhij", group_onehot, fork_state, precision=upper_limit)
    arrived = (
        lax.all_to_all(query_rows, "head", split_axis=2, concat_axis=0, tiled=True),
        lax.all_to_all(key_rows, "head", split_axis=2, concat_axis=0, tiled=True),
        lax.all_to_all(value_rows, "head", split_axis=2, concat_axis=0, tiled=True),
        lax.all_to_all(log_decay, "head", split_axis=2, concat_axis=0, tiled=True),
        lax.all_to_all(out_grad, "head", split_axis=2, concat_axis=0, tiled=True),
        lax.all_to_all(beta_logit, "head", split_axis=2, concat_axis=0, tiled=True),
    )
    group_len = lax.dynamic_slice_in_dim(valid_len, group_first, group_size)
    gradients, state_grad = branch_backward(
        arrived[0],
        arrived[1],
        arrived[2],
        arrived[3],
        arrived[4],
        arrived[5],
        group_states,
        group_len,
        window_len,
    )
    prompt_grad = jnp.einsum("bp,bhij->phij", group_onehot, state_grad, precision=upper_limit)
    results = (
        lax.all_to_all(gradients[0], "head", split_axis=0, concat_axis=2, tiled=True),
        lax.all_to_all(gradients[1], "head", split_axis=0, concat_axis=2, tiled=True),
        lax.all_to_all(gradients[2], "head", split_axis=0, concat_axis=2, tiled=True),
        lax.all_to_all(gradients[3], "head", split_axis=0, concat_axis=2, tiled=True),
        lax.all_to_all(gradients[4], "head", split_axis=0, concat_axis=2, tiled=True),
    )
    grad_fork = lax.psum(prompt_grad, "grp")
    return (results[0], results[1], results[2], results[3], results[4], grad_fork)


def solution(mesh):
    return jax.shard_map(
        per_device,
        mesh=mesh,
        in_specs=(
            P(("grp", "head"), None, None),
            P(("grp", "head"), None, None),
            P(("grp", "head"), None, None),
            P(("grp", "head"), None, None),
            P(("grp", "head"), None, None),
            P(("grp", "head"), None, None),
            P(None, "head", None, None),
            P(),
            P(),
        ),
        out_specs=(
            P(("grp", "head"), None, None),
            P(("grp", "head"), None, None),
            P(("grp", "head"), None, None),
            P(("grp", "head"), None, None),
            P(("grp", "head"), None, None),
            P(None, "head", None, None),
        ),
        check_vma=False,
    )
```

profile of v0, /device:TPU:0, one launch (start us, length us, event | category | flops | bytes accessed | tf_op | source)
XLA Modules:
  0.0 456.7 jit_solution(5627891447039417884)
XLA Ops:
  9.8 5.2 %all-to-all-start.3 = ((bf16[4,2,256]{2,1,0:T(2,128)(2,1)}), bf16[4,2,256]{2,1,0:T(2,128)(2,1)S(1)}, u32[]{:S(2)}, u32[]{:S(2)}) async-start(bf16[4,2,256]{2,1,0:T(2,128)(2,1)} %reshape.215), calls=%async_computation.3 | async-start | bytes 8192 | tf_op jit(solution)/shard_map/all_to_all | solution.py:131
  16.5 2.2 fusion
  18.9 2.5 copy.138
  21.4 11.6 %reduce.4 = bf16[2048,128]{1,0:T(8,128)(2,1)S(1)} reduce(bf16[2048,1,128]{2,1,0:T(2,128)(2,1)S(1)} %bitcast.185, bf16[]{:T(256)} %broadcast.196), dimensions={1}, to_apply=%bitcast.141.reduce_sub_computation | reduce | bytes 1048578
  33.9 4.4 all-to-all-start.4
  39.1 11.5 %reduce.2 = bf16[2048,128]{1,0:T(8,128)(2,1)S(1)} reduce(bf16[2048,1,128]{2,1,0:T(2,128)(2,1)S(1)} %bitcast.186, bf16[]{:T(256)} %broadcast.196), dimensions={1}, to_apply=%bitcast.131.reduce_sub_computation | reduce | bytes 1048578
  51.6 2.3 copy.127
  53.9 11.5 %reduce = bf16[2048,128]{1,0:T(8,128)(2,1)S(1)} reduce(bf16[2048,1,128]{2,1,0:T(2,128)(2,1)S(1)} %bitcast.187, bf16[]{:T(256)} %broadcast.196), dimensions={1}, to_apply=%bitcast.133.reduce_sub_computation | reduce | bytes 1048578
  66.4 2.3 copy.128
  68.7 11.9 %reduce.1 = bf16[2048,128]{1,0:T(8,128)(2,1)S(1)} reduce(bf16[2048,1,128]{2,1,0:T(2,128)(2,1)S(1)} %bitcast.188, bf16[]{:T(256)} %broadcast.196), dimensions={1}, to_apply=%bitcast.135.reduce_sub_computation | reduce | bytes 1048578
  81.6 2.3 copy.123
  83.9 11.5 %reduce.5 = bf16[2048,128]{1,0:T(8,128)(2,1)S(1)} reduce(bf16[2048,1,128]{2,1,0:T(2,128)(2,1)S(1)} %bitcast.184, bf16[]{:T(256)} %broadcast.196), dimensions={1}, to_apply=%bitcast.137.reduce_sub_computation | reduce | bytes 1048578
  96.5 4.2 all-to-all-start.2
  102.3 5.8 %all-to-all-done.2 = bf16[4,2,32768]{2,1,0:T(2,128)(2,1)} async-done(((bf16[4,2,32768]{2,1,0:T(2,128)(2,1)}), bf16[4,2,32768]{2,1,0:T(2,128)(2,1)}, u32[]{:S(2)}, u32[]{:S(2)}) %all-to-all-start.2) | async-done | bytes 524320 | tf_op jit(solution)/shard_map/all_to_all | solution.py:129
  108.1 4.3 all-to-all-start.5
  112.5 3.5 reshape.212
  115.9 2.2 bitcast_convert_fusion.2
  119.9 4.9 %reduce_window_sum.22 = f32[4,4,128,128]{3,2,1,0:T(8,128)S(1)} reduce-window(f32[4,4,128,128]{3,2,1,0:T(8,128)S(1)} %copy.129, f32[]{:T(128)} %constant.38.clone.1), window={size=1x1x128x1 pad=0_0x0_0x127_0x0_0}, to_apply=%region_1.0 | reduce-window | flops 33292288 | bytes 2097156 | tf_op jit(solution)/shard_map/jvp(vmap(jit(cumsum)))/reduce_window_sum | solution.py:24
  126.1 4.2 all-to-all-start.1
  130.3 2.2 reshape.208
  133.7 3.2 all-to-all-done.1
  137.0 4.1 all-to-all-start
  141.1 3.5 reshape.210
  144.6 2.2 bitcast_convert_fusion.3
  147.7 3.5 reshape.214
  151.2 2.2 bitcast_convert_fusion.1
  153.4 2.2 fusion.17
  157.5 2.9 convolution_subtract_fusion
  164.7 159.0 %custom-call.7 = f32[4,4,1,128,128]{3,4,2,1,0:T(8,128)} custom-call(f32[4,4,1,128,128]{4,3,2,1,0:T(8,128)} %add_bitcast_fusion), custom_call_target="InvertDiagBlocksLowerTriangular" | custom-call | tf_op jit(solution)/shard_map/jvp(vmap(jit(_solve_triangular)))/vmap()/triangular_solve | solution.py:42
  323.8 3.8 fusion.10
  333.8 2.3 fusion.6
  338.0 2.6 fusion.23
  341.7 2.3 convolution_add_fusion.3
  344.1 2.5 multiply_reduce_fusion
  348.0 4.2 multiply_reduce_fusion.2
  352.9 3.2 all-to-all-start.10
  356.1 4.1 fusion.5
  360.8 4.3 all-to-all-start.6
  365.1 3.5 fusion.12
  371.7 3.5 all-to-all-start.7
  375.3 3.2 fusion.19
  379.5 2.4 all-to-all-done.7
  381.9 3.5 all-to-all-start.8
  385.8 28.3 %reduce_window_sum.23 = f32[4,4,128,128]{3,2,1,0:T(8,128)S(1)} reduce-window(f32[4,4,128,128]{3,2,1,0:T(8,128)S(1)} %copy.159, f32[]{:T(128)} %constant.38.clone.1), window={size=1x1x128x1 pad=0_0x0_0x0_127x0_0}, to_apply=%region_5.7 | reduce-window | flops 33292288 | bytes 2097156 | tf_op jit(solution)/shard_map/transpose(jvp(vmap(jit(cumsum))))/reduce_window_sum | solution.py:24
  415.3 4.1 all-to-all-start.9
  423.5 2.5 all-to-all-done.9
  427.0 18.6 %all-reduce.2.cloned.1.call-done = f32[8,4,128,128]{3,0,2,1:T(8,128)} async-done(((f32[8,4,128,128]{3,0,2,1:T(8,128)}), f32[8,4,128,128]{3,0,2,1:T(8,128)}) %all-reduce.2.cloned.1.call-update) | async-done | bytes 2097168 | tf_op jit(solution)/shard_map/psum | solution.py:153
  445.6 3.3 copy.167
  (120 shorter events, 46.0 us)
Async XLA Ops:
  7.2 9.4 %copy-start = (f32[8,4,128,128]{3,2,1,0:T(8,128)S(1)}, f32[8,4,128,128]{3,2,1,0:T(8,128)}, u32[]{:S(2)}) copy-start(f32[8,4,128,128]{3,2,1,0:T(8,128)} %param.17) | copy-start | bytes 6291460
  9.8 24.1 %all-to-all-start.3 = ((bf16[4,2,256]{2,1,0:T(2,128)(2,1)}), bf16[4,2,256]{2,1,0:T(2,128)(2,1)S(1)}, u32[]{:S(2)}, u32[]{:S(2)}) async-start(bf16[4,2,256]{2,1,0:T(2,128)(2,1)} %reshape.215), calls=%async_computation.3 | async-start | bytes 8192 | tf_op jit(solution)/shard_map/all_to_all | solution.py:131
  18.8 134.6 %copy-start.13 = (f32[4,4,128,128]{3,0,2,1:T(4,128)}, f32[4,4,128,128]{3,0,2,1:T(4,128)S(1)}, u32[]{:S(2)}) copy-start(f32[4,4,128,128]{3,0,2,1:T(4,128)S(1)} %fusion) | copy-start | bytes 3145732
  21.4 17.0 %copy-start.28 = (bf16[1,128,2048]{2,1,0:T(8,128)(2,1)S(1)}, bf16[1,128,2048]{2,1,0:T(8,128)(2,1)}, u32[]{:S(2)}) copy-start(bf16[1,128,2048]{2,1,0:T(8,128)(2,1)} %param.11) | copy-start | bytes 1572868
  33.9 62.5 %all-to-all-start.4 = ((bf16[4,2,32768]{2,1,0:T(2,128)(2,1)}), bf16[4,2,32768]{2,1,0:T(2,128)(2,1)S(1)}, u32[]{:S(2)}, u32[]{:S(2)}) async-start(bf16[4,2,32768]{2,1,0:T(2,128)(2,1)} %reshape.217), calls=%async_computation.4 | async-start | bytes 1048576 | tf_op jit(solution)/shard_map/all_to_all | solution.py:128
  96.5 11.7 %all-to-all-start.2 = ((bf16[4,2,32768]{2,1,0:T(2,128)(2,1)}), bf16[4,2,32768]{2,1,0:T(2,128)(2,1)}, u32[]{:S(2)}, u32[]{:S(2)}) async-start(bf16[4,2,32768]{2,1,0:T(2,128)(2,1)} %reshape.211), calls=%async_computation.2 | async-start | bytes 1048576 | tf_op jit(solution)/shard_map/all_to_all | solution.py:129
  108.1 17.9 %all-to-all-start.5 = ((bf16[4,2,32768]{2,1,0:T(2,128)(2,1)}), bf16[4,2,32768]{2,1,0:T(2,128)(2,1)}, u32[]{:S(2)}, u32[]{:S(2)}) async-start(bf16[4,2,32768]{2,1,0:T(2,128)(2,1)} %reshape.207), calls=%async_computation.5 | async-start | bytes 1048576 | tf_op jit(solution)/shard_map/all_to_all | solution.py:126
  126.1 10.9 %all-to-all-start.1 = ((bf16[4,2,32768]{2,1,0:T(2,128)(2,1)}), bf16[4,2,32768]{2,1,0:T(2,128)(2,1)}, u32[]{:S(2)}, u32[]{:S(2)}) async-start(bf16[4,2,32768]{2,1,0:T(2,128)(2,1)} %reshape.209), calls=%async_computation.1 | async-start | bytes 1048576 | tf_op jit(solution)/shard_map/all_to_all | solution.py:127
  137.0 10.8 %all-to-all-start = ((bf16[4,2,32768]{2,1,0:T(2,128)(2,1)}), bf16[4,2,32768]{2,1,0:T(2,128)(2,1)}, u32[]{:S(2)}, u32[]{:S(2)}) async-start(bf16[4,2,32768]{2,1,0:T(2,128)(2,1)} %reshape.213), calls=%async_computation | async-start | bytes 1048576 | tf_op jit(solution)/shard_map/all_to_all | solution.py:130
  153.4 2.2 copy-start.2
  153.4 2.2 copy-start.8
  155.6 1.4 copy-start.14
  155.6 1.9 copy-start.23
  157.0 3.4 copy-start.5
  162.4 1.0 copy-start.19
  323.8 3.8 copy-start.3
  327.5 1.9 copy-start.12
  332.6 1.2 copy-start.18
  333.8 2.3 copy-start.21
  336.1 4.4 copy-start.10
  336.2 1.8 copy-start.15
  340.5 1.2 copy-start.24
  341.7 2.3 copy-start.20
  344.1 3.9 copy-start.16
  344.1 2.5 copy-start.6
  346.6 1.4 copy-start.9
  348.0 4.3 copy-start.17
  352.9 7.9 %all-to-all-start.10 = ((bf16[4,128,4]{1,2,0:T(4,128)(2,1)}), bf16[4,128,4]{1,2,0:T(4,128)(2,1)S(1)}, u32[]{:S(2)}, u32[]{:S(2)}) async-start(bf16[4,128,4]{1,2,0:T(4,128)(2,1)} %fusion.55), calls=%async_computation.10 | async-start | bytes 8192 | tf_op jit(solution)/shard_map/all_to_all | solution.py:151
  356.1 9.0 %copy-start.4 = (f32[1,128,2048]{1,0,2:T(1,128)S(1)}, f32[1,128,2048]{1,0,2:T(1,128)}, u32[]{:S(2)}) copy-start(f32[1,128,2048]{1,0,2:T(1,128)} %copy-done.2) | copy-start | bytes 3145732
  360.8 7.8 %copy-start.7 = (f32[4,4,128,128]{2,3,1,0:T(8,128)S(1)}, f32[4,4,128,128]{2,3,1,0:T(8,128)}, u32[]{:S(2)}) copy-start(f32[4,4,128,128]{2,3,1,0:T(8,128)} %copy-done.5) | copy-start | bytes 3145732
  360.8 7.8 %copy-start.11 = (f32[4,4,128,128]{3,2,1,0:T(8,128)S(1)}, f32[4,4,128,128]{3,2,1,0:T(8,128)}, u32[]{:S(2)}) copy-start(f32[4,4,128,128]{3,2,1,0:T(8,128)} %copy-done.10) | copy-start | bytes 3145732
  360.8 10.9 %all-to-all-start.6 = ((bf16[4,128,512]{1,2,0:T(8,128)(2,1)}), bf16[4,128,512]{1,2,0:T(8,128)(2,1)}, u32[]{:S(2)}, u32[]{:S(2)}) async-start(bf16[4,128,512]{1,2,0:T(8,128)(2,1)} %bitcast.190), calls=%async_computation.6 | async-start | bytes 1048576 | tf_op jit(solution)/shard_map/all_to_all | solution.py:147
  371.7 10.2 %all-to-all-start.7 = ((bf16[4,128,512]{1,2,0:T(8,128)(2,1)}), bf16[4,128,512]{1,2,0:T(8,128)(2,1)S(1)}, u32[]{:S(2)}, u32[]{:S(2)}) async-start(bf16[4,128,512]{1,2,0:T(8,128)(2,1)} %bitcast.189), calls=%async_computation.7 | async-start | bytes 1048576 | tf_op jit(solution)/shard_map/all_to_all | solution.py:148
  375.2 3.3 copy-start.25
  375.2 70.4 %all-reduce.2.cloned.1.call-start = ((), (), s32[]{:S(2)}) async-start(), calls=%async_computation.11 | async-start | bytes 4194304 | tf_op jit(solution)/shard_map/psum | solution.py:153
  378.5 6.9 %copy-start.22 = (f32[4,4,128,128]{2,3,1,0:T(8,128)S(1)}, f32[4,4,128,128]{2,3,1,0:T(8,128)}, u32[]{:S(2)}) copy-start(f32[4,4,128,128]{2,3,1,0:T(8,128)} %get-tuple-element.33) | copy-start | bytes 3145732
  381.9 3.5 copy-start.26
  381.9 33.4 %all-to-all-start.8 = ((bf16[4,128,512]{1,2,0:T(8,128)(2,1)}), bf16[4,128,512]{1,2,0:T(8,128)(2,1)S(1)}, u32[]{:S(2)}, u32[]{:S(2)}) async-start(bf16[4,128,512]{1,2,0:T(8,128)(2,1)} %bitcast.56), calls=%async_computation.8 | async-start | bytes 1048576 | tf_op jit(solution)/shard_map/all_to_all | solution.py:149
  414.1 7.4 %copy-start.27 = (bf16[4,128,512]{1,2,0:T(8,128)(2,1)S(1)}, bf16[4,128,512]{1,2,0:T(8,128)(2,1)}, u32[]{:S(2)}) copy-start(bf16[4,128,512]{1,2,0:T(8,128)(2,1)} %copy-done.26) | copy-start | bytes 1572868
  415.3 10.7 %all-to-all-start.9 = ((bf16[4,128,512]{1,2,0:T(8,128)(2,1)}), bf16[4,128,512]{1,2,0:T(8,128)(2,1)S(1)}, u32[]{:S(2)}, u32[]{:S(2)}) async-start(bf16[4,128,512]{1,2,0:T(8,128)(2,1)} %bitcast.61), calls=%async_computation.9 | async-start | bytes 1048576 | tf_op jit(solution)/shard_map/all_to_all | solution.py:150
  426.0 23.5 %copy-start.1 = (f32[8,4,128,128]{3,2,1,0:T(8,128)S(1)}, f32[8,4,128,128]{3,2,1,0:T(8,128)}, u32[]{:S(2)}) copy-start(f32[8,4,128,128]{3,2,1,0:T(8,128)} %param.17) | copy-start | bytes 6291460
Sparse Core Ops, SparseCore 0:
  379.0 66.5 all-reduce.1
where the time goes:
time: 464 us; the launch traced here: 457 us
  other arithmetic  269 us (58%)
  local copies, waits for them, and re-layouts  48 us (10%)
  starting transfers between devices  45 us (10%)
  matrix products  43.5 us (9%)
  waiting for transfers between devices  35.9 us (8%)
  between operations  15.1 us (3%)
    another operation x4, other arithmetic, decay_forward(): jax.scipy.linalg.solve_triangular(identity_block + coupling, target_outpu...  160 us
    unnamed x6, other arithmetic  58.8 us
    unnamed x81, local copies, waits for them, and re-layouts  38.2 us
    another operation x2, other arithmetic, decay_forward(): cum_decay = jnp.cumsum(decay_value, axis=1)  33.2 us
    psum x1, waiting for transfers between devices, per_device(): grad_fork = lax.psum(prompt_grad, 'grp')  18.6 us
  transfers between devices with their start and end apart: 12, of which 8 were waited for; matrix products, arithmetic and copies ran while one was open for 33% of the time, Pallas kernels for 0%

commit v1 on v0

v1 whole, which is shorter than its diff:
```python
import functools

import jax
import jax.numpy as jnp
from jax import lax
from jax.experimental import pallas as pl
from jax.experimental.pallas import tpu as pltpu
from jax.sharding import PartitionSpec as P

HIGH = lax.Precision.HIGH
NN = ((1,), (0,))
NT = ((1,), (1,))
TN = ((0,), (0,))
F32 = jnp.float32
BF16 = jnp.bfloat16


def dot(a, b, dims=NN, precision=None):
    return lax.dot_general(
        a, b, (dims, ((), ())), preferred_element_type=F32, precision=precision
    )


def split(x):
    high = x.astype(BF16)
    return high, (x - high.astype(F32)).astype(BF16)


def encode(x):
    return (x * x * x * jnp.abs(x)).astype(BF16)


def decode(y):
    wide = y.astype(F32)
    root = jnp.sqrt(jnp.sqrt(jnp.abs(wide)))
    return jnp.where(wide < 0, -root, root)


def iota2(shape, axis):
    return lax.broadcasted_iota(jnp.int32, shape, axis)


def unit_lower_inverse(matrices):
    size = matrices[0].shape[0]
    blocks = size // 8
    row, col = iota2((size, size), 0), iota2((size, size), 1)
    on_block = row // 8 == col // 8
    lane8 = iota2((8, size), 1)
    identity8 = (iota2((8, size), 0) == lane8 % 8).astype(F32)
    inverses = []
    for a in matrices:
        compact = jnp.sum(jnp.where(on_block, a, 0.0).reshape(blocks, 8, size), axis=0)
        inverse = identity8
        for m in range(7):
            column = jnp.take_along_axis(compact, lane8 // 8 * 8 + m, axis=1)
            inverse = inverse - column * inverse[m : m + 1]
        inverses.append(jnp.where(on_block, jnp.concatenate([inverse] * blocks, axis=0), 0.0))
    width = 8
    while width * 2 < size:
        lower = (row // (2 * width) == col // (2 * width)) & (row // width > col // width)
        inner = [
            dot(jnp.where(lower, a, 0.0), d, precision=HIGH) for a, d in zip(matrices, inverses)
        ]
        inverses = [d - dot(d, x, precision=HIGH) for d, x in zip(inverses, inner)]
        width *= 2
    results = []
    inner = [
        dot(a[width:, :width], d[:width, :width], precision=HIGH)
        for a, d in zip(matrices, inverses)
    ]
    corner = [dot(d[width:, width:], x, precision=HIGH) for d, x in zip(inverses, inner)]
    for d, x in zip(inverses, corner):
        bottom = jnp.concatenate([-x, d[width:, width:]], axis=1)
        results.append(jnp.concatenate([d[:width], bottom], axis=0))
    return results


def decayed_rows(query_in, key_in, decay_in, valid, tri):
    tokens, head_dim = query_in.shape
    row = iota2((tokens, 1), 0)
    query = query_in.astype(F32)
    key = key_in.astype(F32)
    query_scale = lax.rsqrt(jnp.sum(query * query, axis=1, keepdims=True) + 1e-06)
    key_scale = lax.rsqrt(jnp.sum(key * key, axis=1, keepdims=True) + 1e-06)
    unit_query = query * query_scale
    unit_key = key * key_scale
    decay = jnp.where(row < valid, decay_in, jnp.zeros_like(decay_in))
    cumulative = dot(tri, decay)
    middle = cumulative[tokens // 2 - 1 : tokens // 2]
    cumulative = cumulative - middle
    grow = jnp.exp(cumulative)
    shrink = jnp.exp(-cumulative)
    return dict(
        unit_query=unit_query,
        unit_key=unit_key,
        query_scale=query_scale,
        key_scale=key_scale,
        grow=grow,
        shrink=shrink,
        start=jnp.exp(middle),
        key_forward=unit_key * grow,
        key_earlier=unit_key * shrink,
        query_forward=unit_query * (grow * head_dim**-0.5),
    )


def head_column(values, head):
    lane = iota2(values.shape, 1)
    return jnp.sum(jnp.where(lane == head, values, 0.0), axis=1, keepdims=True)


def first_kernel(
    per_step,
    valid_ref,
    query_ref,
    key_ref,
    decay_ref,
    grad_ref,
    beta_ref,
    value_grad_ref,
    wide_ref,
    inverse_ref,
    coded_ref,
):
    tokens = query_ref.shape[1]
    head_dim = query_ref.shape[2] // per_step
    pieces = coded_ref.shape[0]
    valid = valid_ref[pl.program_id(0)]
    row, col = iota2((tokens, tokens), 0), iota2((tokens, tokens), 1)
    tri = (row >= col).astype(BF16)
    keep = iota2((tokens, 1), 0) < valid
    betas = jax.nn.sigmoid(beta_ref[0].astype(F32)) * keep.astype(F32)
    rows, beta, out_grad = [], [], []
    for j in range(per_step):
        lanes = slice(j * head_dim, (j + 1) * head_dim)
        rows.append(
            decayed_rows(
                query_ref[0, :, lanes], key_ref[0, :, lanes], decay_ref[0, :, lanes], valid, tri
            )
        )
        beta.append(head_column(betas, pl.program_id(1) * per_step + j))
        grad = grad_ref[0, :, lanes]
        out_grad.append(jnp.where(keep, grad, jnp.zeros_like(grad)))
    scores = [
        dot(
            jnp.concatenate([r["key_forward"], r["query_forward"]], axis=0),
            r["key_earlier"],
            NT,
            HIGH,
        )
        for r in rows
    ]
    coupling = [jnp.where(row > col, s[:tokens], 0.0) * b for s, b in zip(scores, beta)]
    attend = [jnp.where(row >= col, s[tokens:], 0.0) for s in scores]
    inverse = unit_lower_inverse(coupling)
    update_grad = []
    for p, g in zip(attend, out_grad):
        high, low = split(p)
        update_grad.append(dot(high, g, TN) + dot(low, g, TN))
    value_grad = [b * dot(d, u, TN, HIGH) for b, d, u in zip(beta, inverse, update_grad)]
    for j in range(per_step):
        r = rows[j]
        high, low = split(r["query_forward"] * r["start"])
        state_grad = (
            dot(high, out_grad[j], TN)
            + dot(low, out_grad[j], TN)
            - dot(r["key_forward"] * r["start"], value_grad[j], TN, HIGH)
        )
        coded_ref[:, j] = encode(state_grad).reshape(pieces, head_dim // pieces, head_dim)
        lanes = slice(j * head_dim, (j + 1) * head_dim)
        value_grad_ref[0, :, lanes] = value_grad[j].astype(BF16)
        wide_ref[0, j] = value_grad[j]
        inverse_ref[0, j] = inverse[j]


def second_kernel(
    per_step,
    valid_ref,
    query_ref,
    key_ref,
    value_ref,
    decay_ref,
    grad_ref,
    beta_ref,
    wide_ref,
    inverse_ref,
    state_ref,
    query_grad_ref,
    key_grad_ref,
    decay_grad_ref,
    beta_grad_ref,
):
    tokens = query_ref.shape[1]
    head_dim = query_ref.shape[2] // per_step
    valid = valid_ref[pl.program_id(0)]
    row, col = iota2((tokens, tokens), 0), iota2((tokens, tokens), 1)
    tri = (row >= col).astype(BF16)
    keep = iota2((tokens, 1), 0) < valid
    logits = beta_ref[0].astype(F32)
    betas = jax.nn.sigmoid(logits) * keep.astype(F32)
    ratios = jnp.exp(-logits)
    beta_grad = jnp.zeros(logits.shape, F32)
    heads = range(per_step)
    lanes = [slice(j * head_dim, (j + 1) * head_dim) for j in heads]
    number = [pl.program_id(1) * per_step + j for j in heads]
    rows = [
        decayed_rows(
            query_ref[0, :, lanes[j]],
            key_ref[0, :, lanes[j]],
            decay_ref[0, :, lanes[j]],
            valid,
            tri,
        )
        for j in heads
    ]
    beta = [head_column(betas, n) for n in number]
    target = [
        value_ref[0, :, lanes[j]].astype(F32)
        - dot(rows[j]["key_forward"] * rows[j]["start"], state_ref[j], precision=HIGH)
        for j in heads
    ]
    update = [dot(inverse_ref[0, j], beta[j] * target[j], precision=HIGH) for j in heads]
    wide = [wide_ref[0, j] for j in heads]
    both = []
    for j in heads:
        grad = grad_ref[0, :, lanes[j]]
        grad = jnp.where(keep, grad, jnp.zeros_like(grad)).astype(F32)
        both.append(jnp.concatenate([grad, -wide[j]], axis=0))
    score_grad = [dot(both[j], update[j], NT, HIGH) for j in heads]
    attend_grad = [jnp.where(row >= col, s[:tokens], 0.0) for s in score_grad]
    coupling_grad = [jnp.where(row > col, s[tokens:], 0.0) for s in score_grad]
    for j in heads:
        r = rows[j]
        through_state = dot(both[j], state_ref[j], NT, HIGH) * r["start"]
        through_rows = dot(
            jnp.concatenate([attend_grad[j], coupling_grad[j]], axis=0),
            r["key_earlier"],
            precision=HIGH,
        )
        forward = through_state + through_rows
        earlier = dot(
            jnp.concatenate([attend_grad[j], coupling_grad[j]], axis=0),
            jnp.concatenate([r["query_forward"], r["key_forward"]], axis=0),
            TN,
            HIGH,
        )
        query_unit_grad = forward[:tokens] * r["grow"] * head_dim**-0.5
        key_later = forward[tokens:] * r["grow"]
        key_before = earlier * r["shrink"]
        key_unit_grad = key_later + key_before
        decay_step = r["unit_query"] * query_unit_grad + r["unit_key"] * (key_later - key_before)
        high, low = split(decay_step)
        decay_grad = dot(tri, high, TN) + dot(tri, low, TN)
        decay_grad_ref[0, :, lanes[j]] = jnp.where(keep, decay_grad, 0.0).astype(BF16)
        along = jnp.sum(r["unit_query"] * query_unit_grad, axis=1, keepdims=True)
        query_grad_ref[0, :, lanes[j]] = (
            r["query_scale"] * (query_unit_grad - r["unit_query"] * along)
        ).astype(BF16)
        along = jnp.sum(r["unit_key"] * key_unit_grad, axis=1, keepdims=True)
        key_grad_ref[0, :, lanes[j]] = (
            r["key_scale"] * (key_unit_grad - r["unit_key"] * along)
        ).astype(BF16)
        strength = jnp.sum(wide[j] * update[j], axis=1, keepdims=True)
        beta_grad = jnp.where(iota2(logits.shape, 1) == number[j], strength * ratios, beta_grad)

    @pl.when(pl.program_id(1) == 0)
    def _():
        beta_grad_ref[0] = beta_grad.astype(BF16)

    @pl.when(pl.program_id(1) > 0)
    def _():
        beta_grad_ref[0] = (beta_grad_ref[0].astype(F32) + beta_grad).astype(BF16)


def sum_kernel(prompt_ref, coded_ref, out_ref, total_ref):
    total_ref[...] = jnp.zeros_like(total_ref)

    def add(branch, carry):
        prompt = prompt_ref[branch]
        total_ref[prompt] += decode(coded_ref[branch])
        return carry

    lax.fori_loop(0, coded_ref.shape[0], add, 0)
    out_ref[...] = encode(total_ref[...])


def spread_kernel(place_ref, *refs):
    out_ref = refs[-1]
    for i, piece in enumerate(refs[:-1]):
        out_ref[:, :, pl.ds(place_ref[i], 1)] = decode(piece[...])[:, :, None]


def gather_pieces(piece, axis_name):
    size = lax.axis_size(axis_name)
    me = lax.axis_index(axis_name)
    pieces, places = [piece], [me]
    chips = size // 2
    power = chips & (chips - 1) == 0
    for step in range(1, chips):
        other = [((c ^ step) if power else (c + step) % chips) for c in range(chips)]
        moves = [(2 * c + core, 2 * other[c] + core) for c in range(chips) for core in range(2)]
        pieces.append(lax.ppermute(piece, axis_name, moves))
        chip = me // 2
        source = (chip ^ step) if power else (chip - step) % chips
        places.append(2 * source + me % 2)
    swap = [(i, i ^ 1) for i in range(size)]
    swapped = [lax.ppermute(x, axis_name, swap) for x in pieces]
    return pieces + swapped, places + [p ^ 1 for p in places]


def per_device(
    query_rows,
    key_rows,
    value_rows,
    log_decay,
    beta_logit,
    out_grad,
    fork_state,
    branch_prompt,
    valid_len,
):
    count, tokens, width = query_rows.shape
    prompts, heads_here, head_dim, _ = fork_state.shape
    members = lax.axis_size("head")
    groups = lax.axis_size("grp")
    heads = members * heads_here
    piece_rows = head_dim // groups
    first_branch = (lax.axis_index("grp") * members + lax.axis_index("head")) * count
    valid = lax.dynamic_slice_in_dim(valid_len, first_branch, count)
    group_prompt = lax.dynamic_slice_in_dim(
        branch_prompt, lax.axis_index("grp") * members * count, members * count
    )
    chosen = jnp.take(fork_state, group_prompt, axis=0)
    states = lax.all_to_all(
        chosen.reshape(members, count * heads_here, head_dim, head_dim), "head", 0, 0, tiled=True
    )
    states = (
        states.reshape(members, count, heads_here, head_dim, head_dim)
        .transpose(1, 0, 2, 3, 4)
        .reshape(count * heads, head_dim, head_dim)
    )

    per_step = next(n for n in (4, 2, 1) if heads % n == 0)
    steps = heads // per_step
    row_block = pl.BlockSpec((1, tokens, per_step * head_dim), lambda b, i, *_: (b, 0, i))
    beta_block = pl.BlockSpec((1, tokens, heads), lambda b, i, *_: (b, 0, 0))
    square_block = pl.BlockSpec((1, per_step, tokens, tokens), lambda b, i, *_: (b, i, 0, 0))
    wide_block = pl.BlockSpec((1, per_step, tokens, head_dim), lambda b, i, *_: (b, i, 0, 0))
    params = pltpu.CompilerParams(vmem_limit_bytes=48 * 2**20)
    rows_type = jax.ShapeDtypeStruct(query_rows.shape, BF16)
    units = count * heads * tokens * tokens * head_dim

    value_grad, wide, inverse, coded = pl.pallas_call(
        functools.partial(first_kernel, per_step),
        grid_spec=pltpu.PrefetchScalarGridSpec(
            num_scalar_prefetch=1,
            grid=(count, steps),
            in_specs=[row_block, row_block, row_block, row_block, beta_block],
            out_specs=[
                row_block,
                wide_block,
                square_block,
                pl.BlockSpec(
                    (groups, per_step, piece_rows, head_dim),
                    lambda b, i, *_: (0, b * steps + i, 0, 0),
                ),
            ],
        ),
        out_shape=[
            rows_type,
            jax.ShapeDtypeStruct((count, heads, tokens, head_dim), F32),
            jax.ShapeDtypeStruct((count, heads, tokens, tokens), F32),
            jax.ShapeDtypeStruct((groups, count * heads, piece_rows, head_dim), BF16),
        ],
        compiler_params=params,
        cost_estimate=pl.CostEstimate(flops=80 * units, bytes_accessed=2**23, transcendentals=0),
        name="state_independent",
    )(valid, query_rows, key_rows, log_decay, out_grad, beta_logit)

    coded = (
        coded.reshape(groups, count, members, heads_here, piece_rows, head_dim)
        .transpose(0, 2, 1, 3, 4, 5)
        .reshape(groups * members, count, heads_here, piece_rows, head_dim)
    )
    arrived = lax.all_to_all(coded, ("grp", "head"), 0, 0, tiled=True)

    query_grad, key_grad, decay_grad, beta_grad = pl.pallas_call(
        functools.partial(second_kernel, per_step),
        grid_spec=pltpu.PrefetchScalarGridSpec(
            num_scalar_prefetch=1,
            grid=(count, steps),
            in_specs=[
                row_block,
                row_block,
                row_block,
                row_block,
                row_block,
                beta_block,
                wide_block,
                square_block,
                pl.BlockSpec(
                    (per_step, head_dim, head_dim), lambda b, i, *_: (b * steps + i, 0, 0)
                ),
            ],
            out_specs=[row_block, row_block, row_block, beta_block],
        ),
        out_shape=[
            rows_type,
            rows_type,
            rows_type,
            jax.ShapeDtypeStruct(beta_logit.shape, BF16),
        ],
        compiler_params=params,
        cost_estimate=pl.CostEstimate(flops=80 * units, bytes_accessed=2**23, transcendentals=0),
        name="state_dependent",
    )(
        valid,
        query_rows,
        key_rows,
        value_rows,
        log_decay,
        out_grad,
        beta_logit,
        wide,
        inverse,
        states,
    )

    piece_shape = (prompts, heads_here, piece_rows, head_dim)
    branches = groups * members * count
    whole = pl.BlockSpec(memory_space=pltpu.VMEM)
    scalars = pl.BlockSpec(memory_space=pltpu.SMEM)
    piece = pl.pallas_call(
        sum_kernel,
        in_specs=[scalars, whole],
        out_specs=whole,
        out_shape=jax.ShapeDtypeStruct(piece_shape, BF16),
        scratch_shapes=[pltpu.VMEM(piece_shape, F32)],
        compiler_params=params,
        name="sum_by_prompt",
    )(branch_prompt, arrived.reshape(branches, heads_here, piece_rows, head_dim))
    pieces, places = gather_pieces(piece, "grp")
    grad_fork = pl.pallas_call(
        spread_kernel,
        in_specs=[scalars] + [whole] * len(pieces),
        out_specs=whole,
        out_shape=jax.ShapeDtypeStruct(
            (prompts, heads_here, groups, piece_rows, head_dim), F32
        ),
        compiler_params=params,
        name="spread_pieces",
    )(jnp.stack(places).astype(jnp.int32), *pieces)
    return (
        query_grad,
        key_grad,
        value_grad,
        decay_grad,
        beta_grad,
        grad_fork.reshape(fork_state.shape),
    )


def solution(mesh):
    rows = P(("grp", "head"), None, None)
    state = P(None, "head", None, None)
    return jax.shard_map(
        per_device,
        mesh=mesh,
        in_specs=(rows, rows, rows, rows, rows, rows, state, P(), P()),
        out_specs=(rows, rows, rows, rows, rows, state),
        check_vma=False,
    )
```

time: 464 us -> 88.3 us (0.19); the launches traced: 457 us -> 87.4 us
  other arithmetic: 269 us -> 2.47 us
  matrix products: 43.5 us -> 0 us
  local copies, waits for them, and re-layouts: 48 us -> 18.4 us
  starting transfers between devices: 45 us -> 16.5 us
  Pallas kernels: 0 us -> 28.1 us
  waiting for transfers between devices: 35.9 us -> 21.1 us
  between operations: 15.1 us -> 0.73 us
    another operation x6 -> x0, other arithmetic: 194 us -> none  [the longest x4 160 us: decay_forward(): jax.scipy.linalg.solve_triangular(identity_block + coupling, target_outpu...]
    unnamed x6 -> x0, other arithmetic: 58.8 us -> none
    dot_general x16 -> x0, matrix products: 34.9 us -> none  [the longest x3 7.5 us: decay_forward(): jnp.einsum('htk,hsk->hts', key_forward_rows, key_earlier_rows, precision=...]
    all_to_all x11 -> x2, starting transfers between devices: 45 us -> 11.5 us  [the longest x1 7.29 us: per_device(): arrived = lax.all_to_all(coded, ('grp', 'head'), 0, 0, tiled=True)]
    pallas_call x0 -> x4, Pallas kernels: none -> 28.1 us  [the longest x1 11.8 us: per_device(): pl.pallas_call(functools.partial(first_kernel, per_step), grid_spec=pltpu...]
    unnamed x81 -> x32, local copies, waits for them, and re-layouts: 38.2 us -> 15.4 us
    psum x1 -> x0, waiting for transfers between devices: 18.6 us -> none  [per_device(): grad_fork = lax.psum(prompt_grad, 'grp')]
    convert_element_type x10 -> x0, other arithmetic: 12.5 us -> none  [the longest x4 7.58 us: split_heads(): array_in.astype(jnp.float32)]
  transfers between devices with their start and end apart: 12 -> 9, of which waited for: 8 -> 3; matrix products, arithmetic and copies ran while one was open for 33% -> 6% of each run, Pallas kernels for 0% -> 15%
where the time goes in v1:
time: 88.3 us; the launch traced here: 87.4 us
  Pallas kernels  28.1 us (32%)
  waiting for transfers between devices  21.1 us (24%)
  local copies, waits for them, and re-layouts  18.4 us (21%)
  starting transfers between devices  16.5 us (19%)
  other arithmetic  2.47 us (3%)
    unnamed x32, local copies, waits for them, and re-layouts  15.4 us
    all_to_all x1, waiting for transfers between devices, per_device(): arrived = lax.all_to_all(coded, ('grp', 'head'), 0, 0, tiled=True)  12.1 us
    pallas_call x1, Pallas kernels, per_device(): pl.pallas_call(functools.partial(first_kernel, per_step), grid_spec=pltpu...  11.8 us
    pallas_call x1, Pallas kernels, per_device(): pl.pallas_call(functools.partial(second_kernel, per_step), grid_spec=pltp...  11.7 us
    ppermute x3, waiting for transfers between devices, gather_pieces(): pieces.append(lax.ppermute(piece, axis_name, moves))  8.95 us
    all_to_all x1, starting transfers between devices, per_device(): arrived = lax.all_to_all(coded, ('grp', 'head'), 0, 0, tiled=True)  7.29 us
    ppermute x3, starting transfers between devices, gather_pieces(): pieces.append(lax.ppermute(piece, axis_name, moves))  4.45 us
    all_to_all x1, starting transfers between devices, per_device(): lax.all_to_all(chosen.reshape(members, count * heads_here, head_dim, head...  4.25 us
  transfers between devices with their start and end apart: 9, of which 3 were waited for; matrix products, arithmetic and copies ran while one was open for 6% of the time, Pallas kernels for 15%

profile of v1, /device:TPU:0, one launch (start us, length us, event | category | flops | bytes accessed | tf_op | source)
XLA Modules:
  0.0 87.4 jit_solution(14876306684677524149)
XLA Ops:
  0.6 0.0 copy-start
  0.7 0.9 %copy.19.beta_ref = bf16[1,128,16]{2,1,0:T(8,128)(2,1)S(1)} copy(bf16[1,128,16]{1,2,0:T(8,128)(2,1)} %param.13) | data formatting | bytes 8192 | tf_op args[4]
  1.6 1.3 %dynamic_slice.6.valid_ref = s32[1]{0:T(128)} dynamic-slice(s32[32]{0:T(128)} %param.17, s32[]{:T(128)S(6)} %select_n.32), dynamic_slice_sizes={1} | dynamic-slice | bytes 12 | tf_op jit(solution)/shard_map/dynamic_slice | solution.py:329
  2.9 0.0 copy-start.2
  2.9 1.0 %copy-done.2 = bf16[1,128,2048]{2,1,0:T(8,128)(2,1)S(1)} copy-done((bf16[1,128,2048]{2,1,0:T(8,128)(2,1)S(1)}, bf16[1,128,2048]{2,1,0:T(8,128)(2,1)}, u32[]{:S(2)}) %copy-start.2) | copy-done | bytes 524312
  3.9 0.0 copy-start.4
  4.0 1.0 %copy-done.4 = bf16[1,128,2048]{2,1,0:T(8,128)(2,1)S(1)} copy-done((bf16[1,128,2048]{2,1,0:T(8,128)(2,1)S(1)}, bf16[1,128,2048]{2,1,0:T(8,128)(2,1)}, u32[]{:S(2)}) %copy-start.4) | copy-done | bytes 524312
  5.0 0.0 copy-start.7
  5.0 1.0 %copy-done.7 = bf16[1,128,2048]{2,1,0:T(8,128)(2,1)S(1)} copy-done((bf16[1,128,2048]{2,1,0:T(8,128)(2,1)S(1)}, bf16[1,128,2048]{2,1,0:T(8,128)(2,1)}, u32[]{:S(2)}) %copy-start.7) | copy-done | bytes 524312
  6.0 1.0 %copy-done.9 = bf16[1,128,2048]{2,1,0:T(8,128)(2,1)S(1)} copy-done((bf16[1,128,2048]{2,1,0:T(8,128)(2,1)S(1)}, bf16[1,128,2048]{2,1,0:T(8,128)(2,1)}, u32[]{:S(2)}) %copy-start.9) | copy-done | bytes 524312
  7.1 11.8 %state_independent.1 = (bf16[1,128,2048]{2,1,0:T(8,128)(2,1)}, f32[1,16,128,128]{3,2,1,0:T(8,128)S(1)}, f32[1,16,128,128]{3,2,1,0:T(8,128)S(1)}, bf16[8,16,16,128]{3,2,1,0:T(8,128)(2,1)}) custom-call(s32[1]{0:T(128)} %dynamic_slice.6.valid_ref, bf16[1,128,2048]{2,1,0:T(8,128)(2,1)S(1)} %copy-done.2, bf16[1,128,2048]{2,1,0:T(8,128)(2,1)S(1)} %copy-done.4, ...), custom_call_target="tpu_custom_call" | custom-call | flops 2684354560 | bytes 8388608 | tf_op jit(solution)/shard_map/state_independent/pallas_call | solution.py:353
  18.9 1.0 %copy-done.11 = f32[1,16,128,128]{3,2,1,0:T(8,128)} copy-done((f32[1,16,128,128]{3,2,1,0:T(8,128)}, f32[1,16,128,128]{3,2,1,0:T(8,128)S(1)}, u32[]{:S(2)}) %copy-start.11) | copy-done | bytes 1048600
  19.9 1.0 %copy-done.13 = f32[1,16,128,128]{3,2,1,0:T(8,128)} copy-done((f32[1,16,128,128]{3,2,1,0:T(8,128)}, f32[1,16,128,128]{3,2,1,0:T(8,128)S(1)}, u32[]{:S(2)}) %copy-start.13) | copy-done | bytes 1048600
  20.9 7.3 %all-to-all-start.1 = ((bf16[32,1,4,16,128]{4,3,2,1,0:T(8,128)(2,1)}), bf16[32,1,4,16,128]{4,3,2,1,0:T(8,128)(2,1)S(1)}, u32[]{:S(2)}, u32[]{:S(2)}) async-start(bf16[32,1,4,16,128]{4,3,2,1,0:T(8,128)(2,1)} %bitcast.10), calls=%async_computation.1 | async-start | bytes 1048576 | tf_op jit(solution)/shard_map/all_to_all | solution.py:385
  28.2 0.0 copy-done.1
  28.2 0.1 compare_and_fusion
  28.3 0.0 copy-done
  28.3 1.6 %gather_fusion = f32[4,4,128,128]{3,2,1,0:T(8,128)} fusion(f32[8,4,128,128]{3,2,1,0:T(8,128)S(1)} %copy-done, s32[1024]{0:T(1024)S(1)} %pad_clamp_fusion), kind=kCustom, calls=%fused_computation | custom fusion | bytes 2097168 | tf_op jit(solution)/shard_map/jit(_take)/gather | solution.py:333
  29.9 2.4 %broadcast_select_fusion = f32[4,4,128,128]{3,2,1,0:T(8,128)} fusion(f32[4,4,128,128]{3,2,1,0:T(8,128)} %gather_fusion, pred[4]{0:T(512)(128)(4,1)S(1)} %get-tuple-element.34), kind=kLoop, calls=%fused_computation.1 | loop fusion | flops 262144 | bytes 2097156 | tf_op jit(solution)/shard_map/jit(_take)/select_n | solution.py:333
  32.3 12.1 %all-to-all-done.1 = bf16[32,1,4,16,128]{4,3,2,1,0:T(8,128)(2,1)S(1)} async-done(((bf16[32,1,4,16,128]{4,3,2,1,0:T(8,128)(2,1)}), bf16[32,1,4,16,128]{4,3,2,1,0:T(8,128)(2,1)S(1)}, u32[]{:S(2)}, u32[]{:S(2)}) %all-to-all-start.1) | async-done | bytes 524320 | tf_op jit(solution)/shard_map/all_to_all | solution.py:385
  44.4 4.2 %all-to-all-start = ((f32[4,4,128,128]{3,2,1,0:T(8,128)}), f32[4,4,128,128]{3,2,1,0:T(8,128)}, u32[]{:S(2)}, u32[]{:S(2)}) async-start(f32[4,4,128,128]{3,2,1,0:T(8,128)} %broadcast_select_fusion), calls=%async_computation | async-start | bytes 2097152 | tf_op jit(solution)/shard_map/all_to_all | solution.py:334
  48.7 1.5 %sum_by_prompt.1.refs_0_ = bf16[8,4,16,128]{3,2,1,0:T(8,128)(2,1)S(1)} custom-call(s32[32]{0:T(128)S(1)} %copy-done.1, bf16[32,4,16,128]{3,2,1,0:T(8,128)(2,1)S(1)} %bitcast.14), custom_call_target="tpu_custom_call" | custom-call | tf_op jit(solution)/shard_map/sum_by_prompt/pallas_call | solution.py:433
  50.2 1.5 %collective-permute-start.2 = (bf16[8,4,16,128]{3,2,1,0:T(8,128)(2,1)S(1)}, bf16[8,4,16,128]{3,2,1,0:T(8,128)(2,1)S(1)}, u32[]{:S(2)}, u32[]{:S(2)}) collective-permute-start(bf16[8,4,16,128]{3,2,1,0:T(8,128)(2,1)S(1)} %sum_by_prompt.1.refs_0_), channel_id=1, source_target_pairs={{0,24},{4,28},{8,16},{12,20},{16,8},{20,12},{24,0},{28,4},{1,25},{... | collective-permute-start | bytes 393224 | tf_op jit(solution)/shard_map/ppermute | solution.py:302
  51.7 0.9 %collective-permute-start.1 = (bf16[8,4,16,128]{3,2,1,0:T(8,128)(2,1)S(1)}, bf16[8,4,16,128]{3,2,1,0:T(8,128)(2,1)S(1)}, u32[]{:S(2)}, u32[]{:S(2)}) collective-permute-start(bf16[8,4,16,128]{3,2,1,0:T(8,128)(2,1)S(1)} %sum_by_prompt.1.refs_0_), channel_id=1, source_target_pairs={{0,16},{4,20},{8,24},{12,28},{16,0},{20,4},{24,8},{28,12},{1,17},{... | collective-permute-start | bytes 393224 | tf_op jit(solution)/shard_map/ppermute | solution.py:302
  52.7 2.0 %collective-permute-start = (bf16[8,4,16,128]{3,2,1,0:T(8,128)(2,1)S(1)}, bf16[8,4,16,128]{3,2,1,0:T(8,128)(2,1)S(1)}, u32[]{:S(2)}, u32[]{:S(2)}) collective-permute-start(bf16[8,4,16,128]{3,2,1,0:T(8,128)(2,1)S(1)} %sum_by_prompt.1.refs_0_), channel_id=1, source_target_pairs={{0,8},{4,12},{8,0},{12,4},{16,24},{20,28},{24,16},{28,20},{1,9},{5... | collective-permute-start | bytes 393224 | tf_op jit(solution)/shard_map/ppermute | solution.py:302
  54.7 0.1 stack.35.place_ref
  54.7 0.0 collective-permute-start.3
  54.8 3.8 %collective-permute-done.2.refs_3_ = bf16[8,4,16,128]{3,2,1,0:T(8,128)(2,1)S(1)} collective-permute-done((bf16[8,4,16,128]{3,2,1,0:T(8,128)(2,1)S(1)}, bf16[8,4,16,128]{3,2,1,0:T(8,128)(2,1)S(1)}, u32[]{:S(2)}, u32[]{:S(2)}) %collective-permute-start.2) | collective-permute-done | bytes 131104 | tf_op jit(solution)/shard_map/ppermute | solution.py:302
  58.5 0.0 collective-permute-start.6
  58.5 5.2 %collective-permute-done.1.refs_2_ = bf16[8,4,16,128]{3,2,1,0:T(8,128)(2,1)S(1)} collective-permute-done((bf16[8,4,16,128]{3,2,1,0:T(8,128)(2,1)S(1)}, bf16[8,4,16,128]{3,2,1,0:T(8,128)(2,1)S(1)}, u32[]{:S(2)}, u32[]{:S(2)}) %collective-permute-start.1) | collective-permute-done | bytes 131104 | tf_op jit(solution)/shard_map/ppermute | solution.py:302
  63.7 0.0 collective-permute-start.5
  63.7 0.0 collective-permute-done.refs_1_
  63.7 0.5 collective-permute-start.4
  64.2 0.0 all-to-all-done
  64.2 1.0 %copy-done.3 = bf16[1,128,2048]{2,1,0:T(8,128)(2,1)S(1)} copy-done((bf16[1,128,2048]{2,1,0:T(8,128)(2,1)S(1)}, bf16[1,128,2048]{2,1,0:T(8,128)(2,1)}, u32[]{:S(2)}) %copy-start.3) | copy-done | bytes 524312
  65.3 1.0 %copy-done.5 = bf16[1,128,2048]{2,1,0:T(8,128)(2,1)S(1)} copy-done((bf16[1,128,2048]{2,1,0:T(8,128)(2,1)S(1)}, bf16[1,128,2048]{2,1,0:T(8,128)(2,1)}, u32[]{:S(2)}) %copy-start.5) | copy-done | bytes 524312
  66.3 1.0 %copy-done.6 = bf16[1,128,2048]{2,1,0:T(8,128)(2,1)S(1)} copy-done((bf16[1,128,2048]{2,1,0:T(8,128)(2,1)S(1)}, bf16[1,128,2048]{2,1,0:T(8,128)(2,1)}, u32[]{:S(2)}) %copy-start.6) | copy-done | bytes 524312
  67.4 1.0 %copy-done.8 = bf16[1,128,2048]{2,1,0:T(8,128)(2,1)S(1)} copy-done((bf16[1,128,2048]{2,1,0:T(8,128)(2,1)S(1)}, bf16[1,128,2048]{2,1,0:T(8,128)(2,1)}, u32[]{:S(2)}) %copy-start.8) | copy-done | bytes 524312
  68.4 1.0 %copy-done.10 = bf16[1,128,2048]{2,1,0:T(8,128)(2,1)S(1)} copy-done((bf16[1,128,2048]{2,1,0:T(8,128)(2,1)S(1)}, bf16[1,128,2048]{2,1,0:T(8,128)(2,1)}, u32[]{:S(2)}) %copy-start.10) | copy-done | bytes 524312
  69.4 1.2 %copy-done.12 = f32[1,16,128,128]{3,2,1,0:T(8,128)S(1)} copy-done((f32[1,16,128,128]{3,2,1,0:T(8,128)S(1)}, f32[1,16,128,128]{3,2,1,0:T(8,128)}, u32[]{:S(2)}) %copy-start.12) | copy-done | bytes 1048600
  70.7 1.2 %copy-done.14 = f32[1,16,128,128]{3,2,1,0:T(8,128)S(1)} copy-done((f32[1,16,128,128]{3,2,1,0:T(8,128)S(1)}, f32[1,16,128,128]{3,2,1,0:T(8,128)}, u32[]{:S(2)}) %copy-start.14) | copy-done | bytes 1048600
  71.9 11.7 %state_dependent.1 = (bf16[1,128,2048]{2,1,0:T(8,128)(2,1)}, bf16[1,128,2048]{2,1,0:T(8,128)(2,1)}, bf16[1,128,2048]{2,1,0:T(8,128)(2,1)}, bf16[1,128,16]{2,1,0:T(8,128)(2,1)S(1)}) custom-call(s32[1]{0:T(128)} %dynamic_slice.6.valid_ref, bf16[1,128,2048]{2,1,0:T(8,128)(2,1)S(1)} %copy-done.3, bf16[1,128,2048]{2,1,0:T(8,128)(2,1)S(1)} %copy-done.5, ...), custom_call_target="tpu_custom_call" | custom-call | flops 2684354560 | bytes 8388608 | tf_op jit(solution)/shard_map/state_dependent/pallas_call | solution.py:387
  83.6 0.7 copy.21
  84.2 0.0 collective-permute-done.3.refs_4_
  84.2 0.0 collective-permute-done.6.refs_7_
  84.2 0.0 collective-permute-done.5.refs_6_
  84.2 0.0 collective-permute-done.4.refs_5_
  84.2 3.1 %spread_pieces.1 = f32[8,4,8,16,128]{4,3,2,1,0:T(8,128)} custom-call(s32[8]{0:T(128)S(1)} %stack.35.place_ref, bf16[8,4,16,128]{3,2,1,0:T(8,128)(2,1)S(1)} %sum_by_prompt.1.refs_0_, bf16[8,4,16,128]{3,2,1,0:T(8,128)(2,1)S(1)} %collective-permute-done.refs_1_, bf16[8,4,16,128]{3,2,1,0:T(8,128)(2,1)S(1)} %collective-permute-done.1.refs_2_, ...), custom_call_target="tpu_custom_call" | custom-call | tf_op jit(solution)/shard_map/spread_pieces/pallas_call | solution.py:443
  (12 shorter events, 0.0 us)
Async XLA Ops:
  0.6 27.7 %copy-start = (f32[8,4,128,128]{3,2,1,0:T(8,128)S(1)}, f32[8,4,128,128]{3,2,1,0:T(8,128)}, u32[]{:S(2)}) copy-start(f32[8,4,128,128]{3,2,1,0:T(8,128)} %param.15) | copy-start | bytes 6291460
  2.9 1.0 %copy-start.2 = (bf16[1,128,2048]{2,1,0:T(8,128)(2,1)S(1)}, bf16[1,128,2048]{2,1,0:T(8,128)(2,1)}, u32[]{:S(2)}) copy-start(bf16[1,128,2048]{2,1,0:T(8,128)(2,1)} %query_ref.3) | copy-start | bytes 1572868
  3.9 1.0 %copy-start.4 = (bf16[1,128,2048]{2,1,0:T(8,128)(2,1)S(1)}, bf16[1,128,2048]{2,1,0:T(8,128)(2,1)}, u32[]{:S(2)}) copy-start(bf16[1,128,2048]{2,1,0:T(8,128)(2,1)} %key_ref.3) | copy-start | bytes 1572868
  5.0 1.0 %copy-start.7 = (bf16[1,128,2048]{2,1,0:T(8,128)(2,1)S(1)}, bf16[1,128,2048]{2,1,0:T(8,128)(2,1)}, u32[]{:S(2)}) copy-start(bf16[1,128,2048]{2,1,0:T(8,128)(2,1)} %decay_ref.3) | copy-start | bytes 1572868
  6.0 1.0 %copy-start.9 = (bf16[1,128,2048]{2,1,0:T(8,128)(2,1)S(1)}, bf16[1,128,2048]{2,1,0:T(8,128)(2,1)}, u32[]{:S(2)}) copy-start(bf16[1,128,2048]{2,1,0:T(8,128)(2,1)} %grad_ref.3) | copy-start | bytes 1572868
  7.1 21.1 %copy-start.1 = (s32[32]{0:T(128)S(1)}, s32[32]{0:T(128)}, u32[]{:S(2)}) copy-start(s32[32]{0:T(128)} %prompt_ref.1) | copy-start | bytes 388
  18.9 1.0 %copy-start.11 = (f32[1,16,128,128]{3,2,1,0:T(8,128)}, f32[1,16,128,128]{3,2,1,0:T(8,128)S(1)}, u32[]{:S(2)}) copy-start(f32[1,16,128,128]{3,2,1,0:T(8,128)S(1)} %get-tuple-element.14.wide_ref) | copy-start | bytes 3145732
  19.9 1.0 %copy-start.13 = (f32[1,16,128,128]{3,2,1,0:T(8,128)}, f32[1,16,128,128]{3,2,1,0:T(8,128)S(1)}, u32[]{:S(2)}) copy-start(f32[1,16,128,128]{3,2,1,0:T(8,128)S(1)} %get-tuple-element.15.inverse_ref) | copy-start | bytes 3145732
  20.9 23.6 %all-to-all-start.1 = ((bf16[32,1,4,16,128]{4,3,2,1,0:T(8,128)(2,1)}), bf16[32,1,4,16,128]{4,3,2,1,0:T(8,128)(2,1)S(1)}, u32[]{:S(2)}, u32[]{:S(2)}) async-start(bf16[32,1,4,16,128]{4,3,2,1,0:T(8,128)(2,1)} %bitcast.10), calls=%async_computation.1 | async-start | bytes 1048576 | tf_op jit(solution)/shard_map/all_to_all | solution.py:385
  44.4 19.8 %all-to-all-start = ((f32[4,4,128,128]{3,2,1,0:T(8,128)}), f32[4,4,128,128]{3,2,1,0:T(8,128)}, u32[]{:S(2)}, u32[]{:S(2)}) async-start(f32[4,4,128,128]{3,2,1,0:T(8,128)} %broadcast_select_fusion), calls=%async_computation | async-start | bytes 2097152 | tf_op jit(solution)/shard_map/all_to_all | solution.py:334
  50.2 8.3 %collective-permute-start.2 = (bf16[8,4,16,128]{3,2,1,0:T(8,128)(2,1)S(1)}, bf16[8,4,16,128]{3,2,1,0:T(8,128)(2,1)S(1)}, u32[]{:S(2)}, u32[]{:S(2)}) collective-permute-start(bf16[8,4,16,128]{3,2,1,0:T(8,128)(2,1)S(1)} %sum_by_prompt.1.refs_0_), channel_id=1, source_target_pairs={{0,24},{4,28},{8,16},{12,20},{16,8},{20,12},{24,0},{28,4},{1,25},{... | collective-permute-start | bytes 393224 | tf_op jit(solution)/shard_map/ppermute | solution.py:302
  51.7 12.0 %collective-permute-start.1 = (bf16[8,4,16,128]{3,2,1,0:T(8,128)(2,1)S(1)}, bf16[8,4,16,128]{3,2,1,0:T(8,128)(2,1)S(1)}, u32[]{:S(2)}, u32[]{:S(2)}) collective-permute-start(bf16[8,4,16,128]{3,2,1,0:T(8,128)(2,1)S(1)} %sum_by_prompt.1.refs_0_), channel_id=1, source_target_pairs={{0,16},{4,20},{8,24},{12,28},{16,0},{20,4},{24,8},{28,12},{1,17},{... | collective-permute-start | bytes 393224 | tf_op jit(solution)/shard_map/ppermute | solution.py:302
  52.7 11.0 %collective-permute-start = (bf16[8,4,16,128]{3,2,1,0:T(8,128)(2,1)S(1)}, bf16[8,4,16,128]{3,2,1,0:T(8,128)(2,1)S(1)}, u32[]{:S(2)}, u32[]{:S(2)}) collective-permute-start(bf16[8,4,16,128]{3,2,1,0:T(8,128)(2,1)S(1)} %sum_by_prompt.1.refs_0_), channel_id=1, source_target_pairs={{0,8},{4,12},{8,0},{12,4},{16,24},{20,28},{24,16},{28,20},{1,9},{5... | collective-permute-start | bytes 393224 | tf_op jit(solution)/shard_map/ppermute | solution.py:302
  54.7 29.5 %collective-permute-start.3 = (bf16[8,4,16,128]{3,2,1,0:T(8,128)(2,1)S(1)}, bf16[8,4,16,128]{3,2,1,0:T(8,128)(2,1)S(1)}, u32[]{:S(2)}, u32[]{:S(2)}) collective-permute-start(bf16[8,4,16,128]{3,2,1,0:T(8,128)(2,1)S(1)} %sum_by_prompt.1.refs_0_), channel_id=1, source_target_pairs={{0,4},{4,0},{8,12},{12,8},{16,20},{20,16},{24,28},{28,24},{1,5},{5... | collective-permute-start | bytes 393224 | tf_op jit(solution)/shard_map/ppermute | solution.py:307
  58.5 25.7 %collective-permute-start.6 = (bf16[8,4,16,128]{3,2,1,0:T(8,128)(2,1)S(1)}, bf16[8,4,16,128]{3,2,1,0:T(8,128)(2,1)S(1)}, u32[]{:S(2)}, u32[]{:S(2)}) collective-permute-start(bf16[8,4,16,128]{3,2,1,0:T(8,128)(2,1)S(1)} %collective-permute-done.2.refs_3_), channel_id=1, source_target_pairs={{0,4},{4,0},{8,12},{12,8},{16,20},{20,16},{24,28},{28,24},{1,5},{5... | collective-permute-start | bytes 393224 | tf_op jit(solution)/shard_map/ppermute | solution.py:307
  63.7 20.5 %collective-permute-start.5 = (bf16[8,4,16,128]{3,2,1,0:T(8,128)(2,1)S(1)}, bf16[8,4,16,128]{3,2,1,0:T(8,128)(2,1)S(1)}, u32[]{:S(2)}, u32[]{:S(2)}) collective-permute-start(bf16[8,4,16,128]{3,2,1,0:T(8,128)(2,1)S(1)} %collective-permute-done.1.refs_2_), channel_id=1, source_target_pairs={{0,4},{4,0},{8,12},{12,8},{16,20},{20,16},{24,28},{28,24},{1,5},{5... | collective-permute-start | bytes 393224 | tf_op jit(solution)/shard_map/ppermute | solution.py:307
  63.7 20.5 %collective-permute-start.4 = (bf16[8,4,16,128]{3,2,1,0:T(8,128)(2,1)S(1)}, bf16[8,4,16,128]{3,2,1,0:T(8,128)(2,1)S(1)}, u32[]{:S(2)}, u32[]{:S(2)}) collective-permute-start(bf16[8,4,16,128]{3,2,1,0:T(8,128)(2,1)S(1)} %collective-permute-done.refs_1_), channel_id=1, source_target_pairs={{0,4},{4,0},{8,12},{12,8},{16,20},{20,16},{24,28},{28,24},{1,5},{5... | collective-permute-start | bytes 393224 | tf_op jit(solution)/shard_map/ppermute | solution.py:307
  64.2 1.0 %copy-start.3 = (bf16[1,128,2048]{2,1,0:T(8,128)(2,1)S(1)}, bf16[1,128,2048]{2,1,0:T(8,128)(2,1)}, u32[]{:S(2)}) copy-start(bf16[1,128,2048]{2,1,0:T(8,128)(2,1)} %query_ref.3) | copy-start | bytes 1572868
  65.3 1.0 %copy-start.5 = (bf16[1,128,2048]{2,1,0:T(8,128)(2,1)S(1)}, bf16[1,128,2048]{2,1,0:T(8,128)(2,1)}, u32[]{:S(2)}) copy-start(bf16[1,128,2048]{2,1,0:T(8,128)(2,1)} %key_ref.3) | copy-start | bytes 1572868
  66.3 1.0 %copy-start.6 = (bf16[1,128,2048]{2,1,0:T(8,128)(2,1)S(1)}, bf16[1,128,2048]{2,1,0:T(8,128)(2,1)}, u32[]{:S(2)}) copy-start(bf16[1,128,2048]{2,1,0:T(8,128)(2,1)} %value_ref.1) | copy-start | bytes 1572868
  67.4 1.0 %copy-start.8 = (bf16[1,128,2048]{2,1,0:T(8,128)(2,1)S(1)}, bf16[1,128,2048]{2,1,0:T(8,128)(2,1)}, u32[]{:S(2)}) copy-start(bf16[1,128,2048]{2,1,0:T(8,128)(2,1)} %decay_ref.3) | copy-start | bytes 1572868
  68.4 1.0 %copy-start.10 = (bf16[1,128,2048]{2,1,0:T(8,128)(2,1)S(1)}, bf16[1,128,2048]{2,1,0:T(8,128)(2,1)}, u32[]{:S(2)}) copy-start(bf16[1,128,2048]{2,1,0:T(8,128)(2,1)} %grad_ref.3) | copy-start | bytes 1572868
  69.4 1.2 %copy-start.12 = (f32[1,16,128,128]{3,2,1,0:T(8,128)S(1)}, f32[1,16,128,128]{3,2,1,0:T(8,128)}, u32[]{:S(2)}) copy-start(f32[1,16,128,128]{3,2,1,0:T(8,128)} %copy-done.11) | copy-start | bytes 3145732
  70.7 1.2 %copy-start.14 = (f32[1,16,128,128]{3,2,1,0:T(8,128)S(1)}, f32[1,16,128,128]{3,2,1,0:T(8,128)}, u32[]{:S(2)}) copy-start(f32[1,16,128,128]{3,2,1,0:T(8,128)} %copy-done.13) | copy-start | bytes 3145732

commit v2 on v1

v2 whole, which is shorter than its diff:
```python
import functools

import jax
import jax.numpy as jnp
from jax import lax
from jax.experimental import pallas as pl
from jax.experimental.pallas import tpu as pltpu
from jax.sharding import PartitionSpec as P

HIGH = lax.Precision.HIGH
NN = ((1,), (0,))
NT = ((1,), (1,))
TN = ((0,), (0,))
F32 = jnp.float32
BF16 = jnp.bfloat16


def dot(a, b, dims=NN, precision=None):
    return lax.dot_general(
        a, b, (dims, ((), ())), preferred_element_type=F32, precision=precision
    )


def split(x):
    high = x.astype(BF16)
    return high, (x - high.astype(F32)).astype(BF16)


def encode(x):
    return (x * x * x * jnp.abs(x)).astype(BF16)


def decode(y):
    wide = y.astype(F32)
    root = lax.rsqrt(lax.rsqrt(jnp.abs(wide)))
    return jnp.where(wide < 0, -root, root)


def iota2(shape, axis):
    return lax.broadcasted_iota(jnp.int32, shape, axis)


def dot3(a, b):
    return dot(a[0], b[0]) + dot(a[1], b[0]) + dot(a[0], b[1])


def stack(a, b, axis):
    return tuple(jnp.concatenate([x, y], axis=axis) for x, y in zip(a, b))


def unit_upper_inverse(matrices, width):
    size = matrices[0].shape[0]
    blocks = size // width
    row, col = iota2((size, size), 0), iota2((size, size), 1)
    on_block = row // width == col // width
    lane = iota2((8, size), 1)
    identity = (iota2((width, size), 0) == iota2((width, size), 1) % width).astype(F32)
    inverses = []
    for a in matrices:
        compact = jnp.sum(jnp.where(on_block, a, 0.0).reshape(blocks, width, size), axis=0)
        slabs = [compact[i : i + 8] for i in range(0, width, 8)]
        result = [identity[i : i + 8] for i in range(0, width, 8)]
        for m in reversed(range(1, width)):
            source = result[m // 8][m % 8 : m % 8 + 1]
            for i in range((m - 1) // 8 + 1):
                column = jnp.take_along_axis(slabs[i], lane // width * width + m, axis=1)
                result[i] = result[i] - column * source
        inverses.append(jnp.where(on_block, jnp.concatenate(result * blocks, axis=0), 0.0))
    while width * 2 < size:
        upper = (row // (2 * width) == col // (2 * width)) & (row // width < col // width)
        parts = [split(d) for d in inverses]
        inner = [dot3(split(jnp.where(upper, a, 0.0)), d) for a, d in zip(matrices, parts)]
        inverses = [d - dot3(p, split(x)) for d, p, x in zip(inverses, parts, inner)]
        width *= 2
    results = []
    first = [split(d[:width, :width]) for d in inverses]
    second = [split(d[width:, width:]) for d in inverses]
    inner = [dot3(split(a[:width, width:]), d) for a, d in zip(matrices, second)]
    corner = [dot3(d, split(x)) for d, x in zip(first, inner)]
    for d, x in zip(inverses, corner):
        top = jnp.concatenate([d[:width, :width], -x], axis=1)
        results.append(jnp.concatenate([top, d[width:]], axis=0))
    return results


def decayed_rows(query_in, key_in, decay_in, valid, tri):
    tokens, head_dim = query_in.shape
    row = iota2((tokens, 1), 0)
    query = query_in.astype(F32)
    key = key_in.astype(F32)
    query_scale = lax.rsqrt(jnp.sum(query * query, axis=1, keepdims=True) + 1e-06)
    key_scale = lax.rsqrt(jnp.sum(key * key, axis=1, keepdims=True) + 1e-06)
    unit_query = query * query_scale
    unit_key = key * key_scale
    decay = jnp.where(row < valid, decay_in, jnp.zeros_like(decay_in))
    cumulative = dot(tri, decay)
    middle = cumulative[tokens // 2 - 1 : tokens // 2]
    cumulative = cumulative - middle
    grow = jnp.exp(cumulative)
    shrink = jnp.exp(-cumulative)
    return dict(
        unit_query=unit_query,
        unit_key=unit_key,
        query_scale=query_scale,
        key_scale=key_scale,
        grow=grow,
        shrink=shrink,
        start=jnp.exp(middle),
        key_forward=unit_key * grow,
        key_earlier=unit_key * shrink,
        query_forward=unit_query * (grow * head_dim**-0.5),
    )


def head_column(values, head):
    lane = iota2(values.shape, 1)
    return jnp.sum(jnp.where(lane == head, values, 0.0), axis=1, keepdims=True)


def own_branch(count):
    place = lax.axis_index("grp") * lax.axis_size("head") + lax.axis_index("head")
    return place * count


def first_kernel(
    per_step,
    width,
    valid_ref,
    query_ref,
    key_ref,
    decay_ref,
    grad_ref,
    beta_ref,
    value_grad_ref,
    value_low_ref,
    inverse_ref,
    coded_ref,
):
    tokens = query_ref.shape[1]
    head_dim = query_ref.shape[2] // per_step
    pieces = coded_ref.shape[0]
    valid = valid_ref[own_branch(pl.num_programs(0)) + pl.program_id(0)]
    row, col = iota2((tokens, tokens), 0), iota2((tokens, tokens), 1)
    tri = (row >= col).astype(BF16)
    keep = iota2((tokens, 1), 0) < valid
    lane_keep = iota2((1, tokens), 1) < valid
    flat_betas = jax.nn.sigmoid(beta_ref[0].astype(F32)) * lane_keep.astype(F32)
    betas = flat_betas.T
    heads = range(per_step)
    lanes = [slice(j * head_dim, (j + 1) * head_dim) for j in heads]
    number = [pl.program_id(1) * per_step + j for j in heads]
    rows = [
        decayed_rows(
            query_ref[0, :, lanes[j]], key_ref[0, :, lanes[j]], decay_ref[0, :, lanes[j]], valid, tri
        )
        for j in heads
    ]
    beta = [head_column(betas, n) for n in number]
    flat_beta = [
        jnp.sum(
            jnp.where(iota2(flat_betas.shape, 0) == n, flat_betas, 0.0), axis=0, keepdims=True
        )
        for n in number
    ]
    out_grad = []
    for j in heads:
        grad = grad_ref[0, :, lanes[j]]
        out_grad.append(jnp.where(keep, grad, jnp.zeros_like(grad)))
    across = [
        split(jnp.concatenate([r["key_forward"], r["query_forward"]], axis=0).T) for r in rows
    ]
    scores = [dot3(split(r["key_earlier"]), x) for r, x in zip(rows, across)]
    coupling = [
        jnp.where(row < col, s[:, :tokens] * b, 0.0) for s, b in zip(scores, flat_beta)
    ]
    attend = [split(jnp.where(row <= col, s[:, tokens:], 0.0)) for s in scores]
    inverse = [split(x) for x in unit_upper_inverse(coupling, width)]
    update_grad = [
        split(dot(p[0], g) + dot(p[1], g)) for p, g in zip(attend, out_grad)
    ]
    value_grad = [split(b * dot3(d, u)) for b, d, u in zip(beta, inverse, update_grad)]
    for j in heads:
        high = jnp.concatenate([-value_grad[j][0], out_grad[j]], axis=0)
        start = jnp.broadcast_to(rows[j]["start"], (8, head_dim)).T[:, :1]
        state_grad = start * (
            dot(across[j][0], high)
            + dot(across[j][1], high)
            - dot(across[j][0][:, :tokens], value_grad[j][1])
        )
        coded_ref[:, j] = encode(state_grad).reshape(pieces, head_dim // pieces, head_dim)
        value_grad_ref[0, :, lanes[j]] = value_grad[j][0]
        value_low_ref[0, :, lanes[j]] = value_grad[j][1]
        inverse_ref[0, j] = jnp.concatenate(inverse[j], axis=1)


def choose_kernel(prompt_ref, state_ref, *rest):
    chosen, (held_ref, arrival, departure) = rest[:-3], rest[-3:]
    members, count = len(chosen), chosen[0].shape[0]
    group_first = lax.axis_index("grp") * members * count
    reads, writes = [], []
    for step in range(members):
        receiver, _ = meeting(step)
        for b in range(count):
            prompt = prompt_ref[group_first + receiver * count + b]
            slot = step * count + b
            reads.append(
                pltpu.make_async_copy(state_ref.at[prompt], held_ref.at[slot], arrival.at[slot])
            )
            writes.append(
                pltpu.make_async_copy(held_ref.at[slot], chosen[step].at[b], departure.at[slot])
            )
    for read in reads:
        read.start()
    for read, write in zip(reads, writes):
        read.wait()
        write.start()
    for write in writes:
        write.wait()


def second_kernel(
    per_step,
    members,
    valid_ref,
    query_ref,
    key_ref,
    value_ref,
    decay_ref,
    grad_ref,
    beta_ref,
    value_grad_ref,
    value_low_ref,
    inverse_ref,
    *rest,
):
    arrived, rest = rest[:members], rest[members:]
    query_grad_ref, key_grad_ref, decay_grad_ref, beta_grad_ref, strength_ref = rest[:5]
    state_ref, arrival = rest[5:]
    tokens = query_ref.shape[1]
    head_dim = query_ref.shape[2] // per_step
    step = pl.program_id(1)

    @pl.when(step == 0)
    def _():
        copies = []
        for i in range(members):
            _, sender = meeting(i)
            copies.append(
                pltpu.make_async_copy(
                    arrived[i].at[pl.program_id(0)], state_ref.at[sender], arrival.at[i]
                )
            )
        for copy in copies:
            copy.start()
        for copy in copies:
            copy.wait()
        strength_ref[...] = jnp.zeros_like(strength_ref)

    valid = valid_ref[own_branch(pl.num_programs(0)) + pl.program_id(0)]
    row, col = iota2((tokens, tokens), 0), iota2((tokens, tokens), 1)
    tri = (row >= col).astype(BF16)
    later = (row <= col).astype(BF16)
    later = jnp.concatenate([later, later], axis=1)
    keep = iota2((tokens, 1), 0) < valid
    logits = beta_ref[0].astype(F32).T
    betas = jax.nn.sigmoid(logits) * keep.astype(F32)
    heads = range(per_step)
    lanes = [slice(j * head_dim, (j + 1) * head_dim) for j in heads]
    number = [step * per_step + j for j in heads]
    here = state_ref.shape[1]
    rows = [
        decayed_rows(
            query_ref[0, :, lanes[j]],
            key_ref[0, :, lanes[j]],
            decay_ref[0, :, lanes[j]],
            valid,
            tri,
        )
        for j in heads
    ]
    beta = [head_column(betas, n) for n in number]
    state = [state_ref[n // here, n % here] for n in number]
    target = [
        value_ref[0, :, lanes[j]].astype(F32)
        - dot3(split(rows[j]["key_forward"] * rows[j]["start"]), split(state[j]))
        for j in heads
    ]
    update = [
        split(
            dot3(
                split((b * x).T),
                (inverse_ref[0, j, :, :tokens], inverse_ref[0, j, :, tokens:]),
            )
        )
        for j, b, x in zip(heads, beta, target)
    ]
    against = [stack(u, split(x.T), 1) for u, x in zip(update, state)]
    products = []
    for j in heads:
        grad = grad_ref[0, :, lanes[j]]
        grad = jnp.where(keep, grad, jnp.zeros_like(grad))
        high = jnp.concatenate([grad, -value_grad_ref[0, :, lanes[j]]], axis=0)
        total = dot(high, against[j][0]) + dot(high, against[j][1])
        low = dot(value_low_ref[0, :, lanes[j]], against[j][0])
        products.append((total[:tokens], total[tokens:] - low))

    strengths = strength_ref[...]
    attend_grad = [jnp.where(row >= col, p[0][:, :tokens], 0.0) for p in products]
    coupling_grad = [jnp.where(row > col, p[1][:, :tokens], 0.0) for p in products]
    through_rows = [
        dot3(split(jnp.concatenate([p, c], axis=0)), split(r["key_earlier"]))
        for p, c, r in zip(attend_grad, coupling_grad, rows)
    ]
    earlier = [
        dot3(
            split(jnp.concatenate([p.T, c.T], axis=1)),
            split(jnp.concatenate([r["query_forward"], r["key_forward"]], axis=0)),
        )
        for p, c, r in zip(attend_grad, coupling_grad, rows)
    ]
    for j in heads:
        r = rows[j]
        query_forward = products[j][0][:, tokens:] * r["start"] + through_rows[j][:tokens]
        key_forward = products[j][1][:, tokens:] * r["start"] + through_rows[j][tokens:]
        query_unit_grad = query_forward * (r["grow"] * head_dim**-0.5)
        key_later = key_forward * r["grow"]
        key_before = earlier[j] * r["shrink"]
        key_unit_grad = key_later + key_before
        decay_step = r["unit_query"] * query_unit_grad + r["unit_key"] * (key_later - key_before)
        decay_grad = dot(later, jnp.concatenate(split(decay_step), axis=0))
        decay_grad_ref[0, :, lanes[j]] = jnp.where(keep, decay_grad, 0.0).astype(BF16)
        along = jnp.sum(r["unit_query"] * query_unit_grad, axis=1, keepdims=True)
        query_grad_ref[0, :, lanes[j]] = (
            r["query_scale"] * (query_unit_grad - r["unit_query"] * along)
        ).astype(BF16)
        along = jnp.sum(r["unit_key"] * key_unit_grad, axis=1, keepdims=True)
        key_grad_ref[0, :, lanes[j]] = (
            r["key_scale"] * (key_unit_grad - r["unit_key"] * along)
        ).astype(BF16)
        strength = jnp.sum(
            jnp.where(row == col, -products[j][1][:, :tokens], 0.0), axis=1, keepdims=True
        )
        strengths = jnp.where(iota2(logits.shape, 1) == number[j], strength, strengths)
    strength_ref[...] = strengths

    @pl.when(step == pl.num_programs(1) - 1)
    def _():
        beta_grad_ref[0] = (strength_ref[...] * jnp.exp(-logits)).T.astype(BF16)


def sum_kernel(prompt_ref, coded_ref, out_ref, total_ref):
    total_ref[...] = jnp.zeros_like(total_ref)

    def add(branch, carry):
        total_ref[prompt_ref[branch]] += decode(coded_ref[branch])
        return carry

    lax.fori_loop(0, coded_ref.shape[0], add, 0, unroll=4)
    out_ref[...] = encode(total_ref[...])


def spread_kernel(*refs):
    out_ref = refs[-1]
    pieces = refs[:-1]
    chips = len(pieces) // 2
    for i, piece in enumerate(pieces):
        place = source(i % chips, chips) ^ (i // chips)
        out_ref[:, :, pl.ds(place, 1)] = decode(piece[...])[:, :, None]


def source(step, chips):
    me = lax.axis_index("grp")
    if chips & (chips - 1) == 0:
        return me ^ (2 * step)
    return (me // 2 - step + chips) % chips * 2 + me % 2


def gather_pieces(piece, beside):
    size = lax.axis_size("grp")
    chips = size // 2
    power = chips & (chips - 1) == 0
    pieces = [piece]
    for step in range(1, chips):
        other = [((c ^ step) if power else (c + step) % chips) for c in range(chips)]
        moves = [(2 * c + core, 2 * other[c] + core) for c in range(chips) for core in range(2)]
        pieces.append(lax.ppermute(piece, "grp", moves))
    pieces, _ = lax.optimization_barrier((pieces, beside))
    swap = [(i, i ^ 1) for i in range(size)]
    return pieces + [lax.ppermute(x, "grp", swap) for x in pieces]


def moves_at(step, members):
    if members & (members - 1) == 0:
        return [(m, m ^ step) for m in range(members)]
    return [(m, (m + step) % members) for m in range(members)]


def meeting(step):
    members = lax.axis_size("head")
    me = lax.axis_index("head")
    if members & (members - 1) == 0:
        return me ^ step, me ^ step
    return (me + step) % members, (me - step + members) % members


def per_device(
    query_rows,
    key_rows,
    value_rows,
    log_decay,
    beta_logit,
    out_grad,
    fork_state,
    branch_prompt,
    valid_len,
):
    count, tokens, width = query_rows.shape
    prompts, heads_here, head_dim, _ = fork_state.shape
    members = lax.axis_size("head")
    groups = lax.axis_size("grp")
    heads = members * heads_here
    piece_rows = head_dim // groups
    per_step = next(n for n in (8, 4, 2, 1) if heads % n == 0)
    steps = heads // per_step
    params = pltpu.CompilerParams(vmem_limit_bytes=60 * 2**20)
    rows_type = jax.ShapeDtypeStruct(query_rows.shape, BF16)
    units = count * heads * tokens * tokens * head_dim
    betas = jnp.swapaxes(beta_logit, 1, 2)
    anywhere = pl.BlockSpec(memory_space=pl.ANY)

    row_block = pl.BlockSpec((1, tokens, per_step * head_dim), lambda b, i, *_: (b, 0, i))
    beta_block = pl.BlockSpec((1, heads, tokens), lambda b, i, *_: (b, 0, 0))
    inverse_block = pl.BlockSpec(
        (1, per_step, tokens, 2 * tokens), lambda b, i, *_: (b, i, 0, 0)
    )
    value_grad, value_low, inverse, coded = pl.pallas_call(
        functools.partial(first_kernel, per_step, 16),
        grid_spec=pltpu.PrefetchScalarGridSpec(
            num_scalar_prefetch=1,
            grid=(count, steps),
            in_specs=[row_block] * 4 + [beta_block],
            out_specs=[
                row_block,
                row_block,
                inverse_block,
                pl.BlockSpec(
                    (groups, per_step, piece_rows, head_dim),
                    lambda b, i, *_: (0, b * steps + i, 0, 0),
                ),
            ],
        ),
        out_shape=[
            rows_type,
            rows_type,
            jax.ShapeDtypeStruct((count, heads, tokens, 2 * tokens), BF16),
            jax.ShapeDtypeStruct((groups, count * heads, piece_rows, head_dim), BF16),
        ],
        compiler_params=params,
        cost_estimate=pl.CostEstimate(flops=100 * units, bytes_accessed=2**23, transcendentals=0),
        name="state_independent",
    )(valid_len, query_rows, key_rows, log_decay, out_grad, betas)

    states_after, coded = lax.optimization_barrier((fork_state, coded))
    states = pl.pallas_call(
        choose_kernel,
        grid_spec=pltpu.PrefetchScalarGridSpec(
            num_scalar_prefetch=1,
            grid=(1,),
            in_specs=[anywhere],
            out_specs=[anywhere] * members,
            scratch_shapes=[
                pltpu.VMEM((members * count, heads_here, head_dim, head_dim), F32),
                pltpu.SemaphoreType.DMA((members * count,)),
                pltpu.SemaphoreType.DMA((members * count,)),
            ],
        ),
        out_shape=[jax.ShapeDtypeStruct((count, heads_here, head_dim, head_dim), F32)] * members,
        compiler_params=params,
        name="choose_states",
    )(branch_prompt, states_after)
    states = [states[0]] + [
        lax.ppermute(states[step], "head", moves_at(step, members)) for step in range(1, members)
    ]

    coded = (
        coded.reshape(groups, count, members, heads_here, piece_rows, head_dim)
        .transpose(0, 2, 1, 3, 4, 5)
        .reshape(groups * members, count, heads_here, piece_rows, head_dim)
    )
    arrived = lax.all_to_all(coded, ("grp", "head"), 0, 0, tiled=True)

    query_grad, key_grad, decay_grad, beta_grad = pl.pallas_call(
        functools.partial(second_kernel, per_step, members),
        grid_spec=pltpu.PrefetchScalarGridSpec(
            num_scalar_prefetch=1,
            grid=(count, steps),
            in_specs=[row_block] * 5
            + [beta_block, row_block, row_block, inverse_block]
            + [anywhere] * members,
            out_specs=[row_block] * 3 + [beta_block],
            scratch_shapes=[
                pltpu.VMEM((tokens, heads), F32),
                pltpu.VMEM((members, heads_here, head_dim, head_dim), F32),
                pltpu.SemaphoreType.DMA((members,)),
            ],
        ),
        out_shape=[rows_type] * 3 + [jax.ShapeDtypeStruct((count, heads, tokens), BF16)],
        compiler_params=params,
        cost_estimate=pl.CostEstimate(flops=120 * units, bytes_accessed=2**23, transcendentals=0),
        name="state_dependent",
    )(
        valid_len,
        query_rows,
        key_rows,
        value_rows,
        log_decay,
        out_grad,
        betas,
        value_grad,
        value_low,
        inverse,
        *states,
    )

    piece_shape = (prompts, heads_here, piece_rows, head_dim)
    branches = groups * members * count
    whole = pl.BlockSpec(memory_space=pltpu.VMEM)
    scalars = pl.BlockSpec(memory_space=pltpu.SMEM)
    piece = pl.pallas_call(
        sum_kernel,
        in_specs=[scalars, whole],
        out_specs=whole,
        out_shape=jax.ShapeDtypeStruct(piece_shape, BF16),
        scratch_shapes=[pltpu.VMEM(piece_shape, F32)],
        compiler_params=params,
        name="sum_by_prompt",
    )(branch_prompt, arrived.reshape(branches, heads_here, piece_rows, head_dim))
    pieces = gather_pieces(piece, query_grad)
    grad_fork = pl.pallas_call(
        spread_kernel,
        in_specs=[whole] * len(pieces),
        out_specs=whole,
        out_shape=jax.ShapeDtypeStruct(
            (prompts, heads_here, groups, piece_rows, head_dim), F32
        ),
        compiler_params=params,
        name="spread_pieces",
    )(*pieces)
    return (
        query_grad,
        key_grad,
        value_grad,
        decay_grad,
        jnp.swapaxes(beta_grad, 1, 2),
        grad_fork.reshape(fork_state.shape),
    )


def solution(mesh):
    rows = P(("grp", "head"), None, None)
    state = P(None, "head", None, None)
    return jax.shard_map(
        per_device,
        mesh=mesh,
        in_specs=(rows, rows, rows, rows, rows, rows, state, P(), P()),
        out_specs=(rows, rows, rows, rows, rows, state),
        check_vma=False,
    )
```

time: 88.3 us -> 60.2 us (0.68)
  local copies, waits for them, and re-layouts: 18.4 us -> 2.71 us
  waiting for transfers between devices: 21.1 us -> 11.1 us
  other arithmetic: 2.47 us -> 0 us
    unnamed x32 -> x24, local copies, waits for them, and re-layouts: 15.4 us -> 2.71 us
    ppermute x7 -> x10, waiting for transfers between devices: 8.97 us -> 1.03 us  [the longest x4 1.02 us: gather_pieces(): return pieces + [lax.ppermute(x, 'grp', swap) for x in pieces]]
    all_to_all x1 -> x0, starting transfers between devices: 4.25 us -> none  [per_device(): lax.all_to_all(chosen.reshape(members, count * heads_here, head_dim, head...]
    ppermute x7 -> x10, starting transfers between devices: 4.97 us -> 9.02 us  [the longest x3 4.39 us: gather_pieces(): pieces.append(lax.ppermute(piece, 'grp', moves))]
    select_n x1 -> x0, other arithmetic: 2.38 us -> none  [per_device(): chosen = jnp.take(fork_state, group_prompt, axis=0)]
    all_to_all x1, waiting for transfers between devices: 12.1 us -> 10.1 us  [per_device(): arrived = lax.all_to_all(coded, ('grp', 'head'), 0, 0, tiled=True)]
    gather x1 -> x0, local copies, waits for them, and re-layouts: 1.6 us -> none  [per_device(): chosen = jnp.take(fork_state, group_prompt, axis=0)]
    dynamic_slice x1 -> x0, local copies, waits for them, and re-layouts: 1.3 us -> none  [per_device(): valid = lax.dynamic_slice_in_dim(valid_len, first_branch, count)]
  transfers between devices with their start and end apart: 9 -> 11, of which waited for: 3 -> 5; matrix products, arithmetic and copies ran while one was open for 6% -> 0% of each run, Pallas kernels for 15% -> 27%
where the time goes in v2:
time: 60.2 us; the launch traced here: 59.8 us
  Pallas kernels  28.9 us (48%)
  starting transfers between devices  16.3 us (27%)
  waiting for transfers between devices  11.1 us (18%)
  local copies, waits for them, and re-layouts  2.71 us (5%)
  between operations  0.77 us (1%)
    pallas_call x1, Pallas kernels, per_device(): pl.pallas_call(functools.partial(second_kernel, per_step, members), grid_...  11.1 us
    all_to_all x1, waiting for transfers between devices, per_device(): arrived = lax.all_to_all(coded, ('grp', 'head'), 0, 0, tiled=True)  10.1 us
    pallas_call x1, Pallas kernels, per_device(): pl.pallas_call(functools.partial(first_kernel, per_step, 16), grid_spec=p...  9.87 us
    all_to_all x1, starting transfers between devices, per_device(): arrived = lax.all_to_all(coded, ('grp', 'head'), 0, 0, tiled=True)  7.3 us
    ppermute x3, starting transfers between devices, gather_pieces(): pieces.append(lax.ppermute(piece, 'grp', moves))  4.39 us
    ppermute x3, starting transfers between devices, per_device(): lax.ppermute(states[step], 'head', moves_at(step, members))  3.55 us
    pallas_call x1, Pallas kernels, per_device(): pl.pallas_call(spread_kernel, in_specs=[whole] * len(pieces), out_specs=w...  3.15 us
    unnamed x24, local copies, waits for them, and re-layouts  2.71 us
  transfers between devices with their start and end apart: 11, of which 5 were waited for; matrix products, arithmetic and copies ran while one was open for 0% of the time, Pallas kernels for 27%

profile of v2, /device:TPU:0, one launch (start us, length us, event | category | flops | bytes accessed | tf_op | source)
XLA Modules:
  0.0 59.8 jit_solution(1873191539172285048)
XLA Ops:
  0.6 9.9 %state_independent.1 = (bf16[1,128,2048]{2,1,0:T(8,128)(2,1)}, bf16[1,128,2048]{2,1,0:T(8,128)(2,1)}, bf16[1,16,128,256]{3,2,1,0:T(8,128)(2,1)}, bf16[8,16,16,128]{3,2,1,0:T(8,128)(2,1)}) custom-call(s32[32]{0:T(128)} %valid_ref.3, bf16[1,128,2048]{2,1,0:T(8,128)(2,1)} %query_ref.3, bf16[1,128,2048]{2,1,0:T(8,128)(2,1)} %key_ref.3, ...), custom_call_target="tpu_custom_call" | custom-call | flops 3355443200 | bytes 8388608 | tf_op jit(solution)/shard_map/state_independent/pallas_call | solution.py:436
  10.5 7.3 %all-to-all-start = ((bf16[32,1,4,16,128]{4,3,2,1,0:T(8,128)(2,1)}), bf16[32,1,4,16,128]{4,3,2,1,0:T(8,128)(2,1)S(1)}, u32[]{:S(2)}, u32[]{:S(2)}) async-start(bf16[32,1,4,16,128]{4,3,2,1,0:T(8,128)(2,1)} %bitcast.9), calls=%async_computation | async-start | bytes 1048576 | tf_op jit(solution)/shard_map/all_to_all | solution.py:490
  17.8 2.7 %choose_states.1 = (f32[1,4,128,128]{3,2,1,0:T(8,128)}, f32[1,4,128,128]{3,2,1,0:T(8,128)}, f32[1,4,128,128]{3,2,1,0:T(8,128)}, f32[1,4,128,128]{3,2,1,0:T(8,128)}) custom-call(s32[32]{0:T(128)} %prompt_ref.3, f32[8,4,128,128]{3,2,1,0:T(8,128)} %state_ref), custom_call_target="tpu_custom_call" | custom-call | tf_op jit(solution)/shard_map/choose_states/pallas_call | solution.py:464
  20.5 1.8 %collective-permute-start = (f32[1,4,128,128]{3,2,1,0:T(8,128)}, f32[1,4,128,128]{3,2,1,0:T(8,128)S(1)}, u32[]{:S(2)}, u32[]{:S(2)}) collective-permute-start(f32[1,4,128,128]{3,2,1,0:T(8,128)} %get-tuple-element.30), channel_id=1, source_target_pairs={{0,1},{1,0},{2,3},{3,2},{4,5},{5,4},{6,7},{7,6},{8,9},{9,8},{10,11... | collective-permute-start | bytes 786440 | tf_op jit(solution)/shard_map/ppermute | solution.py:482
  22.3 1.5 %collective-permute-start.1 = (f32[1,4,128,128]{3,2,1,0:T(8,128)}, f32[1,4,128,128]{3,2,1,0:T(8,128)S(1)}, u32[]{:S(2)}, u32[]{:S(2)}) collective-permute-start(f32[1,4,128,128]{3,2,1,0:T(8,128)} %get-tuple-element.31), channel_id=1, source_target_pairs={{0,2},{1,3},{2,0},{3,1},{4,6},{5,7},{6,4},{7,5},{8,10},{9,11},{10,... | collective-permute-start | bytes 786440 | tf_op jit(solution)/shard_map/ppermute | solution.py:482
  23.8 0.3 collective-permute-start.2
  24.0 10.1 %all-to-all-done = bf16[32,1,4,16,128]{4,3,2,1,0:T(8,128)(2,1)S(1)} async-done(((bf16[32,1,4,16,128]{4,3,2,1,0:T(8,128)(2,1)}), bf16[32,1,4,16,128]{4,3,2,1,0:T(8,128)(2,1)S(1)}, u32[]{:S(2)}, u32[]{:S(2)}) %all-to-all-start) | async-done | bytes 524320 | tf_op jit(solution)/shard_map/all_to_all | solution.py:490
  34.1 0.0 copy-start
  34.1 0.8 %copy-done = bf16[32,1,4,16,128]{4,3,2,1,0:T(8,128)(2,1)} copy-done((bf16[32,1,4,16,128]{4,3,2,1,0:T(8,128)(2,1)}, bf16[32,1,4,16,128]{4,3,2,1,0:T(8,128)(2,1)S(1)}, u32[]{:S(2)}) %copy-start) | copy-done | bytes 524312
  34.9 2.1 %sum_by_prompt.1.refs_0_ = bf16[8,4,16,128]{3,2,1,0:T(8,128)(2,1)} custom-call(s32[32]{0:T(128)} %prompt_ref.3, bf16[32,4,16,128]{3,2,1,0:T(8,128)(2,1)} %bitcast.8), custom_call_target="tpu_custom_call" | custom-call | tf_op jit(solution)/shard_map/sum_by_prompt/pallas_call | solution.py:529
  37.0 1.4 %collective-permute-start.5 = (bf16[8,4,16,128]{3,2,1,0:T(8,128)(2,1)}, bf16[8,4,16,128]{3,2,1,0:T(8,128)(2,1)S(1)}, u32[]{:S(2)}, u32[]{:S(2)}) collective-permute-start(bf16[8,4,16,128]{3,2,1,0:T(8,128)(2,1)} %sum_by_prompt.1.refs_0_), channel_id=1, source_target_pairs={{0,24},{4,28},{8,16},{12,20},{16,8},{20,12},{24,0},{28,4},{1,25},{... | collective-permute-start | bytes 393224 | tf_op jit(solution)/shard_map/ppermute | solution.py:386
  38.5 1.1 %collective-permute-start.4 = (bf16[8,4,16,128]{3,2,1,0:T(8,128)(2,1)}, bf16[8,4,16,128]{3,2,1,0:T(8,128)(2,1)S(1)}, u32[]{:S(2)}, u32[]{:S(2)}) collective-permute-start(bf16[8,4,16,128]{3,2,1,0:T(8,128)(2,1)} %sum_by_prompt.1.refs_0_), channel_id=1, source_target_pairs={{0,16},{4,20},{8,24},{12,28},{16,0},{20,4},{24,8},{28,12},{1,17},{... | collective-permute-start | bytes 393224 | tf_op jit(solution)/shard_map/ppermute | solution.py:386
  39.5 0.0 collective-permute-done.rest_1_
  39.5 0.0 copy-start.9
  39.5 1.9 %collective-permute-start.3 = (bf16[8,4,16,128]{3,2,1,0:T(8,128)(2,1)}, bf16[8,4,16,128]{3,2,1,0:T(8,128)(2,1)S(1)}, u32[]{:S(2)}, u32[]{:S(2)}) collective-permute-start(bf16[8,4,16,128]{3,2,1,0:T(8,128)(2,1)} %sum_by_prompt.1.refs_0_), channel_id=1, source_target_pairs={{0,8},{4,12},{8,0},{12,4},{16,24},{20,28},{24,16},{28,20},{1,9},{5... | collective-permute-start | bytes 393224 | tf_op jit(solution)/shard_map/ppermute | solution.py:386
  41.4 0.0 collective-permute-done.1.rest_2_
  41.4 0.0 copy-start.10
  41.4 0.0 collective-permute-done.2.rest_3_
  41.5 0.0 copy-start.11
  41.5 0.0 copy-done.9
  41.5 0.7 %copy-done.10 = f32[1,4,128,128]{3,2,1,0:T(8,128)} copy-done((f32[1,4,128,128]{3,2,1,0:T(8,128)}, f32[1,4,128,128]{3,2,1,0:T(8,128)S(1)}, u32[]{:S(2)}) %copy-start.10) | copy-done | bytes 262168
  42.2 0.1 copy-done.11
  42.3 0.0 copy-start.1
  42.3 11.1 %state_dependent.1 = (bf16[1,128,2048]{2,1,0:T(8,128)(2,1)}, bf16[1,128,2048]{2,1,0:T(8,128)(2,1)}, bf16[1,128,2048]{2,1,0:T(8,128)(2,1)}, bf16[1,16,128]{2,1,0:T(8,128)(2,1)}) custom-call(s32[32]{0:T(128)} %valid_ref.3, bf16[1,128,2048]{2,1,0:T(8,128)(2,1)} %query_ref.3, bf16[1,128,2048]{2,1,0:T(8,128)(2,1)} %key_ref.3, bf16[1,128,2048]{2,1,0:T(8,128)(2,1)} %value_ref.1, ...), custom_call_target="tpu_custom_call" | custom-call | flops 4026531840 | bytes 8388608 | tf_op jit(solution)/shard_map/state_dependent/pallas_call | solution.py:492
  53.4 0.0 collective-permute-done.5.refs_3_
  53.4 0.0 copy-start.2
  53.4 0.0 collective-permute-done.4.refs_2_
  53.4 0.0 copy-start.3
  53.4 0.0 collective-permute-done.3.refs_1_
  53.4 0.0 copy-start.4
  53.4 0.0 copy-done.1
  53.4 0.1 collective-permute-start.6
  53.5 0.5 collective-permute-start.7
  54.0 0.1 collective-permute-start.8
  54.1 0.4 collective-permute-start.9
  54.5 0.3 collective-permute-done.6.refs_4_
  54.9 0.0 copy-start.5
  54.9 0.2 collective-permute-done.7.refs_5_
  55.0 0.3 collective-permute-done.8.refs_6_
  55.4 0.2 collective-permute-done.9.refs_7_
  55.6 0.0 copy-done.2
  55.6 0.0 copy-done.3
  55.6 0.0 copy-done.4
  55.6 0.0 copy-done.5
  55.6 0.1 copy-done.6
  55.7 0.3 copy-done.7
  56.0 0.7 %copy-done.8 = bf16[8,4,16,128]{3,2,1,0:T(8,128)(2,1)} copy-done((bf16[8,4,16,128]{3,2,1,0:T(8,128)(2,1)}, bf16[8,4,16,128]{3,2,1,0:T(8,128)(2,1)S(1)}, u32[]{:S(2)}) %copy-start.8) | copy-done | bytes 131096
  56.7 3.2 %spread_pieces.1 = f32[8,4,8,16,128]{4,3,2,1,0:T(8,128)} custom-call(bf16[8,4,16,128]{3,2,1,0:T(8,128)(2,1)} %sum_by_prompt.1.refs_0_, bf16[8,4,16,128]{3,2,1,0:T(8,128)(2,1)} %copy-done.4, bf16[8,4,16,128]{3,2,1,0:T(8,128)(2,1)} %copy-done.3, bf16[8,4,16,128]{3,2,1,0:T(8,128)(2,1)} %copy-done.2, bf16[8,4,16,128]{3,2,1,0:T(8,128)(2,1)} %copy-done.5, ...), custom_call_target="tpu_custom_call" | custom-call | tf_op jit(solution)/shard_map/spread_pieces/pallas_call | solution.py:539
  (3 shorter events, 0.0 us)
Async XLA Ops:
  10.5 23.6 %all-to-all-start = ((bf16[32,1,4,16,128]{4,3,2,1,0:T(8,128)(2,1)}), bf16[32,1,4,16,128]{4,3,2,1,0:T(8,128)(2,1)S(1)}, u32[]{:S(2)}, u32[]{:S(2)}) async-start(bf16[32,1,4,16,128]{4,3,2,1,0:T(8,128)(2,1)} %bitcast.9), calls=%async_computation | async-start | bytes 1048576 | tf_op jit(solution)/shard_map/all_to_all | solution.py:490
  20.5 19.1 %collective-permute-start = (f32[1,4,128,128]{3,2,1,0:T(8,128)}, f32[1,4,128,128]{3,2,1,0:T(8,128)S(1)}, u32[]{:S(2)}, u32[]{:S(2)}) collective-permute-start(f32[1,4,128,128]{3,2,1,0:T(8,128)} %get-tuple-element.30), channel_id=1, source_target_pairs={{0,1},{1,0},{2,3},{3,2},{4,5},{5,4},{6,7},{7,6},{8,9},{9,8},{10,11... | collective-permute-start | bytes 786440 | tf_op jit(solution)/shard_map/ppermute | solution.py:482
  22.3 19.1 %collective-permute-start.1 = (f32[1,4,128,128]{3,2,1,0:T(8,128)}, f32[1,4,128,128]{3,2,1,0:T(8,128)S(1)}, u32[]{:S(2)}, u32[]{:S(2)}) collective-permute-start(f32[1,4,128,128]{3,2,1,0:T(8,128)} %get-tuple-element.31), channel_id=1, source_target_pairs={{0,2},{1,3},{2,0},{3,1},{4,6},{5,7},{6,4},{7,5},{8,10},{9,11},{10,... | collective-permute-start | bytes 786440 | tf_op jit(solution)/shard_map/ppermute | solution.py:482
  23.8 17.7 %collective-permute-start.2 = (f32[1,4,128,128]{3,2,1,0:T(8,128)}, f32[1,4,128,128]{3,2,1,0:T(8,128)S(1)}, u32[]{:S(2)}, u32[]{:S(2)}) collective-permute-start(f32[1,4,128,128]{3,2,1,0:T(8,128)} %get-tuple-element.32), channel_id=1, source_target_pairs={{0,3},{1,2},{2,1},{3,0},{4,7},{5,6},{6,5},{7,4},{8,11},{9,10},{10,... | collective-permute-start | bytes 786440 | tf_op jit(solution)/shard_map/ppermute | solution.py:482
  34.1 0.8 %copy-start = (bf16[32,1,4,16,128]{4,3,2,1,0:T(8,128)(2,1)}, bf16[32,1,4,16,128]{4,3,2,1,0:T(8,128)(2,1)S(1)}, u32[]{:S(2)}) copy-start(bf16[32,1,4,16,128]{4,3,2,1,0:T(8,128)(2,1)S(1)} %all-to-all-done) | copy-start | bytes 1572868
  37.0 16.3 %collective-permute-start.5 = (bf16[8,4,16,128]{3,2,1,0:T(8,128)(2,1)}, bf16[8,4,16,128]{3,2,1,0:T(8,128)(2,1)S(1)}, u32[]{:S(2)}, u32[]{:S(2)}) collective-permute-start(bf16[8,4,16,128]{3,2,1,0:T(8,128)(2,1)} %sum_by_prompt.1.refs_0_), channel_id=1, source_target_pairs={{0,24},{4,28},{8,16},{12,20},{16,8},{20,12},{24,0},{28,4},{1,25},{... | collective-permute-start | bytes 393224 | tf_op jit(solution)/shard_map/ppermute | solution.py:386
  38.5 14.9 %collective-permute-start.4 = (bf16[8,4,16,128]{3,2,1,0:T(8,128)(2,1)}, bf16[8,4,16,128]{3,2,1,0:T(8,128)(2,1)S(1)}, u32[]{:S(2)}, u32[]{:S(2)}) collective-permute-start(bf16[8,4,16,128]{3,2,1,0:T(8,128)(2,1)} %sum_by_prompt.1.refs_0_), channel_id=1, source_target_pairs={{0,16},{4,20},{8,24},{12,28},{16,0},{20,4},{24,8},{28,12},{1,17},{... | collective-permute-start | bytes 393224 | tf_op jit(solution)/shard_map/ppermute | solution.py:386
  39.5 1.9 %copy-start.9 = (f32[1,4,128,128]{3,2,1,0:T(8,128)}, f32[1,4,128,128]{3,2,1,0:T(8,128)S(1)}, u32[]{:S(2)}) copy-start(f32[1,4,128,128]{3,2,1,0:T(8,128)S(1)} %collective-permute-done.rest_1_) | copy-start | bytes 786436
  39.5 13.9 %collective-permute-start.3 = (bf16[8,4,16,128]{3,2,1,0:T(8,128)(2,1)}, bf16[8,4,16,128]{3,2,1,0:T(8,128)(2,1)S(1)}, u32[]{:S(2)}, u32[]{:S(2)}) collective-permute-start(bf16[8,4,16,128]{3,2,1,0:T(8,128)(2,1)} %sum_by_prompt.1.refs_0_), channel_id=1, source_target_pairs={{0,8},{4,12},{8,0},{12,4},{16,24},{20,28},{24,16},{28,20},{1,9},{5... | collective-permute-start | bytes 393224 | tf_op jit(solution)/shard_map/ppermute | solution.py:386
  41.4 0.7 %copy-start.10 = (f32[1,4,128,128]{3,2,1,0:T(8,128)}, f32[1,4,128,128]{3,2,1,0:T(8,128)S(1)}, u32[]{:S(2)}) copy-start(f32[1,4,128,128]{3,2,1,0:T(8,128)S(1)} %collective-permute-done.1.rest_2_) | copy-start | bytes 786436
  41.5 0.8 %copy-start.11 = (f32[1,4,128,128]{3,2,1,0:T(8,128)}, f32[1,4,128,128]{3,2,1,0:T(8,128)S(1)}, u32[]{:S(2)}) copy-start(f32[1,4,128,128]{3,2,1,0:T(8,128)S(1)} %collective-permute-done.2.rest_3_) | copy-start | bytes 786436
  42.3 11.2 %copy-start.1 = (bf16[8,4,16,128]{3,2,1,0:T(8,128)(2,1)S(1)}, bf16[8,4,16,128]{3,2,1,0:T(8,128)(2,1)}, u32[]{:S(2)}) copy-start(bf16[8,4,16,128]{3,2,1,0:T(8,128)(2,1)} %sum_by_prompt.1.refs_0_) | copy-start | bytes 393220
  53.4 2.2 %copy-start.2 = (bf16[8,4,16,128]{3,2,1,0:T(8,128)(2,1)}, bf16[8,4,16,128]{3,2,1,0:T(8,128)(2,1)S(1)}, u32[]{:S(2)}) copy-start(bf16[8,4,16,128]{3,2,1,0:T(8,128)(2,1)S(1)} %collective-permute-done.5.refs_3_) | copy-start | bytes 393220
  53.4 2.2 %copy-start.3 = (bf16[8,4,16,128]{3,2,1,0:T(8,128)(2,1)}, bf16[8,4,16,128]{3,2,1,0:T(8,128)(2,1)S(1)}, u32[]{:S(2)}) copy-start(bf16[8,4,16,128]{3,2,1,0:T(8,128)(2,1)S(1)} %collective-permute-done.4.refs_2_) | copy-start | bytes 393220
  53.4 2.1 %copy-start.4 = (bf16[8,4,16,128]{3,2,1,0:T(8,128)(2,1)}, bf16[8,4,16,128]{3,2,1,0:T(8,128)(2,1)S(1)}, u32[]{:S(2)}) copy-start(bf16[8,4,16,128]{3,2,1,0:T(8,128)(2,1)S(1)} %collective-permute-done.3.refs_1_) | copy-start | bytes 393220
  53.4 1.4 %collective-permute-start.6 = (bf16[8,4,16,128]{3,2,1,0:T(8,128)(2,1)S(1)}, bf16[8,4,16,128]{3,2,1,0:T(8,128)(2,1)S(1)}, u32[]{:S(2)}, u32[]{:S(2)}) collective-permute-start(bf16[8,4,16,128]{3,2,1,0:T(8,128)(2,1)S(1)} %copy-done.1), channel_id=1, source_target_pairs={{0,4},{4,0},{8,12},{12,8},{16,20},{20,16},{24,28},{28,24},{1,5},{5... | collective-permute-start | bytes 393224 | tf_op jit(solution)/shard_map/ppermute | solution.py:389
  53.5 1.5 %collective-permute-start.7 = (bf16[8,4,16,128]{3,2,1,0:T(8,128)(2,1)S(1)}, bf16[8,4,16,128]{3,2,1,0:T(8,128)(2,1)S(1)}, u32[]{:S(2)}, u32[]{:S(2)}) collective-permute-start(bf16[8,4,16,128]{3,2,1,0:T(8,128)(2,1)S(1)} %collective-permute-done.3.refs_1_), channel_id=1, source_target_pairs={{0,4},{4,0},{8,12},{12,8},{16,20},{20,16},{24,28},{28,24},{1,5},{5... | collective-permute-start | bytes 393224 | tf_op jit(solution)/shard_map/ppermute | solution.py:389
  54.0 1.3 %collective-permute-start.8 = (bf16[8,4,16,128]{3,2,1,0:T(8,128)(2,1)S(1)}, bf16[8,4,16,128]{3,2,1,0:T(8,128)(2,1)S(1)}, u32[]{:S(2)}, u32[]{:S(2)}) collective-permute-start(bf16[8,4,16,128]{3,2,1,0:T(8,128)(2,1)S(1)} %collective-permute-done.4.refs_2_), channel_id=1, source_target_pairs={{0,4},{4,0},{8,12},{12,8},{16,20},{20,16},{24,28},{28,24},{1,5},{5... | collective-permute-start | bytes 393224 | tf_op jit(solution)/shard_map/ppermute | solution.py:389
  54.1 1.5 %collective-permute-start.9 = (bf16[8,4,16,128]{3,2,1,0:T(8,128)(2,1)S(1)}, bf16[8,4,16,128]{3,2,1,0:T(8,128)(2,1)S(1)}, u32[]{:S(2)}, u32[]{:S(2)}) collective-permute-start(bf16[8,4,16,128]{3,2,1,0:T(8,128)(2,1)S(1)} %collective-permute-done.5.refs_3_), channel_id=1, source_target_pairs={{0,4},{4,0},{8,12},{12,8},{16,20},{20,16},{24,28},{28,24},{1,5},{5... | collective-permute-start | bytes 393224 | tf_op jit(solution)/shard_map/ppermute | solution.py:389
  54.9 0.7 %copy-start.5 = (bf16[8,4,16,128]{3,2,1,0:T(8,128)(2,1)}, bf16[8,4,16,128]{3,2,1,0:T(8,128)(2,1)S(1)}, u32[]{:S(2)}) copy-start(bf16[8,4,16,128]{3,2,1,0:T(8,128)(2,1)S(1)} %collective-permute-done.6.refs_4_) | copy-start | bytes 393220
  55.0 0.7 %copy-start.6 = (bf16[8,4,16,128]{3,2,1,0:T(8,128)(2,1)}, bf16[8,4,16,128]{3,2,1,0:T(8,128)(2,1)S(1)}, u32[]{:S(2)}) copy-start(bf16[8,4,16,128]{3,2,1,0:T(8,128)(2,1)S(1)} %collective-permute-done.7.refs_5_) | copy-start | bytes 393220
  55.4 0.7 %copy-start.7 = (bf16[8,4,16,128]{3,2,1,0:T(8,128)(2,1)}, bf16[8,4,16,128]{3,2,1,0:T(8,128)(2,1)S(1)}, u32[]{:S(2)}) copy-start(bf16[8,4,16,128]{3,2,1,0:T(8,128)(2,1)S(1)} %collective-permute-done.8.refs_6_) | copy-start | bytes 393220
  56.0 0.7 %copy-start.8 = (bf16[8,4,16,128]{3,2,1,0:T(8,128)(2,1)}, bf16[8,4,16,128]{3,2,1,0:T(8,128)(2,1)S(1)}, u32[]{:S(2)}) copy-start(bf16[8,4,16,128]{3,2,1,0:T(8,128)(2,1)S(1)} %collective-permute-done.9.refs_7_) | copy-start | bytes 393220

commit v3 on v2

--- a/solution.py
+++ b/solution.py
@@ -112,85 +112,144 @@
     )
 
 
-def head_column(values, head):
-    lane = iota2(values.shape, 1)
-    return jnp.sum(jnp.where(lane == head, values, 0.0), axis=1, keepdims=True)
-
-
 def own_branch(count):
     place = lax.axis_index("grp") * lax.axis_size("head") + lax.axis_index("head")
     return place * count
 
 
+def halves(heads, head_dim):
+    parts = 2 if heads % 2 == 0 else 1
+    size = heads // parts
+    numbers = [range(p * size, (p + 1) * size) for p in range(parts)]
+    return [(list(n), slice(n[0] * head_dim, (n[-1] + 1) * head_dim)) for n in numbers]
+
+
+def start_all(pairs, done, first=0):
+    copies = [pltpu.make_async_copy(a, b, done.at[first + i]) for i, (a, b) in enumerate(pairs)]
+    for copy in copies:
+        copy.start()
+    return copies
+
+
+def head_lanes(j, head_dim):
+    return slice(j * head_dim, (j + 1) * head_dim)
+
+
 def first_kernel(
-    per_step,
     width,
     valid_ref,
-    query_ref,
-    key_ref,
-    decay_ref,
-    grad_ref,
+    query_hbm,
+    key_hbm,
+    decay_hbm,
+    grad_hbm,
+    beta_hbm,
+    value_grad_hbm,
+    value_low_hbm,
+    inverse_hbm,
+    coded_hbm,
+    rows_ref,
     beta_ref,
     value_grad_ref,
     value_low_ref,
     inverse_ref,
     coded_ref,
+    arrival,
+    departure,
 ):
-    tokens = query_ref.shape[1]
-    head_dim = query_ref.shape[2] // per_step
-    pieces = coded_ref.shape[0]
-    valid = valid_ref[own_branch(pl.num_programs(0)) + pl.program_id(0)]
+    branch = pl.program_id(0)
+    heads, tokens, _ = inverse_ref.shape
+    pieces, _, piece_rows, head_dim = coded_ref.shape
+    parts = halves(heads, head_dim)
+    inputs = (query_hbm, key_hbm, decay_hbm)
+
+    def fetch(p):
+        lanes = parts[p][1]
+        return start_all(
+            [(x.at[branch, :, lanes], rows_ref.at[i, :, lanes]) for i, x in enumerate(inputs)],
+            arrival,
+            3 * p,
+        )
+
+    arriving = fetch(0)
+    valid = valid_ref[own_branch(pl.num_programs(0)) + branch]
     row, col = iota2((tokens, tokens), 0), iota2((tokens, tokens), 1)
     tri = (row >= col).astype(BF16)
     keep = iota2((tokens, 1), 0) < valid
     lane_keep = iota2((1, tokens), 1) < valid
-    flat_betas = jax.nn.sigmoid(beta_ref[0].astype(F32)) * lane_keep.astype(F32)
+    rows, across, scores = [], [], []
+    for p, (numbers, _) in enumerate(parts):
+        for copy in arriving:
+            copy.wait()
+        if p + 1 < len(parts):
+            arriving = fetch(p + 1)
+        else:
+            arriving = start_all(
+                [(beta_hbm.at[branch], beta_ref), (grad_hbm.at[branch], rows_ref.at[3])],
+                arrival,
+                3 * len(parts),
+            )
+        fresh = [
+            decayed_rows(*(rows_ref[i, :, head_lanes(j, head_dim)] for i in range(3)), valid, tri)
+            for j in numbers
+        ]
+        turned = [
+            split(jnp.concatenate([r["key_forward"], r["query_forward"]], axis=0).T) for r in fresh
+        ]
+        scores += [dot3(split(r["key_earlier"]), x) for r, x in zip(fresh, turned)]
+        rows += fresh
+        across += turned
+    for copy in arriving:
+        copy.wait()
+    out_grad = []
+    for j in range(heads):
+        grad = rows_ref[3, :, head_lanes(j, head_dim)]
+        out_grad.append(jnp.where(keep, grad, jnp.zeros_like(grad)))
+    flat_betas = jax.nn.sigmoid(beta_ref[...].astype(F32)) * lane_keep.astype(F32)
     betas = flat_betas.T
-    heads = range(per_step)
-    lanes = [slice(j * head_dim, (j + 1) * head_dim) for j in heads]
-    number = [pl.program_id(1) * per_step + j for j in heads]
-    rows = [
-        decayed_rows(
-            query_ref[0, :, lanes[j]], key_ref[0, :, lanes[j]], decay_ref[0, :, lanes[j]], valid, tri
-        )
-        for j in heads
-    ]
-    beta = [head_column(betas, n) for n in number]
-    flat_beta = [
-        jnp.sum(
-            jnp.where(iota2(flat_betas.shape, 0) == n, flat_betas, 0.0), axis=0, keepdims=True
-        )
-        for n in number
-    ]
-    out_grad = []
-    for j in heads:
-        grad = grad_ref[0, :, lanes[j]]
-        out_grad.append(jnp.where(keep, grad, jnp.zeros_like(grad)))
-    across = [
-        split(jnp.concatenate([r["key_forward"], r["query_forward"]], axis=0).T) for r in rows
-    ]
-    scores = [dot3(split(r["key_earlier"]), x) for r, x in zip(rows, across)]
+    every = range(heads)
+    beta = [betas[:, j : j + 1] for j in every]
     coupling = [
-        jnp.where(row < col, s[:, :tokens] * b, 0.0) for s, b in zip(scores, flat_beta)
+        jnp.where(row < col, s[:, :tokens] * flat_betas[j : j + 1], 0.0)
+        for j, s in enumerate(scores)
     ]
     attend = [split(jnp.where(row <= col, s[:, tokens:], 0.0)) for s in scores]
     inverse = [split(x) for x in unit_upper_inverse(coupling, width)]
-    update_grad = [
-        split(dot(p[0], g) + dot(p[1], g)) for p, g in zip(attend, out_grad)
-    ]
+    for j in every:
+        inverse_ref[j] = jnp.concatenate(inverse[j], axis=1)
+    leaving = start_all([(inverse_ref, inverse_hbm.at[branch])], departure)
+    update_grad = [split(dot(p[0], g) + dot(p[1], g)) for p, g in zip(attend, out_grad)]
     value_grad = [split(b * dot3(d, u)) for b, d, u in zip(beta, inverse, update_grad)]
-    for j in heads:
-        high = jnp.concatenate([-value_grad[j][0], out_grad[j]], axis=0)
-        start = jnp.broadcast_to(rows[j]["start"], (8, head_dim)).T[:, :1]
-        state_grad = start * (
-            dot(across[j][0], high)
-            + dot(across[j][1], high)
-            - dot(across[j][0][:, :tokens], value_grad[j][1])
+    for j in every:
+        value_grad_ref[:, head_lanes(j, head_dim)] = value_grad[j][0]
+        value_low_ref[:, head_lanes(j, head_dim)] = value_grad[j][1]
+    leaving += start_all(
+        [
+            (value_grad_ref, value_grad_hbm.at[branch]),
+            (value_low_ref, value_low_hbm.at[branch]),
+        ],
+        departure,
+        1,
+    )
+    for p, (numbers, _) in enumerate(parts):
+        for j in numbers:
+            high = jnp.concatenate([-value_grad[j][0], out_grad[j]], axis=0)
+            start = jnp.broadcast_to(rows[j]["start"], (8, head_dim)).T[:, :1]
+            state_grad = start * (
+                dot(across[j][0], high)
+                + dot(across[j][1], high)
+                - dot(across[j][0][:, :tokens], value_grad[j][1])
+            )
+            coded_ref[:, j] = encode(state_grad).reshape(pieces, piece_rows, head_dim)
+        first, size = numbers[0], len(numbers)
+        copy = pltpu.make_async_copy(
+            coded_ref.at[:, pl.ds(first, size)],
+            coded_hbm.at[:, pl.ds(branch * heads + first, size)],
+            departure.at[3 + p],
         )
-        coded_ref[:, j] = encode(state_grad).reshape(pieces, head_dim // pieces, head_dim)
-        value_grad_ref[0, :, lanes[j]] = value_grad[j][0]
-        value_low_ref[0, :, lanes[j]] = value_grad[j][1]
-        inverse_ref[0, j] = jnp.concatenate(inverse[j], axis=1)
+        copy.start()
+        leaving.append(copy)
+    for copy in leaving:
+        copy.wait()
 
 
 def choose_kernel(prompt_ref, state_ref, *rest):
@@ -218,93 +277,70 @@
         write.wait()
 
 
-def second_kernel(
-    per_step,
-    members,
-    valid_ref,
-    query_ref,
-    key_ref,
-    value_ref,
-    decay_ref,
-    grad_ref,
-    beta_ref,
-    value_grad_ref,
-    value_low_ref,
-    inverse_ref,
-    *rest,
-):
-    arrived, rest = rest[:members], rest[members:]
-    query_grad_ref, key_grad_ref, decay_grad_ref, beta_grad_ref, strength_ref = rest[:5]
-    state_ref, arrival = rest[5:]
-    tokens = query_ref.shape[1]
-    head_dim = query_ref.shape[2] // per_step
-    step = pl.program_id(1)
-
-    @pl.when(step == 0)
-    def _():
-        copies = []
-        for i in range(members):
-            _, sender = meeting(i)
-            copies.append(
-                pltpu.make_async_copy(
-                    arrived[i].at[pl.program_id(0)], state_ref.at[sender], arrival.at[i]
-                )
-            )
-        for copy in copies:
-            copy.start()
-        for copy in copies:
-            copy.wait()
-        strength_ref[...] = jnp.zeros_like(strength_ref)
-
-    valid = valid_ref[own_branch(pl.num_programs(0)) + pl.program_id(0)]
+def second_kernel(members, valid_ref, *refs):
+    row_hbm, (beta_hbm, inverse_hbm), refs = refs[:7], refs[7:9], refs[9:]
+    state_hbm, out_hbm, refs = refs[:members], refs[members : members + 4], refs[members + 4 :]
+    rows_ref, beta_ref, inverse_ref, state_ref, out_ref, beta_grad_ref, arrival, departure = refs
+    branch = pl.program_id(0)
+    heads, tokens, _ = inverse_ref.shape
+    head_dim = rows_ref.shape[2] // heads
+    here = state_ref.shape[1]
+    parts = halves(heads, head_dim)
+    pairs = []
+    for numbers, lanes in parts:
+        for i, ref in enumerate(row_hbm):
+            pairs.append((ref.at[branch, :, lanes], rows_ref.at[i, :, lanes]))
+        some = pl.ds(numbers[0], len(numbers))
+        pairs.append((inverse_hbm.at[branch, some], inverse_ref.at[some]))
+    for i in range(members):
+        _, sender = meeting(i)
+        pairs.append((state_hbm[i].at[branch], state_ref.at[sender]))
+    pairs.append((beta_hbm.at[branch], beta_ref))
+    arriving = start_all(pairs, arrival)
+    each = len(row_hbm) + 1
+
+    valid = valid_ref[own_branch(pl.num_programs(0)) + branch]
     row, col = iota2((tokens, tokens), 0), iota2((tokens, tokens), 1)
     tri = (row >= col).astype(BF16)
     later = (row <= col).astype(BF16)
     later = jnp.concatenate([later, later], axis=1)
     keep = iota2((tokens, 1), 0) < valid
-    logits = beta_ref[0].astype(F32).T
+    rows, own_rows = [], []
+    for p, (numbers, _) in enumerate(parts):
+        for copy in arriving[each * p : each * (p + 1)]:
+            copy.wait()
+        for j in numbers:
+            own_rows.append([rows_ref[i, :, head_lanes(j, head_dim)] for i in range(len(row_hbm))])
+            query, key, _, decay = own_rows[j][:4]
+            rows.append(decayed_rows(query, key, decay, valid, tri))
+    for copy in arriving[each * len(parts) :]:
+        copy.wait()
+    logits = beta_ref[...].astype(F32).T
     betas = jax.nn.sigmoid(logits) * keep.astype(F32)
-    heads = range(per_step)
-    lanes = [slice(j * head_dim, (j + 1) * head_dim) for j in heads]
-    number = [step * per_step + j for j in heads]
-    here = state_ref.shape[1]
-    rows = [
-        decayed_rows(
-            query_ref[0, :, lanes[j]],
-            key_ref[0, :, lanes[j]],
-            decay_ref[0, :, lanes[j]],
-            valid,
-            tri,
-        )
-        for j in heads
-    ]
-    beta = [head_column(betas, n) for n in number]
-    state = [state_ref[n // here, n % here] for n in number]
+    every = range(heads)
+    state = [state_ref[j // here, j % here] for j in every]
     target = [
-        value_ref[0, :, lanes[j]].astype(F32)
+        own_rows[j][2].astype(F32)
         - dot3(split(rows[j]["key_forward"] * rows[j]["start"]), split(state[j]))
-        for j in heads
+        for j in every
     ]
     update = [
         split(
             dot3(
-                split((b * x).T),
-                (inverse_ref[0, j, :, :tokens], inverse_ref[0, j, :, tokens:]),
+                split((betas[:, j : j + 1] * target[j]).T),
+                (inverse_ref[j, :, :tokens], inverse_ref[j, :, tokens:]),
             )
         )
-        for j, b, x in zip(heads, beta, target)
+        for j in every
     ]
     against = [stack(u, split(x.T), 1) for u, x in zip(update, state)]
     products = []
-    for j in heads:
-        grad = grad_ref[0, :, lanes[j]]
+    for j in every:
+        grad, high, low = own_rows[j][4:]
         grad = jnp.where(keep, grad, jnp.zeros_like(grad))
-        high = jnp.concatenate([grad, -value_grad_ref[0, :, lanes[j]]], axis=0)
+        high = jnp.concatenate([grad, -high], axis=0)
         total = dot(high, against[j][0]) + dot(high, against[j][1])
-        low = dot(value_low_ref[0, :, lanes[j]], against[j][0])
-        products.append((total[:tokens], total[tokens:] - low))
-
-    strengths = strength_ref[...]
+        products.append((total[:tokens], total[tokens:] - dot(low, against[j][0])))
     attend_grad = [jnp.where(row >= col, p[0][:, :tokens], 0.0) for p in products]
     coupling_grad = [jnp.where(row > col, p[1][:, :tokens], 0.0) for p in products]
     through_rows = [
@@ -318,34 +354,44 @@
         )
         for p, c, r in zip(attend_grad, coupling_grad, rows)
     ]
-    for j in heads:
-        r = rows[j]
-        query_forward = products[j][0][:, tokens:] * r["start"] + through_rows[j][:tokens]
-        key_forward = products[j][1][:, tokens:] * r["start"] + through_rows[j][tokens:]
-        query_unit_grad = query_forward * (r["grow"] * head_dim**-0.5)
-        key_later = key_forward * r["grow"]
-        key_before = earlier[j] * r["shrink"]
-        key_unit_grad = key_later + key_before
-        decay_step = r["unit_query"] * query_unit_grad + r["unit_key"] * (key_later - key_before)
-        decay_grad = dot(later, jnp.concatenate(split(decay_step), axis=0))
-        decay_grad_ref[0, :, lanes[j]] = jnp.where(keep, decay_grad, 0.0).astype(BF16)
-        along = jnp.sum(r["unit_query"] * query_unit_grad, axis=1, keepdims=True)
-        query_grad_ref[0, :, lanes[j]] = (
-            r["query_scale"] * (query_unit_grad - r["unit_query"] * along)
-        ).astype(BF16)
-        along = jnp.sum(r["unit_key"] * key_unit_grad, axis=1, keepdims=True)
-        key_grad_ref[0, :, lanes[j]] = (
-            r["key_scale"] * (key_unit_grad - r["unit_key"] * along)
-        ).astype(BF16)
-        strength = jnp.sum(
-            jnp.where(row == col, -products[j][1][:, :tokens], 0.0), axis=1, keepdims=True
-        )
-        strengths = jnp.where(iota2(logits.shape, 1) == number[j], strength, strengths)
-    strength_ref[...] = strengths
-
-    @pl.when(step == pl.num_programs(1) - 1)
-    def _():
-        beta_grad_ref[0] = (strength_ref[...] * jnp.exp(-logits)).T.astype(BF16)
+    strengths = jnp.zeros(logits.shape, F32)
+    leaving = []
+    for numbers, lanes in parts:
+        for j in numbers:
+            r = rows[j]
+            query_forward = products[j][0][:, tokens:] * r["start"] + through_rows[j][:tokens]
+            key_forward = products[j][1][:, tokens:] * r["start"] + through_rows[j][tokens:]
+            query_unit_grad = query_forward * (r["grow"] * head_dim**-0.5)
+            key_later = key_forward * r["grow"]
+            key_before = earlier[j] * r["shrink"]
+            key_unit_grad = key_later + key_before
+            decay_step = r["unit_query"] * query_unit_grad + r["unit_key"] * (
+                key_later - key_before
+            )
+            decay_grad = dot(later, jnp.concatenate(split(decay_step), axis=0))
+            decay_grad = jnp.where(keep, decay_grad, 0.0)
+            along = jnp.sum(r["unit_query"] * query_unit_grad, axis=1, keepdims=True)
+            query_grad = r["query_scale"] * (query_unit_grad - r["unit_query"] * along)
+            along = jnp.sum(r["unit_key"] * key_unit_grad, axis=1, keepdims=True)
+            key_grad = r["key_scale"] * (key_unit_grad - r["unit_key"] * along)
+            for i, grad in enumerate((query_grad, key_grad, decay_grad)):
+                out_ref[i, :, head_lanes(j, head_dim)] = grad.astype(BF16)
+            strength = jnp.sum(
+                jnp.where(row == col, -products[j][1][:, :tokens], 0.0), axis=1, keepdims=True
+            )
+            strengths = jnp.where(iota2(logits.shape, 1) == j, strength, strengths)
+        for i in range(3):
+            copy = pltpu.make_async_copy(
+                out_ref.at[i, :, lanes], out_hbm[i].at[branch, :, lanes], departure.at[len(leaving)]
+            )
+            copy.start()
+            leaving.append(copy)
+    beta_grad_ref[...] = (strengths * jnp.exp(-logits)).T.astype(BF16)
+    copy = pltpu.make_async_copy(beta_grad_ref, out_hbm[3].at[branch], departure.at[len(leaving)])
+    copy.start()
+    leaving.append(copy)
+    for copy in leaving:
+        copy.wait()
 
 
 def sum_kernel(prompt_ref, coded_ref, out_ref, total_ref):
@@ -355,17 +401,26 @@
         total_ref[prompt_ref[branch]] += decode(coded_ref[branch])
         return carry
 
-    lax.fori_loop(0, coded_ref.shape[0], add, 0, unroll=4)
+    lax.fori_loop(0, coded_ref.shape[0], add, 0, unroll=8)
     out_ref[...] = encode(total_ref[...])
 
 
 def spread_kernel(*refs):
-    out_ref = refs[-1]
-    pieces = refs[:-1]
+    pieces, (out_hbm, out_ref, departure) = refs[:-3], refs[-3:]
     chips = len(pieces) // 2
-    for i, piece in enumerate(pieces):
-        place = source(i % chips, chips) ^ (i // chips)
-        out_ref[:, :, pl.ds(place, 1)] = decode(piece[...])[:, :, None]
+    prompts = out_ref.shape[0]
+    parts = next(n for n in (4, 2, 1) if prompts % n == 0)
+    size = prompts // parts
+    leaving = []
+    for p in range(parts):
+        some = pl.ds(p * size, size)
+        for i, piece in enumerate(pieces):
+            place = source(i % chips, chips) ^ (i // chips)
+            out_ref[some, :, pl.ds(place, 1)] = decode(piece[some])[:, :, None]
+        leaving.append(pltpu.make_async_copy(out_ref.at[some], out_hbm.at[some], departure.at[p]))
+        leaving[p].start()
+    for copy in leaving:
+        copy.wait()
 
 
 def source(step, chips):
@@ -420,33 +475,30 @@
     groups = lax.axis_size("grp")
     heads = members * heads_here
     piece_rows = head_dim // groups
-    per_step = next(n for n in (8, 4, 2, 1) if heads % n == 0)
-    steps = heads // per_step
-    params = pltpu.CompilerParams(vmem_limit_bytes=60 * 2**20)
+    params = pltpu.CompilerParams(vmem_limit_bytes=62 * 2**20)
+    small = pltpu.CompilerParams(vmem_limit_bytes=16 * 2**20)
     rows_type = jax.ShapeDtypeStruct(query_rows.shape, BF16)
     units = count * heads * tokens * tokens * head_dim
     betas = jnp.swapaxes(beta_logit, 1, 2)
     anywhere = pl.BlockSpec(memory_space=pl.ANY)
 
-    row_block = pl.BlockSpec((1, tokens, per_step * head_dim), lambda b, i, *_: (b, 0, i))
-    beta_block = pl.BlockSpec((1, heads, tokens), lambda b, i, *_: (b, 0, 0))
-    inverse_block = pl.BlockSpec(
-        (1, per_step, tokens, 2 * tokens), lambda b, i, *_: (b, i, 0, 0)
-    )
+    parts = len(halves(heads, head_dim))
     value_grad, value_low, inverse, coded = pl.pallas_call(
-        functools.partial(first_kernel, per_step, 16),
+        functools.partial(first_kernel, 16),
         grid_spec=pltpu.PrefetchScalarGridSpec(
             num_scalar_prefetch=1,
-            grid=(count, steps),
-            in_specs=[row_block] * 4 + [beta_block],
-            out_specs=[
-                row_block,
-                row_block,
-                inverse_block,
-                pl.BlockSpec(
-                    (groups, per_step, piece_rows, head_dim),
-                    lambda b, i, *_: (0, b * steps + i, 0, 0),
-                ),
+            grid=(count,),
+            in_specs=[anywhere] * 5,
+            out_specs=[anywhere] * 4,
+            scratch_shapes=[
+                pltpu.VMEM((4, tokens, width), BF16),
+                pltpu.VMEM((heads, tokens), BF16),
+                pltpu.VMEM((tokens, width), BF16),
+                pltpu.VMEM((tokens, width), BF16),
+                pltpu.VMEM((heads, tokens, 2 * tokens), BF16),
+                pltpu.VMEM((groups, heads, piece_rows, head_dim), BF16),
+                pltpu.SemaphoreType.DMA((3 * parts + 2,)),
+                pltpu.SemaphoreType.DMA((3 + parts,)),
             ],
         ),
         out_shape=[
@@ -490,18 +542,21 @@
     arrived = lax.all_to_all(coded, ("grp", "head"), 0, 0, tiled=True)
 
     query_grad, key_grad, decay_grad, beta_grad = pl.pallas_call(
-        functools.partial(second_kernel, per_step, members),
+        functools.partial(second_kernel, members),
         grid_spec=pltpu.PrefetchScalarGridSpec(
             num_scalar_prefetch=1,
-            grid=(count, steps),
-            in_specs=[row_block] * 5
-            + [beta_block, row_block, row_block, inverse_block]
-            + [anywhere] * members,
-            out_specs=[row_block] * 3 + [beta_block],
+            grid=(count,),
+            in_specs=[anywhere] * (9 + members),
+            out_specs=[anywhere] * 4,
             scratch_shapes=[
-                pltpu.VMEM((tokens, heads), F32),
+                pltpu.VMEM((7, tokens, width), BF16),
+                pltpu.VMEM((heads, tokens), BF16),
+                pltpu.VMEM((heads, tokens, 2 * tokens), BF16),
                 pltpu.VMEM((members, heads_here, head_dim, head_dim), F32),
-                pltpu.SemaphoreType.DMA((members,)),
+                pltpu.VMEM((3, tokens, width), BF16),
+                pltpu.VMEM((heads, tokens), BF16),
+                pltpu.SemaphoreType.DMA((8 * parts + members + 1,)),
+                pltpu.SemaphoreType.DMA((3 * parts + 1,)),
             ],
         ),
         out_shape=[rows_type] * 3 + [jax.ShapeDtypeStruct((count, heads, tokens), BF16)],
@@ -515,9 +570,9 @@
         value_rows,
         log_decay,
         out_grad,
-        betas,
         value_grad,
         value_low,
+        betas,
         inverse,
         *states,
     )
@@ -532,18 +587,18 @@
         out_specs=whole,
         out_shape=jax.ShapeDtypeStruct(piece_shape, BF16),
         scratch_shapes=[pltpu.VMEM(piece_shape, F32)],
-        compiler_params=params,
+        compiler_params=small,
         name="sum_by_prompt",
     )(branch_prompt, arrived.reshape(branches, heads_here, piece_rows, head_dim))
     pieces = gather_pieces(piece, query_grad)
+    fork_shape = (prompts, heads_here, groups, piece_rows, head_dim)
     grad_fork = pl.pallas_call(
         spread_kernel,
         in_specs=[whole] * len(pieces),
-        out_specs=whole,
-        out_shape=jax.ShapeDtypeStruct(
-            (prompts, heads_here, groups, piece_rows, head_dim), F32
-        ),
-        compiler_params=params,
+        out_specs=anywhere,
+        out_shape=jax.ShapeDtypeStruct(fork_shape, F32),
+        scratch_shapes=[pltpu.VMEM(fork_shape, F32), pltpu.SemaphoreType.DMA((4,))],
+        compiler_params=small,
         name="spread_pieces",
     )(*pieces)
     return (

time: 60.2 us -> 54.2 us (0.900)
  Pallas kernels: 28.9 us -> 24.7 us
  local copies, waits for them, and re-layouts: 2.71 us -> 0.81 us
    pallas_call x3, Pallas kernels: 24.1 us -> 21.1 us  [the longest x1 10.1 us: per_device(): pl.pallas_call(functools.partial(second_kernel, members), grid_spec=pltpu...]
    unnamed x24 -> x8, local copies, waits for them, and re-layouts: 2.71 us -> 0.81 us
    pallas_call x1, Pallas kernels: 2.13 us -> 0.93 us  [per_device(): pl.pallas_call(sum_kernel, in_specs=[scalars, whole], out_specs=whole, ou...]
  transfers between devices with their start and end apart: 11 -> 11, of which waited for: 5 -> 5; matrix products, arithmetic and copies ran while one was open for 0% -> 0% of each run, Pallas kernels for 27% -> 25%
where the time goes in v3:
time: 54.2 us; the launch traced here: 53.9 us
  Pallas kernels  24.7 us (46%)
  starting transfers between devices  16.6 us (31%)
  waiting for transfers between devices  10.9 us (20%)
  between operations  0.9 us (2%)
  local copies, waits for them, and re-layouts  0.81 us (1%)
    pallas_call x1, Pallas kernels, per_device(): pl.pallas_call(functools.partial(second_kernel, members), grid_spec=pltpu...  10.1 us
    all_to_all x1, waiting for transfers between devices, per_device(): arrived = lax.all_to_all(coded, ('grp', 'head'), 0, 0, tiled=True)  9.91 us
    pallas_call x1, Pallas kernels, per_device(): pl.pallas_call(functools.partial(first_kernel, 16), grid_spec=pltpu.Prefe...  9.52 us
    all_to_all x1, starting transfers between devices, per_device(): arrived = lax.all_to_all(coded, ('grp', 'head'), 0, 0, tiled=True)  7.47 us
    ppermute x3, starting transfers between devices, gather_pieces(): pieces.append(lax.ppermute(piece, 'grp', moves))  4.45 us
    ppermute x3, starting transfers between devices, per_device(): lax.ppermute(states[step], 'head', moves_at(step, members))  3.55 us
    pallas_call x1, Pallas kernels, per_device(): pl.pallas_call(choose_kernel, grid_spec=pltpu.PrefetchScalarGridSpec(num_...  2.65 us
    pallas_call x1, Pallas kernels, per_device(): pl.pallas_call(spread_kernel, in_specs=[whole] * len(pieces), out_specs=a...  1.49 us
  transfers between devices with their start and end apart: 11, of which 5 were waited for; matrix products, arithmetic and copies ran while one was open for 0% of the time, Pallas kernels for 25%

profile of v3, /device:TPU:0, one launch (start us, length us, event | category | flops | bytes accessed | tf_op | source)
XLA Modules:
  0.0 53.9 jit_solution(4056160039634989703)
XLA Ops:
  0.6 9.5 %state_independent.1 = (bf16[1,128,2048]{2,1,0:T(8,128)(2,1)}, bf16[1,128,2048]{2,1,0:T(8,128)(2,1)}, bf16[1,16,128,256]{3,2,1,0:T(8,128)(2,1)}, bf16[8,16,16,128]{3,2,1,0:T(8,128)(2,1)}) custom-call(s32[32]{0:T(128)} %valid_ref.3, bf16[1,128,2048]{2,1,0:T(8,128)(2,1)} %refs_0_.1, bf16[1,128,2048]{2,1,0:T(8,128)(2,1)} %refs_1_.1, ...), custom_call_target="tpu_custom_call" | custom-call | flops 3355443200 | bytes 8388608 | tf_op jit(solution)/shard_map/state_independent/pallas_call | solution.py:486
  10.2 0.0 copy-start
  10.2 7.5 %all-to-all-start = ((bf16[32,1,4,16,128]{4,3,2,1,0:T(8,128)(2,1)}), bf16[32,1,4,16,128]{4,3,2,1,0:T(8,128)(2,1)S(1)}, u32[]{:S(2)}, u32[]{:S(2)}) async-start(bf16[32,1,4,16,128]{4,3,2,1,0:T(8,128)(2,1)} %bitcast.9), calls=%async_computation | async-start | bytes 1048576 | tf_op jit(solution)/shard_map/all_to_all | solution.py:542
  17.6 2.7 %choose_states.1 = (f32[1,4,128,128]{3,2,1,0:T(8,128)}, f32[1,4,128,128]{3,2,1,0:T(8,128)}, f32[1,4,128,128]{3,2,1,0:T(8,128)}, f32[1,4,128,128]{3,2,1,0:T(8,128)}) custom-call(s32[32]{0:T(128)} %prompt_ref.3, f32[8,4,128,128]{3,2,1,0:T(8,128)} %state_ref), custom_call_target="tpu_custom_call" | custom-call | tf_op jit(solution)/shard_map/choose_states/pallas_call | solution.py:516
  20.3 1.7 %collective-permute-start = (f32[1,4,128,128]{3,2,1,0:T(8,128)}, f32[1,4,128,128]{3,2,1,0:T(8,128)S(1)}, u32[]{:S(2)}, u32[]{:S(2)}) collective-permute-start(f32[1,4,128,128]{3,2,1,0:T(8,128)} %get-tuple-element.30), channel_id=1, source_target_pairs={{0,1},{1,0},{2,3},{3,2},{4,5},{5,4},{6,7},{7,6},{8,9},{9,8},{10,11... | collective-permute-start | bytes 786440 | tf_op jit(solution)/shard_map/ppermute | solution.py:534
  22.0 1.5 %collective-permute-start.1 = (f32[1,4,128,128]{3,2,1,0:T(8,128)}, f32[1,4,128,128]{3,2,1,0:T(8,128)S(1)}, u32[]{:S(2)}, u32[]{:S(2)}) collective-permute-start(f32[1,4,128,128]{3,2,1,0:T(8,128)} %get-tuple-element.31), channel_id=1, source_target_pairs={{0,2},{1,3},{2,0},{3,1},{4,6},{5,7},{6,4},{7,5},{8,10},{9,11},{10,... | collective-permute-start | bytes 786440 | tf_op jit(solution)/shard_map/ppermute | solution.py:534
  23.4 0.4 collective-permute-start.2
  23.9 9.9 %all-to-all-done = bf16[32,1,4,16,128]{4,3,2,1,0:T(8,128)(2,1)S(1)} async-done(((bf16[32,1,4,16,128]{4,3,2,1,0:T(8,128)(2,1)}), bf16[32,1,4,16,128]{4,3,2,1,0:T(8,128)(2,1)S(1)}, u32[]{:S(2)}, u32[]{:S(2)}) %all-to-all-start) | async-done | bytes 524320 | tf_op jit(solution)/shard_map/all_to_all | solution.py:542
  33.8 0.0 copy-done
  33.8 0.9 %sum_by_prompt.1.refs_0_ = bf16[8,4,16,128]{3,2,1,0:T(8,128)(2,1)S(1)} custom-call(s32[32]{0:T(128)S(1)} %copy-done, bf16[32,4,16,128]{3,2,1,0:T(8,128)(2,1)S(1)} %bitcast.7), custom_call_target="tpu_custom_call" | custom-call | tf_op jit(solution)/shard_map/sum_by_prompt/pallas_call | solution.py:584
  34.7 1.5 %collective-permute-start.5 = (bf16[8,4,16,128]{3,2,1,0:T(8,128)(2,1)S(1)}, bf16[8,4,16,128]{3,2,1,0:T(8,128)(2,1)S(1)}, u32[]{:S(2)}, u32[]{:S(2)}) collective-permute-start(bf16[8,4,16,128]{3,2,1,0:T(8,128)(2,1)S(1)} %sum_by_prompt.1.refs_0_), channel_id=1, source_target_pairs={{0,24},{4,28},{8,16},{12,20},{16,8},{20,12},{24,0},{28,4},{1,25},{... | collective-permute-start | bytes 393224 | tf_op jit(solution)/shard_map/ppermute | solution.py:441
  36.2 1.1 %collective-permute-start.4 = (bf16[8,4,16,128]{3,2,1,0:T(8,128)(2,1)S(1)}, bf16[8,4,16,128]{3,2,1,0:T(8,128)(2,1)S(1)}, u32[]{:S(2)}, u32[]{:S(2)}) collective-permute-start(bf16[8,4,16,128]{3,2,1,0:T(8,128)(2,1)S(1)} %sum_by_prompt.1.refs_0_), channel_id=1, source_target_pairs={{0,16},{4,20},{8,24},{12,28},{16,0},{20,4},{24,8},{28,12},{1,17},{... | collective-permute-start | bytes 393224 | tf_op jit(solution)/shard_map/ppermute | solution.py:441
  37.3 0.0 collective-permute-done.refs_10_
  37.3 0.0 copy-start.1
  37.3 1.9 %collective-permute-start.3 = (bf16[8,4,16,128]{3,2,1,0:T(8,128)(2,1)S(1)}, bf16[8,4,16,128]{3,2,1,0:T(8,128)(2,1)S(1)}, u32[]{:S(2)}, u32[]{:S(2)}) collective-permute-start(bf16[8,4,16,128]{3,2,1,0:T(8,128)(2,1)S(1)} %sum_by_prompt.1.refs_0_), channel_id=1, source_target_pairs={{0,8},{4,12},{8,0},{12,4},{16,24},{20,28},{24,16},{28,20},{1,9},{5... | collective-permute-start | bytes 393224 | tf_op jit(solution)/shard_map/ppermute | solution.py:441
  39.2 0.0 collective-permute-done.1.refs_11_
  39.2 0.0 copy-start.2
  39.2 0.0 collective-permute-done.2.refs_12_
  39.2 0.0 copy-start.3
  39.2 0.0 copy-done.1
  39.2 0.7 %copy-done.2 = f32[1,4,128,128]{3,2,1,0:T(8,128)} copy-done((f32[1,4,128,128]{3,2,1,0:T(8,128)}, f32[1,4,128,128]{3,2,1,0:T(8,128)S(1)}, u32[]{:S(2)}) %copy-start.2) | copy-done | bytes 262168
  39.9 0.1 copy-done.3
  40.0 10.1 %state_dependent.1 = (bf16[1,128,2048]{2,1,0:T(8,128)(2,1)}, bf16[1,128,2048]{2,1,0:T(8,128)(2,1)}, bf16[1,128,2048]{2,1,0:T(8,128)(2,1)}, bf16[1,16,128]{2,1,0:T(8,128)(2,1)}) custom-call(s32[32]{0:T(128)} %valid_ref.3, bf16[1,128,2048]{2,1,0:T(8,128)(2,1)} %refs_0_.1, bf16[1,128,2048]{2,1,0:T(8,128)(2,1)} %refs_1_.1, bf16[1,128,2048]{2,1,0:T(8,128)(2,1)} %refs_2_.1, ...), custom_call_target="tpu_custom_call" | custom-call | flops 4026531840 | bytes 8388608 | tf_op jit(solution)/shard_map/state_dependent/pallas_call | solution.py:544
  50.1 0.0 collective-permute-done.5.refs_3_
  50.1 0.0 collective-permute-done.4.refs_2_
  50.1 0.0 collective-permute-done.3.refs_1_
  50.1 0.1 collective-permute-start.6
  50.2 0.5 collective-permute-start.7
  50.7 0.1 collective-permute-start.8
  50.7 0.4 collective-permute-start.9
  51.2 0.3 collective-permute-done.6.refs_4_
  51.5 0.2 collective-permute-done.7.refs_5_
  51.7 0.3 collective-permute-done.8.refs_6_
  52.0 0.2 collective-permute-done.9.refs_7_
  52.2 1.5 %spread_pieces.1 = f32[8,4,8,16,128]{4,3,2,1,0:T(8,128)} custom-call(bf16[8,4,16,128]{3,2,1,0:T(8,128)(2,1)S(1)} %sum_by_prompt.1.refs_0_, bf16[8,4,16,128]{3,2,1,0:T(8,128)(2,1)S(1)} %collective-permute-done.3.refs_1_, bf16[8,4,16,128]{3,2,1,0:T(8,128)(2,1)S(1)} %collective-permute-done.4.refs_2_, ...), custom_call_target="tpu_custom_call" | custom-call | tf_op jit(solution)/shard_map/spread_pieces/pallas_call | solution.py:595
Async XLA Ops:
  10.2 23.6 %copy-start = (s32[32]{0:T(128)S(1)}, s32[32]{0:T(128)}, u32[]{:S(2)}) copy-start(s32[32]{0:T(128)} %prompt_ref.3) | copy-start | bytes 388
  10.2 23.6 %all-to-all-start = ((bf16[32,1,4,16,128]{4,3,2,1,0:T(8,128)(2,1)}), bf16[32,1,4,16,128]{4,3,2,1,0:T(8,128)(2,1)S(1)}, u32[]{:S(2)}, u32[]{:S(2)}) async-start(bf16[32,1,4,16,128]{4,3,2,1,0:T(8,128)(2,1)} %bitcast.9), calls=%async_computation | async-start | bytes 1048576 | tf_op jit(solution)/shard_map/all_to_all | solution.py:542
  20.3 17.0 %collective-permute-start = (f32[1,4,128,128]{3,2,1,0:T(8,128)}, f32[1,4,128,128]{3,2,1,0:T(8,128)S(1)}, u32[]{:S(2)}, u32[]{:S(2)}) collective-permute-start(f32[1,4,128,128]{3,2,1,0:T(8,128)} %get-tuple-element.30), channel_id=1, source_target_pairs={{0,1},{1,0},{2,3},{3,2},{4,5},{5,4},{6,7},{7,6},{8,9},{9,8},{10,11... | collective-permute-start | bytes 786440 | tf_op jit(solution)/shard_map/ppermute | solution.py:534
  22.0 17.2 %collective-permute-start.1 = (f32[1,4,128,128]{3,2,1,0:T(8,128)}, f32[1,4,128,128]{3,2,1,0:T(8,128)S(1)}, u32[]{:S(2)}, u32[]{:S(2)}) collective-permute-start(f32[1,4,128,128]{3,2,1,0:T(8,128)} %get-tuple-element.31), channel_id=1, source_target_pairs={{0,2},{1,3},{2,0},{3,1},{4,6},{5,7},{6,4},{7,5},{8,10},{9,11},{10,... | collective-permute-start | bytes 786440 | tf_op jit(solution)/shard_map/ppermute | solution.py:534
  23.4 15.7 %collective-permute-start.2 = (f32[1,4,128,128]{3,2,1,0:T(8,128)}, f32[1,4,128,128]{3,2,1,0:T(8,128)S(1)}, u32[]{:S(2)}, u32[]{:S(2)}) collective-permute-start(f32[1,4,128,128]{3,2,1,0:T(8,128)} %get-tuple-element.32), channel_id=1, source_target_pairs={{0,3},{1,2},{2,1},{3,0},{4,7},{5,6},{6,5},{7,4},{8,11},{9,10},{10,... | collective-permute-start | bytes 786440 | tf_op jit(solution)/shard_map/ppermute | solution.py:534
  34.7 15.4 %collective-permute-start.5 = (bf16[8,4,16,128]{3,2,1,0:T(8,128)(2,1)S(1)}, bf16[8,4,16,128]{3,2,1,0:T(8,128)(2,1)S(1)}, u32[]{:S(2)}, u32[]{:S(2)}) collective-permute-start(bf16[8,4,16,128]{3,2,1,0:T(8,128)(2,1)S(1)} %sum_by_prompt.1.refs_0_), channel_id=1, source_target_pairs={{0,24},{4,28},{8,16},{12,20},{16,8},{20,12},{24,0},{28,4},{1,25},{... | collective-permute-start | bytes 393224 | tf_op jit(solution)/shard_map/ppermute | solution.py:441
  36.2 13.9 %collective-permute-start.4 = (bf16[8,4,16,128]{3,2,1,0:T(8,128)(2,1)S(1)}, bf16[8,4,16,128]{3,2,1,0:T(8,128)(2,1)S(1)}, u32[]{:S(2)}, u32[]{:S(2)}) collective-permute-start(bf16[8,4,16,128]{3,2,1,0:T(8,128)(2,1)S(1)} %sum_by_prompt.1.refs_0_), channel_id=1, source_target_pairs={{0,16},{4,20},{8,24},{12,28},{16,0},{20,4},{24,8},{28,12},{1,17},{... | collective-permute-start | bytes 393224 | tf_op jit(solution)/shard_map/ppermute | solution.py:441
  37.3 1.9 %copy-start.1 = (f32[1,4,128,128]{3,2,1,0:T(8,128)}, f32[1,4,128,128]{3,2,1,0:T(8,128)S(1)}, u32[]{:S(2)}) copy-start(f32[1,4,128,128]{3,2,1,0:T(8,128)S(1)} %collective-permute-done.refs_10_) | copy-start | bytes 786436
  37.3 12.8 %collective-permute-start.3 = (bf16[8,4,16,128]{3,2,1,0:T(8,128)(2,1)S(1)}, bf16[8,4,16,128]{3,2,1,0:T(8,128)(2,1)S(1)}, u32[]{:S(2)}, u32[]{:S(2)}) collective-permute-start(bf16[8,4,16,128]{3,2,1,0:T(8,128)(2,1)S(1)} %sum_by_prompt.1.refs_0_), channel_id=1, source_target_pairs={{0,8},{4,12},{8,0},{12,4},{16,24},{20,28},{24,16},{28,20},{1,9},{5... | collective-permute-start | bytes 393224 | tf_op jit(solution)/shard_map/ppermute | solution.py:441
  39.2 0.7 %copy-start.2 = (f32[1,4,128,128]{3,2,1,0:T(8,128)}, f32[1,4,128,128]{3,2,1,0:T(8,128)S(1)}, u32[]{:S(2)}) copy-start(f32[1,4,128,128]{3,2,1,0:T(8,128)S(1)} %collective-permute-done.1.refs_11_) | copy-start | bytes 786436
  39.2 0.8 %copy-start.3 = (f32[1,4,128,128]{3,2,1,0:T(8,128)}, f32[1,4,128,128]{3,2,1,0:T(8,128)S(1)}, u32[]{:S(2)}) copy-start(f32[1,4,128,128]{3,2,1,0:T(8,128)S(1)} %collective-permute-done.2.refs_12_) | copy-start | bytes 786436
  50.1 1.4 %collective-permute-start.6 = (bf16[8,4,16,128]{3,2,1,0:T(8,128)(2,1)S(1)}, bf16[8,4,16,128]{3,2,1,0:T(8,128)(2,1)S(1)}, u32[]{:S(2)}, u32[]{:S(2)}) collective-permute-start(bf16[8,4,16,128]{3,2,1,0:T(8,128)(2,1)S(1)} %sum_by_prompt.1.refs_0_), channel_id=1, source_target_pairs={{0,4},{4,0},{8,12},{12,8},{16,20},{20,16},{24,28},{28,24},{1,5},{5... | collective-permute-start | bytes 393224 | tf_op jit(solution)/shard_map/ppermute | solution.py:444
  50.2 1.5 %collective-permute-start.7 = (bf16[8,4,16,128]{3,2,1,0:T(8,128)(2,1)S(1)}, bf16[8,4,16,128]{3,2,1,0:T(8,128)(2,1)S(1)}, u32[]{:S(2)}, u32[]{:S(2)}) collective-permute-start(bf16[8,4,16,128]{3,2,1,0:T(8,128)(2,1)S(1)} %collective-permute-done.3.refs_1_), channel_id=1, source_target_pairs={{0,4},{4,0},{8,12},{12,8},{16,20},{20,16},{24,28},{28,24},{1,5},{5... | collective-permute-start | bytes 393224 | tf_op jit(solution)/shard_map/ppermute | solution.py:444
  50.7 1.3 %collective-permute-start.8 = (bf16[8,4,16,128]{3,2,1,0:T(8,128)(2,1)S(1)}, bf16[8,4,16,128]{3,2,1,0:T(8,128)(2,1)S(1)}, u32[]{:S(2)}, u32[]{:S(2)}) collective-permute-start(bf16[8,4,16,128]{3,2,1,0:T(8,128)(2,1)S(1)} %collective-permute-done.4.refs_2_), channel_id=1, source_target_pairs={{0,4},{4,0},{8,12},{12,8},{16,20},{20,16},{24,28},{28,24},{1,5},{5... | collective-permute-start | bytes 393224 | tf_op jit(solution)/shard_map/ppermute | solution.py:444
  50.7 1.5 %collective-permute-start.9 = (bf16[8,4,16,128]{3,2,1,0:T(8,128)(2,1)S(1)}, bf16[8,4,16,128]{3,2,1,0:T(8,128)(2,1)S(1)}, u32[]{:S(2)}, u32[]{:S(2)}) collective-permute-start(bf16[8,4,16,128]{3,2,1,0:T(8,128)(2,1)S(1)} %collective-permute-done.5.refs_3_), channel_id=1, source_target_pairs={{0,4},{4,0},{8,12},{12,8},{16,20},{20,16},{24,28},{28,24},{1,5},{5... | collective-permute-start | bytes 393224 | tf_op jit(solution)/shard_map/ppermute | solution.py:444

commit v4 on v3

--- a/solution.py
+++ b/solution.py
@@ -40,8 +40,8 @@
     return lax.broadcasted_iota(jnp.int32, shape, axis)
 
 
-def dot3(a, b):
-    return dot(a[0], b[0]) + dot(a[1], b[0]) + dot(a[0], b[1])
+def dot3(a, b, dims=NN):
+    return dot(a[0], b[0], dims) + dot(a[1], b[0], dims) + dot(a[0], b[1], dims)
 
 
 def stack(a, b, axis):
@@ -327,8 +327,9 @@
     update = [
         split(
             dot3(
-                split((betas[:, j : j + 1] * target[j]).T),
+                split(betas[:, j : j + 1] * target[j]),
                 (inverse_ref[j, :, :tokens], inverse_ref[j, :, tokens:]),
+                TN,
             )
         )
         for j in every
@@ -343,16 +344,11 @@
         products.append((total[:tokens], total[tokens:] - dot(low, against[j][0])))
     attend_grad = [jnp.where(row >= col, p[0][:, :tokens], 0.0) for p in products]
     coupling_grad = [jnp.where(row > col, p[1][:, :tokens], 0.0) for p in products]
-    through_rows = [
-        dot3(split(jnp.concatenate([p, c], axis=0)), split(r["key_earlier"]))
-        for p, c, r in zip(attend_grad, coupling_grad, rows)
-    ]
+    both = [split(jnp.concatenate([p, c], axis=0)) for p, c in zip(attend_grad, coupling_grad)]
+    through_rows = [dot3(x, split(r["key_earlier"])) for x, r in zip(both, rows)]
     earlier = [
-        dot3(
-            split(jnp.concatenate([p.T, c.T], axis=1)),
-            split(jnp.concatenate([r["query_forward"], r["key_forward"]], axis=0)),
-        )
-        for p, c, r in zip(attend_grad, coupling_grad, rows)
+        dot3(x, split(jnp.concatenate([r["query_forward"], r["key_forward"]], axis=0)), TN)
+        for x, r in zip(both, rows)
     ]
     strengths = jnp.zeros(logits.shape, F32)
     leaving = []
@@ -415,7 +411,7 @@
     for p in range(parts):
         some = pl.ds(p * size, size)
         for i, piece in enumerate(pieces):
-            place = source(i % chips, chips) ^ (i // chips)
+            place = source(-i % chips, chips) ^ (i // chips)
             out_ref[some, :, pl.ds(place, 1)] = decode(piece[some])[:, :, None]
         leaving.append(pltpu.make_async_copy(out_ref.at[some], out_hbm.at[some], departure.at[p]))
         leaving[p].start()
@@ -435,13 +431,14 @@
     chips = size // 2
     power = chips & (chips - 1) == 0
     pieces = [piece]
-    for step in range(1, chips):
+    for step in reversed(range(1, chips)):
         other = [((c ^ step) if power else (c + step) % chips) for c in range(chips)]
         moves = [(2 * c + core, 2 * other[c] + core) for c in range(chips) for core in range(2)]
         pieces.append(lax.ppermute(piece, "grp", moves))
-    pieces, _ = lax.optimization_barrier((pieces, beside))
     swap = [(i, i ^ 1) for i in range(size)]
-    return pieces + [lax.ppermute(x, "grp", swap) for x in pieces]
+    swapped = lax.ppermute(piece, "grp", swap)
+    pieces, swapped, _ = lax.optimization_barrier((pieces, swapped, beside))
+    return pieces + [swapped] + [lax.ppermute(x, "grp", swap) for x in pieces[1:]]
 
 
 def moves_at(step, members):

time: 54.2 us -> 54 us (level)
  transfers between devices with their start and end apart: 11 -> 11, of which waited for: 5 -> 4; matrix products, arithmetic and copies ran while one was open for 0% -> 0% of each run, Pallas kernels for 25% -> 25%
where the time goes in v4:
time: 54 us; the launch traced here: 53.7 us
  Pallas kernels  24.6 us (46%)
  starting transfers between devices  16.4 us (30%)
  waiting for transfers between devices  10.9 us (20%)
  between operations  0.91 us (2%)
  local copies, waits for them, and re-layouts  0.8 us (1%)
    pallas_call x1, Pallas kernels, per_device(): pl.pallas_call(functools.partial(second_kernel, members), grid_spec=pltpu...  10 us
    all_to_all x1, waiting for transfers between devices, per_device(): arrived = lax.all_to_all(coded, ('grp', 'head'), 0, 0, tiled=True)  9.91 us
    pallas_call x1, Pallas kernels, per_device(): pl.pallas_call(functools.partial(first_kernel, 16), grid_spec=pltpu.Prefe...  9.52 us
    all_to_all x1, starting transfers between devices, per_device(): arrived = lax.all_to_all(coded, ('grp', 'head'), 0, 0, tiled=True)  7.47 us
    ppermute x3, starting transfers between devices, gather_pieces(): pieces.append(lax.ppermute(piece, 'grp', moves))  4.45 us
    ppermute x3, starting transfers between devices, per_device(): lax.ppermute(states[step], 'head', moves_at(step, members))  3.55 us
    pallas_call x1, Pallas kernels, per_device(): pl.pallas_call(choose_kernel, grid_spec=pltpu.PrefetchScalarGridSpec(num_...  2.65 us
    pallas_call x1, Pallas kernels, per_device(): pl.pallas_call(spread_kernel, in_specs=[whole] * len(pieces), out_specs=a...  1.49 us
  transfers between devices with their start and end apart: 11, of which 4 were waited for; matrix products, arithmetic and copies ran while one was open for 0% of the time, Pallas kernels for 25%

profile of v4, /device:TPU:0, one launch (start us, length us, event | category | flops | bytes accessed | tf_op | source)
XLA Modules:
  0.0 53.7 jit_solution(584736103643791167)
XLA Ops:
  0.6 9.5 %state_independent.1 = (bf16[1,128,2048]{2,1,0:T(8,128)(2,1)}, bf16[1,128,2048]{2,1,0:T(8,128)(2,1)}, bf16[1,16,128,256]{3,2,1,0:T(8,128)(2,1)}, bf16[8,16,16,128]{3,2,1,0:T(8,128)(2,1)}) custom-call(s32[32]{0:T(128)} %valid_ref.3, bf16[1,128,2048]{2,1,0:T(8,128)(2,1)} %refs_0_.1, bf16[1,128,2048]{2,1,0:T(8,128)(2,1)} %refs_1_.1, ...), custom_call_target="tpu_custom_call" | custom-call | flops 3355443200 | bytes 8388608 | tf_op jit(solution)/shard_map/state_independent/pallas_call | solution.py:483
  10.2 0.0 copy-start
  10.2 7.5 %all-to-all-start = ((bf16[32,1,4,16,128]{4,3,2,1,0:T(8,128)(2,1)}), bf16[32,1,4,16,128]{4,3,2,1,0:T(8,128)(2,1)S(1)}, u32[]{:S(2)}, u32[]{:S(2)}) async-start(bf16[32,1,4,16,128]{4,3,2,1,0:T(8,128)(2,1)} %bitcast.9), calls=%async_computation | async-start | bytes 1048576 | tf_op jit(solution)/shard_map/all_to_all | solution.py:539
  17.6 2.7 %choose_states.1 = (f32[1,4,128,128]{3,2,1,0:T(8,128)}, f32[1,4,128,128]{3,2,1,0:T(8,128)}, f32[1,4,128,128]{3,2,1,0:T(8,128)}, f32[1,4,128,128]{3,2,1,0:T(8,128)}) custom-call(s32[32]{0:T(128)} %prompt_ref.3, f32[8,4,128,128]{3,2,1,0:T(8,128)} %state_ref), custom_call_target="tpu_custom_call" | custom-call | tf_op jit(solution)/shard_map/choose_states/pallas_call | solution.py:513
  20.3 1.7 %collective-permute-start = (f32[1,4,128,128]{3,2,1,0:T(8,128)}, f32[1,4,128,128]{3,2,1,0:T(8,128)S(1)}, u32[]{:S(2)}, u32[]{:S(2)}) collective-permute-start(f32[1,4,128,128]{3,2,1,0:T(8,128)} %get-tuple-element.31), channel_id=1, source_target_pairs={{0,1},{1,0},{2,3},{3,2},{4,5},{5,4},{6,7},{7,6},{8,9},{9,8},{10,11... | collective-permute-start | bytes 786440 | tf_op jit(solution)/shard_map/ppermute | solution.py:531
  22.0 1.5 %collective-permute-start.1 = (f32[1,4,128,128]{3,2,1,0:T(8,128)}, f32[1,4,128,128]{3,2,1,0:T(8,128)S(1)}, u32[]{:S(2)}, u32[]{:S(2)}) collective-permute-start(f32[1,4,128,128]{3,2,1,0:T(8,128)} %get-tuple-element.32), channel_id=1, source_target_pairs={{0,2},{1,3},{2,0},{3,1},{4,6},{5,7},{6,4},{7,5},{8,10},{9,11},{10,... | collective-permute-start | bytes 786440 | tf_op jit(solution)/shard_map/ppermute | solution.py:531
  23.4 0.4 collective-permute-start.2
  23.9 9.9 %all-to-all-done = bf16[32,1,4,16,128]{4,3,2,1,0:T(8,128)(2,1)S(1)} async-done(((bf16[32,1,4,16,128]{4,3,2,1,0:T(8,128)(2,1)}), bf16[32,1,4,16,128]{4,3,2,1,0:T(8,128)(2,1)S(1)}, u32[]{:S(2)}, u32[]{:S(2)}) %all-to-all-start) | async-done | bytes 524320 | tf_op jit(solution)/shard_map/all_to_all | solution.py:539
  33.8 0.0 copy-done
  33.8 0.9 %sum_by_prompt.1.refs_0_ = bf16[8,4,16,128]{3,2,1,0:T(8,128)(2,1)S(1)} custom-call(s32[32]{0:T(128)S(1)} %copy-done, bf16[32,4,16,128]{3,2,1,0:T(8,128)(2,1)S(1)} %bitcast.7), custom_call_target="tpu_custom_call" | custom-call | tf_op jit(solution)/shard_map/sum_by_prompt/pallas_call | solution.py:581
  34.7 1.5 %collective-permute-start.3 = (bf16[8,4,16,128]{3,2,1,0:T(8,128)(2,1)S(1)}, bf16[8,4,16,128]{3,2,1,0:T(8,128)(2,1)S(1)}, u32[]{:S(2)}, u32[]{:S(2)}) collective-permute-start(bf16[8,4,16,128]{3,2,1,0:T(8,128)(2,1)S(1)} %sum_by_prompt.1.refs_0_), channel_id=1, source_target_pairs={{0,24},{4,28},{8,16},{12,20},{16,8},{20,12},{24,0},{28,4},{1,25},{... | collective-permute-start | bytes 393224 | tf_op jit(solution)/shard_map/ppermute | solution.py:437
  36.2 1.1 %collective-permute-start.4 = (bf16[8,4,16,128]{3,2,1,0:T(8,128)(2,1)S(1)}, bf16[8,4,16,128]{3,2,1,0:T(8,128)(2,1)S(1)}, u32[]{:S(2)}, u32[]{:S(2)}) collective-permute-start(bf16[8,4,16,128]{3,2,1,0:T(8,128)(2,1)S(1)} %sum_by_prompt.1.refs_0_), channel_id=1, source_target_pairs={{0,16},{4,20},{8,24},{12,28},{16,0},{20,4},{24,8},{28,12},{1,17},{... | collective-permute-start | bytes 393224 | tf_op jit(solution)/shard_map/ppermute | solution.py:437
  37.3 0.0 collective-permute-done.refs_10_
  37.3 0.0 copy-start.1
  37.3 1.9 %collective-permute-start.5 = (bf16[8,4,16,128]{3,2,1,0:T(8,128)(2,1)S(1)}, bf16[8,4,16,128]{3,2,1,0:T(8,128)(2,1)S(1)}, u32[]{:S(2)}, u32[]{:S(2)}) collective-permute-start(bf16[8,4,16,128]{3,2,1,0:T(8,128)(2,1)S(1)} %sum_by_prompt.1.refs_0_), channel_id=1, source_target_pairs={{0,8},{4,12},{8,0},{12,4},{16,24},{20,28},{24,16},{28,20},{1,9},{5... | collective-permute-start | bytes 393224 | tf_op jit(solution)/shard_map/ppermute | solution.py:437
  39.2 0.0 collective-permute-done.1.refs_11_
  39.2 0.0 copy-start.2
  39.2 0.0 collective-permute-start.6
  39.2 0.0 collective-permute-done.2.refs_12_
  39.2 0.0 copy-start.3
  39.2 0.0 copy-done.1
  39.2 0.7 %copy-done.2 = f32[1,4,128,128]{3,2,1,0:T(8,128)} copy-done((f32[1,4,128,128]{3,2,1,0:T(8,128)}, f32[1,4,128,128]{3,2,1,0:T(8,128)S(1)}, u32[]{:S(2)}) %copy-start.2) | copy-done | bytes 262168
  39.9 0.1 copy-done.3
  40.0 10.0 %state_dependent.1 = (bf16[1,128,2048]{2,1,0:T(8,128)(2,1)}, bf16[1,128,2048]{2,1,0:T(8,128)(2,1)}, bf16[1,128,2048]{2,1,0:T(8,128)(2,1)}, bf16[1,16,128]{2,1,0:T(8,128)(2,1)}) custom-call(s32[32]{0:T(128)} %valid_ref.3, bf16[1,128,2048]{2,1,0:T(8,128)(2,1)} %refs_0_.1, bf16[1,128,2048]{2,1,0:T(8,128)(2,1)} %refs_1_.1, bf16[1,128,2048]{2,1,0:T(8,128)(2,1)} %refs_2_.1, ...), custom_call_target="tpu_custom_call" | custom-call | flops 4026531840 | bytes 8388608 | tf_op jit(solution)/shard_map/state_dependent/pallas_call | solution.py:541
  50.0 0.0 collective-permute-done.3.refs_1_
  50.0 0.0 collective-permute-done.4.refs_2_
  50.0 0.0 collective-permute-done.5.refs_3_
  50.0 0.0 collective-permute-done.6.refs_4_
  50.1 0.5 collective-permute-start.7
  50.5 0.1 collective-permute-start.8
  50.6 0.4 collective-permute-start.9
  51.0 0.5 collective-permute-done.7.refs_5_
  51.5 0.4 collective-permute-done.8.refs_6_
  51.9 0.2 collective-permute-done.9.refs_7_
  52.0 1.5 %spread_pieces.1 = f32[8,4,8,16,128]{4,3,2,1,0:T(8,128)} custom-call(bf16[8,4,16,128]{3,2,1,0:T(8,128)(2,1)S(1)} %sum_by_prompt.1.refs_0_, bf16[8,4,16,128]{3,2,1,0:T(8,128)(2,1)S(1)} %collective-permute-done.3.refs_1_, bf16[8,4,16,128]{3,2,1,0:T(8,128)(2,1)S(1)} %collective-permute-done.4.refs_2_, ...), custom_call_target="tpu_custom_call" | custom-call | tf_op jit(solution)/shard_map/spread_pieces/pallas_call | solution.py:592
Async XLA Ops:
  10.2 23.6 %copy-start = (s32[32]{0:T(128)S(1)}, s32[32]{0:T(128)}, u32[]{:S(2)}) copy-start(s32[32]{0:T(128)} %prompt_ref.3) | copy-start | bytes 388
  10.2 23.6 %all-to-all-start = ((bf16[32,1,4,16,128]{4,3,2,1,0:T(8,128)(2,1)}), bf16[32,1,4,16,128]{4,3,2,1,0:T(8,128)(2,1)S(1)}, u32[]{:S(2)}, u32[]{:S(2)}) async-start(bf16[32,1,4,16,128]{4,3,2,1,0:T(8,128)(2,1)} %bitcast.9), calls=%async_computation | async-start | bytes 1048576 | tf_op jit(solution)/shard_map/all_to_all | solution.py:539
  20.3 17.0 %collective-permute-start = (f32[1,4,128,128]{3,2,1,0:T(8,128)}, f32[1,4,128,128]{3,2,1,0:T(8,128)S(1)}, u32[]{:S(2)}, u32[]{:S(2)}) collective-permute-start(f32[1,4,128,128]{3,2,1,0:T(8,128)} %get-tuple-element.31), channel_id=1, source_target_pairs={{0,1},{1,0},{2,3},{3,2},{4,5},{5,4},{6,7},{7,6},{8,9},{9,8},{10,11... | collective-permute-start | bytes 786440 | tf_op jit(solution)/shard_map/ppermute | solution.py:531
  22.0 17.2 %collective-permute-start.1 = (f32[1,4,128,128]{3,2,1,0:T(8,128)}, f32[1,4,128,128]{3,2,1,0:T(8,128)S(1)}, u32[]{:S(2)}, u32[]{:S(2)}) collective-permute-start(f32[1,4,128,128]{3,2,1,0:T(8,128)} %get-tuple-element.32), channel_id=1, source_target_pairs={{0,2},{1,3},{2,0},{3,1},{4,6},{5,7},{6,4},{7,5},{8,10},{9,11},{10,... | collective-permute-start | bytes 786440 | tf_op jit(solution)/shard_map/ppermute | solution.py:531
  23.4 15.7 %collective-permute-start.2 = (f32[1,4,128,128]{3,2,1,0:T(8,128)}, f32[1,4,128,128]{3,2,1,0:T(8,128)S(1)}, u32[]{:S(2)}, u32[]{:S(2)}) collective-permute-start(f32[1,4,128,128]{3,2,1,0:T(8,128)} %get-tuple-element.33), channel_id=1, source_target_pairs={{0,3},{1,2},{2,1},{3,0},{4,7},{5,6},{6,5},{7,4},{8,11},{9,10},{10,... | collective-permute-start | bytes 786440 | tf_op jit(solution)/shard_map/ppermute | solution.py:531
  34.7 15.3 %collective-permute-start.3 = (bf16[8,4,16,128]{3,2,1,0:T(8,128)(2,1)S(1)}, bf16[8,4,16,128]{3,2,1,0:T(8,128)(2,1)S(1)}, u32[]{:S(2)}, u32[]{:S(2)}) collective-permute-start(bf16[8,4,16,128]{3,2,1,0:T(8,128)(2,1)S(1)} %sum_by_prompt.1.refs_0_), channel_id=1, source_target_pairs={{0,24},{4,28},{8,16},{12,20},{16,8},{20,12},{24,0},{28,4},{1,25},{... | collective-permute-start | bytes 393224 | tf_op jit(solution)/shard_map/ppermute | solution.py:437
  36.2 13.8 %collective-permute-start.4 = (bf16[8,4,16,128]{3,2,1,0:T(8,128)(2,1)S(1)}, bf16[8,4,16,128]{3,2,1,0:T(8,128)(2,1)S(1)}, u32[]{:S(2)}, u32[]{:S(2)}) collective-permute-start(bf16[8,4,16,128]{3,2,1,0:T(8,128)(2,1)S(1)} %sum_by_prompt.1.refs_0_), channel_id=1, source_target_pairs={{0,16},{4,20},{8,24},{12,28},{16,0},{20,4},{24,8},{28,12},{1,17},{... | collective-permute-start | bytes 393224 | tf_op jit(solution)/shard_map/ppermute | solution.py:437
  37.3 1.9 %copy-start.1 = (f32[1,4,128,128]{3,2,1,0:T(8,128)}, f32[1,4,128,128]{3,2,1,0:T(8,128)S(1)}, u32[]{:S(2)}) copy-start(f32[1,4,128,128]{3,2,1,0:T(8,128)S(1)} %collective-permute-done.refs_10_) | copy-start | bytes 786436
  37.3 12.8 %collective-permute-start.5 = (bf16[8,4,16,128]{3,2,1,0:T(8,128)(2,1)S(1)}, bf16[8,4,16,128]{3,2,1,0:T(8,128)(2,1)S(1)}, u32[]{:S(2)}, u32[]{:S(2)}) collective-permute-start(bf16[8,4,16,128]{3,2,1,0:T(8,128)(2,1)S(1)} %sum_by_prompt.1.refs_0_), channel_id=1, source_target_pairs={{0,8},{4,12},{8,0},{12,4},{16,24},{20,28},{24,16},{28,20},{1,9},{5... | collective-permute-start | bytes 393224 | tf_op jit(solution)/shard_map/ppermute | solution.py:437
  39.2 0.7 %copy-start.2 = (f32[1,4,128,128]{3,2,1,0:T(8,128)}, f32[1,4,128,128]{3,2,1,0:T(8,128)S(1)}, u32[]{:S(2)}) copy-start(f32[1,4,128,128]{3,2,1,0:T(8,128)S(1)} %collective-permute-done.1.refs_11_) | copy-start | bytes 786436
  39.2 10.9 %collective-permute-start.6 = (bf16[8,4,16,128]{3,2,1,0:T(8,128)(2,1)S(1)}, bf16[8,4,16,128]{3,2,1,0:T(8,128)(2,1)S(1)}, u32[]{:S(2)}, u32[]{:S(2)}) collective-permute-start(bf16[8,4,16,128]{3,2,1,0:T(8,128)(2,1)S(1)} %sum_by_prompt.1.refs_0_), channel_id=1, source_target_pairs={{0,4},{4,0},{8,12},{12,8},{16,20},{20,16},{24,28},{28,24},{1,5},{5... | collective-permute-start | bytes 393224 | tf_op jit(solution)/shard_map/ppermute | solution.py:439
  39.2 0.8 %copy-start.3 = (f32[1,4,128,128]{3,2,1,0:T(8,128)}, f32[1,4,128,128]{3,2,1,0:T(8,128)S(1)}, u32[]{:S(2)}) copy-start(f32[1,4,128,128]{3,2,1,0:T(8,128)S(1)} %collective-permute-done.2.refs_12_) | copy-start | bytes 786436
  50.1 1.4 %collective-permute-start.7 = (bf16[8,4,16,128]{3,2,1,0:T(8,128)(2,1)S(1)}, bf16[8,4,16,128]{3,2,1,0:T(8,128)(2,1)S(1)}, u32[]{:S(2)}, u32[]{:S(2)}) collective-permute-start(bf16[8,4,16,128]{3,2,1,0:T(8,128)(2,1)S(1)} %collective-permute-done.3.refs_1_), channel_id=1, source_target_pairs={{0,4},{4,0},{8,12},{12,8},{16,20},{20,16},{24,28},{28,24},{1,5},{5... | collective-permute-start | bytes 393224 | tf_op jit(solution)/shard_map/ppermute | solution.py:441
  50.5 1.3 %collective-permute-start.8 = (bf16[8,4,16,128]{3,2,1,0:T(8,128)(2,1)S(1)}, bf16[8,4,16,128]{3,2,1,0:T(8,128)(2,1)S(1)}, u32[]{:S(2)}, u32[]{:S(2)}) collective-permute-start(bf16[8,4,16,128]{3,2,1,0:T(8,128)(2,1)S(1)} %collective-permute-done.4.refs_2_), channel_id=1, source_target_pairs={{0,4},{4,0},{8,12},{12,8},{16,20},{20,16},{24,28},{28,24},{1,5},{5... | collective-permute-start | bytes 393224 | tf_op jit(solution)/shard_map/ppermute | solution.py:441
  50.6 1.4 %collective-permute-start.9 = (bf16[8,4,16,128]{3,2,1,0:T(8,128)(2,1)S(1)}, bf16[8,4,16,128]{3,2,1,0:T(8,128)(2,1)S(1)}, u32[]{:S(2)}, u32[]{:S(2)}) collective-permute-start(bf16[8,4,16,128]{3,2,1,0:T(8,128)(2,1)S(1)} %collective-permute-done.5.refs_3_), channel_id=1, source_target_pairs={{0,4},{4,0},{8,12},{12,8},{16,20},{20,16},{24,28},{28,24},{1,5},{5... | collective-permute-start | bytes 393224 | tf_op jit(solution)/shard_map/ppermute | solution.py:441

commit v5 on v4

--- a/solution.py
+++ b/solution.py
@@ -257,7 +257,7 @@
     members, count = len(chosen), chosen[0].shape[0]
     group_first = lax.axis_index("grp") * members * count
     reads, writes = [], []
-    for step in range(members):
+    for step in reversed(range(members)):
         receiver, _ = meeting(step)
         for b in range(count):
             prompt = prompt_ref[group_first + receiver * count + b]
@@ -527,9 +527,9 @@
         compiler_params=params,
         name="choose_states",
     )(branch_prompt, states_after)
-    states = [states[0]] + [
-        lax.ppermute(states[step], "head", moves_at(step, members)) for step in range(1, members)
-    ]
+    states = list(states)
+    for step in reversed(range(1, members)):
+        states[step] = lax.ppermute(states[step], "head", moves_at(step, members))
 
     coded = (
         coded.reshape(groups, count, members, heads_here, piece_rows, head_dim)

time: 54 us -> 54 us (level)
  transfers between devices with their start and end apart: 11 -> 11, of which waited for: 4 -> 4; matrix products, arithmetic and copies ran while one was open for 0% -> 0% of each run, Pallas kernels for 25% -> 26%
where the time goes in v5:
time: 54 us; the launch traced here: 53.7 us
  Pallas kernels  24.7 us (46%)
  starting transfers between devices  16.4 us (30%)
  waiting for transfers between devices  10.8 us (20%)
  between operations  0.91 us (2%)
  local copies, waits for them, and re-layouts  0.8 us (1%)
    pallas_call x1, Pallas kernels, per_device(): pl.pallas_call(functools.partial(second_kernel, members), grid_spec=pltpu...  10 us
    all_to_all x1, waiting for transfers between devices, per_device(): arrived = lax.all_to_all(coded, ('grp', 'head'), 0, 0, tiled=True)  9.77 us
    pallas_call x1, Pallas kernels, per_device(): pl.pallas_call(functools.partial(first_kernel, 16), grid_spec=pltpu.Prefe...  9.52 us
    all_to_all x1, starting transfers between devices, per_device(): arrived = lax.all_to_all(coded, ('grp', 'head'), 0, 0, tiled=True)  7.47 us
    ppermute x3, starting transfers between devices, gather_pieces(): pieces.append(lax.ppermute(piece, 'grp', moves))  4.45 us
    ppermute x3, starting transfers between devices, per_device(): states[step] = lax.ppermute(states[step], 'head', moves_at(step, members))  3.55 us
    pallas_call x1, Pallas kernels, per_device(): pl.pallas_call(choose_kernel, grid_spec=pltpu.PrefetchScalarGridSpec(num_...  2.79 us
    pallas_call x1, Pallas kernels, per_device(): pl.pallas_call(spread_kernel, in_specs=[whole] * len(pieces), out_specs=a...  1.49 us
  transfers between devices with their start and end apart: 11, of which 4 were waited for; matrix products, arithmetic and copies ran while one was open for 0% of the time, Pallas kernels for 26%

profile of v5, /device:TPU:0, one launch (start us, length us, event | category | flops | bytes accessed | tf_op | source)
XLA Modules:
  0.0 53.7 jit_solution(8710240299242672849)
XLA Ops:
  0.6 9.5 %state_independent.1 = (bf16[1,128,2048]{2,1,0:T(8,128)(2,1)}, bf16[1,128,2048]{2,1,0:T(8,128)(2,1)}, bf16[1,16,128,256]{3,2,1,0:T(8,128)(2,1)}, bf16[8,16,16,128]{3,2,1,0:T(8,128)(2,1)}) custom-call(s32[32]{0:T(128)} %valid_ref.3, bf16[1,128,2048]{2,1,0:T(8,128)(2,1)} %refs_0_.1, bf16[1,128,2048]{2,1,0:T(8,128)(2,1)} %refs_1_.1, ...), custom_call_target="tpu_custom_call" | custom-call | flops 3355443200 | bytes 8388608 | tf_op jit(solution)/shard_map/state_independent/pallas_call | solution.py:483
  10.2 0.0 copy-start
  10.2 7.5 %all-to-all-start = ((bf16[32,1,4,16,128]{4,3,2,1,0:T(8,128)(2,1)}), bf16[32,1,4,16,128]{4,3,2,1,0:T(8,128)(2,1)S(1)}, u32[]{:S(2)}, u32[]{:S(2)}) async-start(bf16[32,1,4,16,128]{4,3,2,1,0:T(8,128)(2,1)} %bitcast.9), calls=%async_computation | async-start | bytes 1048576 | tf_op jit(solution)/shard_map/all_to_all | solution.py:539
  17.6 2.8 %choose_states.1 = (f32[1,4,128,128]{3,2,1,0:T(8,128)}, f32[1,4,128,128]{3,2,1,0:T(8,128)}, f32[1,4,128,128]{3,2,1,0:T(8,128)}, f32[1,4,128,128]{3,2,1,0:T(8,128)}) custom-call(s32[32]{0:T(128)} %prompt_ref.3, f32[8,4,128,128]{3,2,1,0:T(8,128)} %state_ref), custom_call_target="tpu_custom_call" | custom-call | tf_op jit(solution)/shard_map/choose_states/pallas_call | solution.py:513
  20.4 1.5 %collective-permute-start = (f32[1,4,128,128]{3,2,1,0:T(8,128)}, f32[1,4,128,128]{3,2,1,0:T(8,128)S(1)}, u32[]{:S(2)}, u32[]{:S(2)}) collective-permute-start(f32[1,4,128,128]{3,2,1,0:T(8,128)} %get-tuple-element.31), channel_id=1, source_target_pairs={{0,1},{1,0},{2,3},{3,2},{4,5},{5,4},{6,7},{7,6},{8,9},{9,8},{10,11... | collective-permute-start | bytes 786440 | tf_op jit(solution)/shard_map/ppermute | solution.py:532
  22.0 1.5 %collective-permute-start.1 = (f32[1,4,128,128]{3,2,1,0:T(8,128)}, f32[1,4,128,128]{3,2,1,0:T(8,128)S(1)}, u32[]{:S(2)}, u32[]{:S(2)}) collective-permute-start(f32[1,4,128,128]{3,2,1,0:T(8,128)} %get-tuple-element.32), channel_id=1, source_target_pairs={{0,2},{1,3},{2,0},{3,1},{4,6},{5,7},{6,4},{7,5},{8,10},{9,11},{10,... | collective-permute-start | bytes 786440 | tf_op jit(solution)/shard_map/ppermute | solution.py:532
  23.4 0.6 %collective-permute-start.2 = (f32[1,4,128,128]{3,2,1,0:T(8,128)}, f32[1,4,128,128]{3,2,1,0:T(8,128)S(1)}, u32[]{:S(2)}, u32[]{:S(2)}) collective-permute-start(f32[1,4,128,128]{3,2,1,0:T(8,128)} %get-tuple-element.33), channel_id=1, source_target_pairs={{0,3},{1,2},{2,1},{3,0},{4,7},{5,6},{6,5},{7,4},{8,11},{9,10},{10,... | collective-permute-start | bytes 786440 | tf_op jit(solution)/shard_map/ppermute | solution.py:532
  24.0 9.8 %all-to-all-done = bf16[32,1,4,16,128]{4,3,2,1,0:T(8,128)(2,1)S(1)} async-done(((bf16[32,1,4,16,128]{4,3,2,1,0:T(8,128)(2,1)}), bf16[32,1,4,16,128]{4,3,2,1,0:T(8,128)(2,1)S(1)}, u32[]{:S(2)}, u32[]{:S(2)}) %all-to-all-start) | async-done | bytes 524320 | tf_op jit(solution)/shard_map/all_to_all | solution.py:539
  33.8 0.0 copy-done
  33.8 0.9 %sum_by_prompt.1.refs_0_ = bf16[8,4,16,128]{3,2,1,0:T(8,128)(2,1)S(1)} custom-call(s32[32]{0:T(128)S(1)} %copy-done, bf16[32,4,16,128]{3,2,1,0:T(8,128)(2,1)S(1)} %bitcast.7), custom_call_target="tpu_custom_call" | custom-call | tf_op jit(solution)/shard_map/sum_by_prompt/pallas_call | solution.py:581
  34.7 1.5 %collective-permute-start.3 = (bf16[8,4,16,128]{3,2,1,0:T(8,128)(2,1)S(1)}, bf16[8,4,16,128]{3,2,1,0:T(8,128)(2,1)S(1)}, u32[]{:S(2)}, u32[]{:S(2)}) collective-permute-start(bf16[8,4,16,128]{3,2,1,0:T(8,128)(2,1)S(1)} %sum_by_prompt.1.refs_0_), channel_id=1, source_target_pairs={{0,24},{4,28},{8,16},{12,20},{16,8},{20,12},{24,0},{28,4},{1,25},{... | collective-permute-start | bytes 393224 | tf_op jit(solution)/shard_map/ppermute | solution.py:437
  36.2 1.1 %collective-permute-start.4 = (bf16[8,4,16,128]{3,2,1,0:T(8,128)(2,1)S(1)}, bf16[8,4,16,128]{3,2,1,0:T(8,128)(2,1)S(1)}, u32[]{:S(2)}, u32[]{:S(2)}) collective-permute-start(bf16[8,4,16,128]{3,2,1,0:T(8,128)(2,1)S(1)} %sum_by_prompt.1.refs_0_), channel_id=1, source_target_pairs={{0,16},{4,20},{8,24},{12,28},{16,0},{20,4},{24,8},{28,12},{1,17},{... | collective-permute-start | bytes 393224 | tf_op jit(solution)/shard_map/ppermute | solution.py:437
  37.3 0.0 collective-permute-done.refs_10_
  37.3 0.0 copy-start.1
  37.3 1.9 %collective-permute-start.5 = (bf16[8,4,16,128]{3,2,1,0:T(8,128)(2,1)S(1)}, bf16[8,4,16,128]{3,2,1,0:T(8,128)(2,1)S(1)}, u32[]{:S(2)}, u32[]{:S(2)}) collective-permute-start(bf16[8,4,16,128]{3,2,1,0:T(8,128)(2,1)S(1)} %sum_by_prompt.1.refs_0_), channel_id=1, source_target_pairs={{0,8},{4,12},{8,0},{12,4},{16,24},{20,28},{24,16},{28,20},{1,9},{5... | collective-permute-start | bytes 393224 | tf_op jit(solution)/shard_map/ppermute | solution.py:437
  39.2 0.0 collective-permute-done.1.refs_11_
  39.2 0.0 copy-start.2
  39.2 0.0 collective-permute-start.6
  39.2 0.0 collective-permute-done.2.refs_12_
  39.2 0.0 copy-start.3
  39.2 0.0 copy-done.1
  39.2 0.7 %copy-done.2 = f32[1,4,128,128]{3,2,1,0:T(8,128)} copy-done((f32[1,4,128,128]{3,2,1,0:T(8,128)}, f32[1,4,128,128]{3,2,1,0:T(8,128)S(1)}, u32[]{:S(2)}) %copy-start.2) | copy-done | bytes 262168
  39.9 0.1 copy-done.3
  40.0 10.0 %state_dependent.1 = (bf16[1,128,2048]{2,1,0:T(8,128)(2,1)}, bf16[1,128,2048]{2,1,0:T(8,128)(2,1)}, bf16[1,128,2048]{2,1,0:T(8,128)(2,1)}, bf16[1,16,128]{2,1,0:T(8,128)(2,1)}) custom-call(s32[32]{0:T(128)} %valid_ref.3, bf16[1,128,2048]{2,1,0:T(8,128)(2,1)} %refs_0_.1, bf16[1,128,2048]{2,1,0:T(8,128)(2,1)} %refs_1_.1, bf16[1,128,2048]{2,1,0:T(8,128)(2,1)} %refs_2_.1, ...), custom_call_target="tpu_custom_call" | custom-call | flops 4026531840 | bytes 8388608 | tf_op jit(solution)/shard_map/state_dependent/pallas_call | solution.py:541
  50.0 0.0 collective-permute-done.3.refs_1_
  50.0 0.0 collective-permute-done.4.refs_2_
  50.0 0.0 collective-permute-done.5.refs_3_
  50.0 0.0 collective-permute-done.6.refs_4_
  50.1 0.5 collective-permute-start.7
  50.5 0.1 collective-permute-start.8
  50.6 0.4 collective-permute-start.9
  51.0 0.5 collective-permute-done.7.refs_5_
  51.5 0.4 collective-permute-done.8.refs_6_
  51.9 0.2 collective-permute-done.9.refs_7_
  52.0 1.5 %spread_pieces.1 = f32[8,4,8,16,128]{4,3,2,1,0:T(8,128)} custom-call(bf16[8,4,16,128]{3,2,1,0:T(8,128)(2,1)S(1)} %sum_by_prompt.1.refs_0_, bf16[8,4,16,128]{3,2,1,0:T(8,128)(2,1)S(1)} %collective-permute-done.3.refs_1_, bf16[8,4,16,128]{3,2,1,0:T(8,128)(2,1)S(1)} %collective-permute-done.4.refs_2_, ...), custom_call_target="tpu_custom_call" | custom-call | tf_op jit(solution)/shard_map/spread_pieces/pallas_call | solution.py:592
Async XLA Ops:
  10.2 23.6 %copy-start = (s32[32]{0:T(128)S(1)}, s32[32]{0:T(128)}, u32[]{:S(2)}) copy-start(s32[32]{0:T(128)} %prompt_ref.3) | copy-start | bytes 388
  10.2 23.6 %all-to-all-start = ((bf16[32,1,4,16,128]{4,3,2,1,0:T(8,128)(2,1)}), bf16[32,1,4,16,128]{4,3,2,1,0:T(8,128)(2,1)S(1)}, u32[]{:S(2)}, u32[]{:S(2)}) async-start(bf16[32,1,4,16,128]{4,3,2,1,0:T(8,128)(2,1)} %bitcast.9), calls=%async_computation | async-start | bytes 1048576 | tf_op jit(solution)/shard_map/all_to_all | solution.py:539
  20.4 16.8 %collective-permute-start = (f32[1,4,128,128]{3,2,1,0:T(8,128)}, f32[1,4,128,128]{3,2,1,0:T(8,128)S(1)}, u32[]{:S(2)}, u32[]{:S(2)}) collective-permute-start(f32[1,4,128,128]{3,2,1,0:T(8,128)} %get-tuple-element.31), channel_id=1, source_target_pairs={{0,1},{1,0},{2,3},{3,2},{4,5},{5,4},{6,7},{7,6},{8,9},{9,8},{10,11... | collective-permute-start | bytes 786440 | tf_op jit(solution)/shard_map/ppermute | solution.py:532
  22.0 17.2 %collective-permute-start.1 = (f32[1,4,128,128]{3,2,1,0:T(8,128)}, f32[1,4,128,128]{3,2,1,0:T(8,128)S(1)}, u32[]{:S(2)}, u32[]{:S(2)}) collective-permute-start(f32[1,4,128,128]{3,2,1,0:T(8,128)} %get-tuple-element.32), channel_id=1, source_target_pairs={{0,2},{1,3},{2,0},{3,1},{4,6},{5,7},{6,4},{7,5},{8,10},{9,11},{10,... | collective-permute-start | bytes 786440 | tf_op jit(solution)/shard_map/ppermute | solution.py:532
  23.4 15.7 %collective-permute-start.2 = (f32[1,4,128,128]{3,2,1,0:T(8,128)}, f32[1,4,128,128]{3,2,1,0:T(8,128)S(1)}, u32[]{:S(2)}, u32[]{:S(2)}) collective-permute-start(f32[1,4,128,128]{3,2,1,0:T(8,128)} %get-tuple-element.33), channel_id=1, source_target_pairs={{0,3},{1,2},{2,1},{3,0},{4,7},{5,6},{6,5},{7,4},{8,11},{9,10},{10,... | collective-permute-start | bytes 786440 | tf_op jit(solution)/shard_map/ppermute | solution.py:532
  34.7 15.3 %collective-permute-start.3 = (bf16[8,4,16,128]{3,2,1,0:T(8,128)(2,1)S(1)}, bf16[8,4,16,128]{3,2,1,0:T(8,128)(2,1)S(1)}, u32[]{:S(2)}, u32[]{:S(2)}) collective-permute-start(bf16[8,4,16,128]{3,2,1,0:T(8,128)(2,1)S(1)} %sum_by_prompt.1.refs_0_), channel_id=1, source_target_pairs={{0,24},{4,28},{8,16},{12,20},{16,8},{20,12},{24,0},{28,4},{1,25},{... | collective-permute-start | bytes 393224 | tf_op jit(solution)/shard_map/ppermute | solution.py:437
  36.2 13.8 %collective-permute-start.4 = (bf16[8,4,16,128]{3,2,1,0:T(8,128)(2,1)S(1)}, bf16[8,4,16,128]{3,2,1,0:T(8,128)(2,1)S(1)}, u32[]{:S(2)}, u32[]{:S(2)}) collective-permute-start(bf16[8,4,16,128]{3,2,1,0:T(8,128)(2,1)S(1)} %sum_by_prompt.1.refs_0_), channel_id=1, source_target_pairs={{0,16},{4,20},{8,24},{12,28},{16,0},{20,4},{24,8},{28,12},{1,17},{... | collective-permute-start | bytes 393224 | tf_op jit(solution)/shard_map/ppermute | solution.py:437
  37.3 1.9 %copy-start.1 = (f32[1,4,128,128]{3,2,1,0:T(8,128)}, f32[1,4,128,128]{3,2,1,0:T(8,128)S(1)}, u32[]{:S(2)}) copy-start(f32[1,4,128,128]{3,2,1,0:T(8,128)S(1)} %collective-permute-done.refs_10_) | copy-start | bytes 786436
  37.3 12.8 %collective-permute-start.5 = (bf16[8,4,16,128]{3,2,1,0:T(8,128)(2,1)S(1)}, bf16[8,4,16,128]{3,2,1,0:T(8,128)(2,1)S(1)}, u32[]{:S(2)}, u32[]{:S(2)}) collective-permute-start(bf16[8,4,16,128]{3,2,1,0:T(8,128)(2,1)S(1)} %sum_by_prompt.1.refs_0_), channel_id=1, source_target_pairs={{0,8},{4,12},{8,0},{12,4},{16,24},{20,28},{24,16},{28,20},{1,9},{5... | collective-permute-start | bytes 393224 | tf_op jit(solution)/shard_map/ppermute | solution.py:437
  39.2 0.7 %copy-start.2 = (f32[1,4,128,128]{3,2,1,0:T(8,128)}, f32[1,4,128,128]{3,2,1,0:T(8,128)S(1)}, u32[]{:S(2)}) copy-start(f32[1,4,128,128]{3,2,1,0:T(8,128)S(1)} %collective-permute-done.1.refs_11_) | copy-start | bytes 786436
  39.2 10.9 %collective-permute-start.6 = (bf16[8,4,16,128]{3,2,1,0:T(8,128)(2,1)S(1)}, bf16[8,4,16,128]{3,2,1,0:T(8,128)(2,1)S(1)}, u32[]{:S(2)}, u32[]{:S(2)}) collective-permute-start(bf16[8,4,16,128]{3,2,1,0:T(8,128)(2,1)S(1)} %sum_by_prompt.1.refs_0_), channel_id=1, source_target_pairs={{0,4},{4,0},{8,12},{12,8},{16,20},{20,16},{24,28},{28,24},{1,5},{5... | collective-permute-start | bytes 393224 | tf_op jit(solution)/shard_map/ppermute | solution.py:439
  39.2 0.8 %copy-start.3 = (f32[1,4,128,128]{3,2,1,0:T(8,128)}, f32[1,4,128,128]{3,2,1,0:T(8,128)S(1)}, u32[]{:S(2)}) copy-start(f32[1,4,128,128]{3,2,1,0:T(8,128)S(1)} %collective-permute-done.2.refs_12_) | copy-start | bytes 786436
  50.1 1.4 %collective-permute-start.7 = (bf16[8,4,16,128]{3,2,1,0:T(8,128)(2,1)S(1)}, bf16[8,4,16,128]{3,2,1,0:T(8,128)(2,1)S(1)}, u32[]{:S(2)}, u32[]{:S(2)}) collective-permute-start(bf16[8,4,16,128]{3,2,1,0:T(8,128)(2,1)S(1)} %collective-permute-done.3.refs_1_), channel_id=1, source_target_pairs={{0,4},{4,0},{8,12},{12,8},{16,20},{20,16},{24,28},{28,24},{1,5},{5... | collective-permute-start | bytes 393224 | tf_op jit(solution)/shard_map/ppermute | solution.py:441
  50.5 1.3 %collective-permute-start.8 = (bf16[8,4,16,128]{3,2,1,0:T(8,128)(2,1)S(1)}, bf16[8,4,16,128]{3,2,1,0:T(8,128)(2,1)S(1)}, u32[]{:S(2)}, u32[]{:S(2)}) collective-permute-start(bf16[8,4,16,128]{3,2,1,0:T(8,128)(2,1)S(1)} %collective-permute-done.4.refs_2_), channel_id=1, source_target_pairs={{0,4},{4,0},{8,12},{12,8},{16,20},{20,16},{24,28},{28,24},{1,5},{5... | collective-permute-start | bytes 393224 | tf_op jit(solution)/shard_map/ppermute | solution.py:441
  50.6 1.4 %collective-permute-start.9 = (bf16[8,4,16,128]{3,2,1,0:T(8,128)(2,1)S(1)}, bf16[8,4,16,128]{3,2,1,0:T(8,128)(2,1)S(1)}, u32[]{:S(2)}, u32[]{:S(2)}) collective-permute-start(bf16[8,4,16,128]{3,2,1,0:T(8,128)(2,1)S(1)} %collective-permute-done.5.refs_3_), channel_id=1, source_target_pairs={{0,4},{4,0},{8,12},{12,8},{16,20},{20,16},{24,28},{28,24},{1,5},{5... | collective-permute-start | bytes 393224 | tf_op jit(solution)/shard_map/ppermute | solution.py:441
